TPU v7x, 128 devices: a whole 4x4x4 slice. The times are simulated.
128 devices in a mesh: seq: 16 (over y, z), fsdp: 4 (over x), tp: 2 (over core).
Axes of the slice: x: 4, y: 4, z: 4, core: 2. Of those that a mesh axis runs over, the one named last changes fastest.
Arguments:
- tokens: bfloat16 [8192, 6144], P('seq'), may hold values from -6 to 6
- w_qkv: bfloat16 [6144, 3, 8192], P('seq', None, ('fsdp', 'tp')), may hold values from -0.078125 to 0.078125
- log_decay: float32 [64, 8192], P(('fsdp', 'tp')), may hold values from -1 to 0, as said below
- doc_lengths: int32 [12], replicated, may hold values from 1 to 6144, 8192 in all
- norm_gain: float32 [8192], P(('fsdp', 'tp')), may hold values from 0.25 to 1.75
Outputs:
- attn_out: bfloat16 [8192, 8192], P('seq', ('fsdp', 'tp'))
Inputs may be any that keep to these rules, and one draw needn't show every extreme that they name: `doc_lengths`: the lengths of the packed documents in order along the sequence; they sum to 8192. `log_decay`: logarithms of decay factors, all negative.
All inputs are finite; a program needn't handle non-finite values.
Results may differ from a plain program's by a relative error of at most 0.0037.
Values may be sent and summed in bfloat16 or wider, within the bound.
No kernel may reach another device: no remote copies, remote signals or barrier semaphores. Data moves between devices by JAX's collectives and lax.ppermute only.
A program may use at most 128 MiB of HBM per device.

v0:
```python
import functools

import jax
import jax.numpy as jnp
from jax import lax
from jax.experimental import pallas as pl
from jax.experimental.pallas import tpu as pltpu
from jax.sharding import PartitionSpec as P

AXES = ("y", "z", "x", "c")
HEADS = 64
HDIM = 128
BLOCK = 256
SIDE = 4
SPAN = 512
DEPTH = 6144
WROWS = 384
HH = 2
COLS = 3 * HH * HDIM
GROUP = SIDE * SPAN
NB = GROUP // BLOCK
VMEM = pltpu.CompilerParams(vmem_limit_bytes=56 * 1024 * 1024)


def move_y(a, d):
    return lax.ppermute(a, "y", [(s, (s + d) % 4) for s in range(4)])


def move_z(a, d):
    return lax.ppermute(a, "z", [(s, (s + d) % 4) for s in range(4)])


def move_x(a, d):
    return lax.ppermute(a, "x", [(s, (s + d) % 4) for s in range(4)])


def swap(a):
    return lax.ppermute(a, "c", [(0, 1), (1, 0)])


def opposed(a, axis, d):
    perm = [(2 * s + c, 2 * ((s + d - 2 * d * c) % 4) + c) for s in range(4) for c in range(2)]
    return lax.ppermute(a, (axis, "c"), perm)


def spread_weights(weights):
    out = []
    for k, piece in enumerate(weights):
        row = [opposed(piece, "z", k) if k else piece]
        for _ in range(SIDE - 1):
            row.append(opposed(row[-1], "y", 1))
        out += row
    return out


def along(place, axis, steps):
    return lax.rem(place[axis] + SIDE + steps * (2 * place[3] - 1), SIDE)


def project(spans, place, x, *refs):
    wrefs = refs[: SIDE * SIDE]
    out, wfull, acc, sem = refs[-4:]
    step = pl.program_id(0)

    def copies(i):
        yy = along(place, 1, i)
        for k in range(SIDE):
            at = pl.multiple_of((yy * SIDE + along(place, 0, k)) * WROWS, WROWS)
            n = SIDE * k + i
            yield pltpu.make_async_copy(wrefs[n], wfull.at[pl.ds(at, WROWS)], sem.at[n])

    @pl.when(step == 0)
    def _():
        for i in range(SIDE):
            for copy in copies(i):
                copy.start()

    for i in range(SIDE):

        @pl.when(step == 0)
        def _():
            for copy in copies(i):
                copy.wait()

        at = pl.multiple_of(along(place, 1, i) * (SIDE * WROWS), SIDE * WROWS)
        part = jnp.dot(
            x[:, pl.ds(at, SIDE * WROWS)],
            wfull[pl.ds(at, SIDE * WROWS), :],
            preferred_element_type=jnp.float32,
        )
        if i == 0:
            acc[...] = part
        else:
            acc[...] += part
    total = acc[...]
    out[...] = (total / (1.0 + jnp.exp(-total))).astype(jnp.bfloat16)


def call_project(place, rows, w, held):
    tile = 256
    per = SPAN // tile
    spans = SIDE - 1 if held else 1

    def there(i, place):
        return (lax.rem(place[0] + (i // per + 1 if held else 0), SIDE) * per + i % per, 0)

    def here(i, place):
        return (i, 0)

    hbm = pl.BlockSpec(memory_space=pl.ANY)
    return pl.pallas_call(
        functools.partial(project, spans),
        out_shape=jax.ShapeDtypeStruct((GROUP, COLS), jnp.bfloat16),
        grid_spec=pltpu.PrefetchScalarGridSpec(
            num_scalar_prefetch=1,
            grid=(spans * per,),
            in_specs=[pl.BlockSpec((tile, DEPTH), there if held else here)]
            + [hbm] * (len(w) + len(held)),
            out_specs=pl.BlockSpec((tile, COLS), there),
            scratch_shapes=[
                pltpu.VMEM((DEPTH, COLS), jnp.bfloat16),
                pltpu.VMEM((tile, COLS), jnp.float32),
                pltpu.SemaphoreType.DMA((SIDE * SIDE,)),
            ],
        ),
        input_output_aliases={2 + len(w): 0} if held else {},
        cost_estimate=pl.CostEstimate(
            flops=2 * spans * SPAN * DEPTH * COLS,
            bytes_accessed=(10 + 7 * spans) << 20,
            transcendentals=0,
        ),
        compiler_params=VMEM,
        name="project_others" if held else "project_own",
    )(place, rows, *w, *held)


def states(proj, kf, passes, local, final):
    for h in range(HH):
        held = jnp.zeros((HDIM, HDIM), jnp.float32)
        for b in range(NB):
            rows = pl.ds(b * BLOCK, BLOCK)
            k = proj[rows, pl.ds((HH + h) * HDIM, HDIM)].astype(jnp.float32)
            v = proj[rows, pl.ds((2 * HH + h) * HDIM, HDIM)]
            kd = (k * kf[rows, pl.ds(h, 1)]).astype(jnp.bfloat16)
            kv = lax.dot_general(
                kd, v, (((0,), (0,)), ((), ())), preferred_element_type=jnp.float32
            )
            local[h, b] = held
            held = passes[h, b] * held + kv
        final[h] = held.astype(jnp.bfloat16)


def intras(proj, cumr, cumc, docr, docc, out):
    row = lax.broadcasted_iota(jnp.int32, (BLOCK, BLOCK), 0)
    col = lax.broadcasted_iota(jnp.int32, (BLOCK, BLOCK), 1)
    lower = row >= col
    for b in range(NB):
        rows = pl.ds(b * BLOCK, BLOCK)
        mask = lower & (docc[rows, :] == docr[pl.ds(b, 1), :])
        for h in range(HH):
            q = proj[rows, pl.ds(h * HDIM, HDIM)]
            k = proj[rows, pl.ds((HH + h) * HDIM, HDIM)]
            v = proj[rows, pl.ds((2 * HH + h) * HDIM, HDIM)]
            scores = lax.dot_general(
                q, k, (((1,), (1,)), ((), ())), preferred_element_type=jnp.float32
            )
            diff = cumc[rows, pl.ds(h, 1)] - cumr[h, pl.ds(b, 1), :]
            decay = jnp.exp(jnp.where(mask, diff, 0.0))
            weights = jnp.where(mask, scores * decay, 0.0).astype(jnp.bfloat16)
            out[rows, pl.ds(h * HDIM, HDIM)] = jnp.dot(
                weights, v, preferred_element_type=jnp.float32
            )


def inters(proj, qf, carry, fac, local, s1, s2, s3, intra, out, squares):
    ones = jnp.ones((8, HDIM), jnp.float32)
    for b in range(NB):
        rows = pl.ds(b * BLOCK, BLOCK)
        total = jnp.zeros((8, BLOCK), jnp.float32)
        for h in range(HH):
            incoming = (
                fac[h, 0] * s1[h].astype(jnp.float32)
                + fac[h, 1] * s2[h].astype(jnp.float32)
                + fac[h, 2] * s3[h].astype(jnp.float32)
            )
            state = (local[h, b] + carry[h, b] * incoming).astype(jnp.bfloat16)
            q = proj[rows, pl.ds(h * HDIM, HDIM)].astype(jnp.float32)
            qd = (q * qf[rows, pl.ds(h, 1)]).astype(jnp.bfloat16)
            att = intra[rows, pl.ds(h * HDIM, HDIM)] + jnp.dot(
                qd, state, preferred_element_type=jnp.float32
            )
            total += lax.dot_general(
                ones,
                att * att,
                (((1,), (1,)), ((), ())),
                precision=lax.Precision.HIGHEST,
                preferred_element_type=jnp.float32,
            )
            out[rows, pl.ds(h * HDIM, HDIM)] = att.astype(jnp.bfloat16)
        squares[pl.ds(b, 1), :] = total[0:1, :]


def finish(place, total, gain, p0, p1, p2, p3, out):
    scale = lax.rsqrt(total[...] / (HEADS * HDIM) + 1e-05)
    for b in range(SPAN // BLOCK):
        rows = pl.ds(b * BLOCK, BLOCK)
        column = jnp.transpose(jnp.broadcast_to(scale[b : b + 1, :], (8, BLOCK)))[:, 0:1]
        for dz, piece in ((0, p0), (3, p1), (1, p2), (2, p3)):
            zz = lax.rem(place[0] + dz, SIDE)
            cols = pl.ds(pl.multiple_of(zz * (HH * HDIM), HH * HDIM), HH * HDIM)
            value = piece[rows, :].astype(jnp.float32) * column
            out[rows, cols] = (value * gain[0:1, cols]).astype(jnp.bfloat16)


def doc_of(points, ends):
    found = jnp.sum((points[..., None] >= ends).astype(jnp.int32), axis=-1)
    return jnp.where(points < 0, -1, found)


def per_device(tokens, w_qkv, log_decay, doc_lengths, norm_gain):
    y, z, x, c = [lax.axis_index(axis) for axis in AXES]
    place = jnp.stack([z, y, x, c]).astype(jnp.int32)

    mine = lax.dynamic_slice(tokens, ((2 * x + c) * 64, 0), (64, DEPTH))
    wview = w_qkv.reshape(WROWS, 3, SIDE, HH * HDIM)
    weights = []
    for d in range(SIDE):
        at = (z + d * (1 - 2 * c)) % SIDE
        weights.append(
            lax.dynamic_slice(wview, (0, 0, at, 0), (WROWS, 3, 1, HH * HDIM)).reshape(WROWS, COLS)
        )
    group = lax.all_gather(mine, ("z", "x", "c"), axis=0, tiled=True)
    w = spread_weights(weights)

    ends = jnp.cumsum(doc_lengths)
    nblocks = GROUP * SIDE // BLOCK
    decays = lax.dynamic_slice(log_decay, (HH * z, 0), (HH, GROUP * SIDE))
    cum_all = jnp.cumsum(decays.reshape(HH, nblocks, BLOCK), axis=2)
    starts = jnp.arange(nblocks, dtype=jnp.int32) * BLOCK
    before_all = doc_of(starts - 1, ends)
    last_all = doc_of(starts + (BLOCK - 1), ends)
    pass_all = jnp.where((before_all == last_all)[None], jnp.exp(cum_all[:, :, -1]), 0.0)
    gpass = jnp.prod(pass_all.reshape(HH, SIDE, NB), axis=2)
    f1 = jnp.where(y >= 1, 1.0, 0.0) * jnp.ones((HH,), jnp.float32)
    prev1 = lax.dynamic_index_in_dim(gpass, jnp.maximum(y - 1, 0), 1, keepdims=False)
    prev2 = lax.dynamic_index_in_dim(gpass, jnp.maximum(y - 2, 0), 1, keepdims=False)
    f2 = jnp.where(y >= 2, prev1, 0.0)
    f3 = jnp.where(y >= 3, prev1 * prev2, 0.0)
    fac = jnp.stack([f1, f2, f3], axis=1)
    passes = lax.dynamic_slice_in_dim(pass_all, NB * y, NB, 1)
    carry = jnp.concatenate(
        [jnp.ones((HH, 1), jnp.float32), jnp.cumprod(passes, axis=1)[:, :-1]], axis=1
    )
    cum = lax.dynamic_slice_in_dim(cum_all, NB * y, NB, 1)
    before = lax.dynamic_slice_in_dim(before_all, NB * y, NB, 0)
    last = lax.dynamic_slice_in_dim(last_all, NB * y, NB, 0)
    points = GROUP * y + jnp.arange(GROUP, dtype=jnp.int32).reshape(NB, BLOCK)
    doc = doc_of(points, ends)
    qfac = jnp.where((doc == before[:, None])[None], jnp.exp(cum), 0.0)
    kfac = jnp.where((doc == last[:, None])[None], jnp.exp(cum[:, :, -1:] - cum), 0.0)
    cumc = cum.reshape(HH, GROUP).T
    qf = qfac.reshape(HH, GROUP).T
    kf = kfac.reshape(HH, GROUP).T
    docc = doc.reshape(GROUP, 1)

    own = call_project(place, tokens, w, [])
    proj = call_project(place, group, w, [own])

    smem = pl.BlockSpec(memory_space=pltpu.SMEM)
    vmem = pl.BlockSpec(memory_space=pltpu.VMEM)
    square = (HDIM, HDIM)
    local, final = pl.pallas_call(
        states,
        out_shape=(
            jax.ShapeDtypeStruct((HH, NB) + square, jnp.float32),
            jax.ShapeDtypeStruct((HH,) + square, jnp.bfloat16),
        ),
        in_specs=[vmem, vmem, smem],
        out_specs=(vmem, vmem),
        cost_estimate=pl.CostEstimate(flops=1 << 27, bytes_accessed=4 << 20, transcendentals=0),
        compiler_params=VMEM,
        name="states",
    )(proj, kf, passes)
    s1, s2, s3 = move_y(final, 1), move_y(final, 2), move_y(final, 3)
    intra = pl.pallas_call(
        intras,
        out_shape=jax.ShapeDtypeStruct((GROUP, HH * HDIM), jnp.float32),
        in_specs=[vmem] * 5,
        out_specs=vmem,
        cost_estimate=pl.CostEstimate(flops=1 << 30, bytes_accessed=8 << 20, transcendentals=1 << 20),
        compiler_params=VMEM,
        name="intras",
    )(proj, cum, cumc, doc, docc)
    att, squares = pl.pallas_call(
        inters,
        out_shape=(
            jax.ShapeDtypeStruct((GROUP, HH * HDIM), jnp.bfloat16),
            jax.ShapeDtypeStruct((NB, BLOCK), jnp.float32),
        ),
        in_specs=[vmem, vmem, smem, smem] + [vmem] * 5,
        out_specs=(vmem, vmem),
        cost_estimate=pl.CostEstimate(flops=1 << 28, bytes_accessed=8 << 20, transcendentals=0),
        compiler_params=VMEM,
        name="inters",
    )(proj, qf, carry, fac, local, s1, s2, s3, intra)

    near = SPAN // BLOCK

    def share(a, d, size):
        return lax.dynamic_slice_in_dim(a, ((z + d) % SIDE) * size, size, 0)

    part = share(squares, 0, near)
    for d in (1, -1, 2):
        part = part + move_z(share(squares, d, near), d)
    part = part + swap(part)
    total = part + move_x(part, 1) + move_x(part, -1) + move_x(part, 2)
    pieces = [share(att, 0, SPAN)] + [move_z(share(att, d, SPAN), d) for d in (1, -1, 2)]
    return pl.pallas_call(
        finish,
        out_shape=jax.ShapeDtypeStruct((SPAN, SIDE * HH * HDIM), jnp.bfloat16),
        in_specs=[smem] + [vmem] * 6,
        out_specs=vmem,
        cost_estimate=pl.CostEstimate(flops=1 << 22, bytes_accessed=3 << 20, transcendentals=0),
        compiler_params=VMEM,
        name="finish",
    )(place, total, norm_gain.reshape(1, -1), *pieces)


def solution(mesh):
    mesh = jax.sharding.Mesh(mesh.devices.reshape(SIDE, SIDE, SIDE, 2), AXES)
    in_specs = (
        P(("y", "z"), None),
        P(("y", "z"), None, ("x", "c")),
        P(("x", "c"), None),
        P(),
        P(("x", "c")),
    )
    out_specs = P(("y", "z"), ("x", "c"))
    return jax.shard_map(
        per_device, mesh=mesh, in_specs=in_specs, out_specs=out_specs, check_vma=False
    )
```

profile of v0, /device:TPU:0, one launch (start us, length us, event | category | flops | bytes accessed | tf_op | source)
XLA Modules:
  0.0 227.2 jit_solution(4942713890086665381)
XLA Ops:
  6.5 2.1 constant_dynamic-slice_fusion.17
  8.8 3.0 %copy.40 = bf16[384,3,1024]{0,2,1:T(8,128)(2,1)S(1)} copy(bf16[384,3,1024]{2,0,1:T(8,128)(2,1)} %param.6) | data formatting | bytes 4718592 | tf_op args[1]
  13.1 2.1 copy.43
  15.2 4.0 %collective-permute-start.7 = (bf16[384,768]{1,0:T(8,128)(2,1)}, bf16[384,768]{1,0:T(8,128)(2,1)S(1)}, u32[]{:S(2)}, u32[]{:S(2)}) collective-permute-start(bf16[384,768]{1,0:T(8,128)(2,1)} %copy.43), channel_id=1, source_target_pairs={{0,16},{1,17},{8,24},{9,25},{16,0},{17,1},{24,8},{25,9},{2,18},{3,... | collective-permute-start | bytes 1769480 | tf_op jit(solution)/shard_map/ppermute | solution.py:43
  19.2 2.2 copy.44
  22.1 2.2 copy.42
  25.8 1.6 collective-permute-start
  29.6 10.3 %collective-permute-done.7.refs_8_ = bf16[384,768]{1,0:T(8,128)(2,1)S(1)} collective-permute-done((bf16[384,768]{1,0:T(8,128)(2,1)}, bf16[384,768]{1,0:T(8,128)(2,1)S(1)}, u32[]{:S(2)}, u32[]{:S(2)}) %collective-permute-start.7) | collective-permute-done | bytes 589856 | tf_op jit(solution)/shard_map/ppermute | solution.py:43
  41.5 17.2 %collective-permute-done.11.refs_12_ = bf16[384,768]{1,0:T(8,128)(2,1)S(1)} collective-permute-done((bf16[384,768]{1,0:T(8,128)(2,1)}, bf16[384,768]{1,0:T(8,128)(2,1)S(1)}, u32[]{:S(2)}, u32[]{:S(2)}) %collective-permute-start.11) | collective-permute-done | bytes 589856 | tf_op jit(solution)/shard_map/ppermute | solution.py:43
  64.1 5.8 %collective-permute-done.12.refs_13_ = bf16[384,768]{1,0:T(8,128)(2,1)} collective-permute-done((bf16[384,768]{1,0:T(8,128)(2,1)S(1)}, bf16[384,768]{1,0:T(8,128)(2,1)}, u32[]{:S(2)}, u32[]{:S(2)}) %collective-permute-start.12) | collective-permute-done | bytes 589856 | tf_op jit(solution)/shard_map/ppermute | solution.py:43
  70.3 6.0 %collective-permute-done.4.refs_5_ = bf16[384,768]{1,0:T(8,128)(2,1)} collective-permute-done((bf16[384,768]{1,0:T(8,128)(2,1)S(1)}, bf16[384,768]{1,0:T(8,128)(2,1)}, u32[]{:S(2)}, u32[]{:S(2)}) %collective-permute-start.4) | collective-permute-done | bytes 589856 | tf_op jit(solution)/shard_map/ppermute | solution.py:43
  76.7 5.8 %collective-permute-done.1.refs_2_ = bf16[384,768]{1,0:T(8,128)(2,1)} collective-permute-done((bf16[384,768]{1,0:T(8,128)(2,1)S(1)}, bf16[384,768]{1,0:T(8,128)(2,1)}, u32[]{:S(2)}, u32[]{:S(2)}) %collective-permute-start.1) | collective-permute-done | bytes 589856 | tf_op jit(solution)/shard_map/ppermute | solution.py:43
  82.9 6.0 %collective-permute-done.9.refs_10_ = bf16[384,768]{1,0:T(8,128)(2,1)} collective-permute-done((bf16[384,768]{1,0:T(8,128)(2,1)}, bf16[384,768]{1,0:T(8,128)(2,1)}, u32[]{:S(2)}, u32[]{:S(2)}) %collective-permute-start.9) | collective-permute-done | bytes 589856 | tf_op jit(solution)/shard_map/ppermute | solution.py:43
  89.2 6.0 %collective-permute-done.13.refs_14_ = bf16[384,768]{1,0:T(8,128)(2,1)} collective-permute-done((bf16[384,768]{1,0:T(8,128)(2,1)}, bf16[384,768]{1,0:T(8,128)(2,1)}, u32[]{:S(2)}, u32[]{:S(2)}) %collective-permute-start.13) | collective-permute-done | bytes 589856 | tf_op jit(solution)/shard_map/ppermute | solution.py:43
  95.6 6.0 %collective-permute-done.5.refs_6_ = bf16[384,768]{1,0:T(8,128)(2,1)} collective-permute-done((bf16[384,768]{1,0:T(8,128)(2,1)}, bf16[384,768]{1,0:T(8,128)(2,1)}, u32[]{:S(2)}, u32[]{:S(2)}) %collective-permute-start.5) | collective-permute-done | bytes 589856 | tf_op jit(solution)/shard_map/ppermute | solution.py:43
  109.9 4.3 %collective-permute-done.10.refs_11_ = bf16[384,768]{1,0:T(8,128)(2,1)} collective-permute-done((bf16[384,768]{1,0:T(8,128)(2,1)}, bf16[384,768]{1,0:T(8,128)(2,1)}, u32[]{:S(2)}, u32[]{:S(2)}) %collective-permute-start.10) | collective-permute-done | bytes 589856 | tf_op jit(solution)/shard_map/ppermute | solution.py:43
  114.2 6.3 %collective-permute-done.14.refs_15_ = bf16[384,768]{1,0:T(8,128)(2,1)} collective-permute-done((bf16[384,768]{1,0:T(8,128)(2,1)}, bf16[384,768]{1,0:T(8,128)(2,1)}, u32[]{:S(2)}, u32[]{:S(2)}) %collective-permute-start.14) | collective-permute-done | bytes 589856 | tf_op jit(solution)/shard_map/ppermute | solution.py:43
  120.5 6.3 %collective-permute-done.6.refs_7_ = bf16[384,768]{1,0:T(8,128)(2,1)} collective-permute-done((bf16[384,768]{1,0:T(8,128)(2,1)}, bf16[384,768]{1,0:T(8,128)(2,1)}, u32[]{:S(2)}, u32[]{:S(2)}) %collective-permute-start.6) | collective-permute-done | bytes 589856 | tf_op jit(solution)/shard_map/ppermute | solution.py:43
  126.8 13.5 %project_own.1.refs_16_ = bf16[2048,768]{1,0:T(8,128)(2,1)} custom-call(s32[4]{0:T(128)} %pad_add_fusion.place, bf16[512,6144]{1,0:T(8,128)(2,1)} %x.3, bf16[384,768]{1,0:T(8,128)(2,1)} %copy-done.1, bf16[384,768]{1,0:T(8,128)(2,1)} %copy-done.5, bf16[384,768]{1,0:T(8,128)(2,1)} %collective-permute-done.1.refs_2_, ...), custom_call_target="tpu_custom_call" | custom-call | flops 4831838208 | bytes 17825792 | tf_op jit(solution)/shard_map/project_own/pallas_call | solution.py:111
  140.4 30.1 %project_others.1.proj = bf16[2048,768]{1,0:T(8,128)(2,1)} custom-call(s32[4]{0:T(128)} %pad_add_fusion.place, bf16[2048,6144]{1,0:T(8,128)(2,1)} %all-gather.2.cloned.1.call-done.x, bf16[384,768]{1,0:T(8,128)(2,1)} %copy-done.1, bf16[384,768]{1,0:T(8,128)(2,1)} %copy-done.5, ...), custom_call_target="tpu_custom_call", output_to_operand_aliasing={{}: (18, {})} | custom-call | flops 14495514624 | bytes 32505856 | tf_op jit(solution)/shard_map/project_others/pallas_call | solution.py:111
  170.6 4.9 %states.1 = (f32[2,8,128,128]{3,2,1,0:T(8,128)}, bf16[2,128,128]{2,1,0:T(8,128)(2,1)}) custom-call(bf16[2048,768]{1,0:T(8,128)(2,1)} %project_others.1.proj, f32[2048,2]{1,0:T(8,128)} %bitcast.33, f32[2,8]{1,0:T(2,128)} %copy-done.14), custom_call_target="tpu_custom_call" | custom-call | flops 134217728 | bytes 4194304 | tf_op jit(solution)/shard_map/states/pallas_call | solution.py:272
  175.7 2.9 %collective-permute-start.16 = (bf16[2,128,128]{2,1,0:T(8,128)(2,1)}, bf16[2,128,128]{2,1,0:T(8,128)(2,1)S(1)}, u32[]{:S(2)}, u32[]{:S(2)}) collective-permute-start(bf16[2,128,128]{2,1,0:T(8,128)(2,1)} %get-tuple-element.10), channel_id=1, source_target_pairs={{0,64},{32,96},{64,0},{96,32},{1,65},{33,97},{65,1},{97,33},{2,66}... | collective-permute-start | bytes 196616 | tf_op jit(solution)/shard_map/ppermute | solution.py:26
  180.1 5.4 %intras.1.intra = f32[2048,256]{1,0:T(8,128)} custom-call(bf16[2048,768]{1,0:T(8,128)(2,1)} %project_others.1.proj, f32[2,8,256]{2,1,0:T(8,128)} %copy-done.6, f32[2048,2]{1,0:T(8,128)} %bitcast.34, s32[8,256]{1,0:T(8,128)} %copy-done.10, s32[2048,1]{1,0:T(8,128)} %bitcast.36), custom_call_target="tpu_custom_call" | custom-call | flops 1073741824 | bytes 8388608 | tf_op jit(solution)/shard_map/intras/pallas_call | solution.py:285
  186.1 6.7 %inters.1 = (bf16[2048,256]{1,0:T(8,128)(2,1)}, f32[8,256]{1,0:T(8,128)}) custom-call(bf16[2048,768]{1,0:T(8,128)(2,1)} %project_others.1.proj, f32[2048,2]{1,0:T(8,128)} %bitcast.35, f32[2,8]{1,0:T(2,128)} %concatenate.3.carry, f32[2,3]{1,0:T(2,128)} %pad_maximum_fusion.fac, f32[2,8,128,128]{3,2,1,0:T(8,128)} %get-tuple-element.9.local, ...), custom_call_target="tpu_custom_call" | custom-call | flops 268435456 | bytes 8388608 | tf_op jit(solution)/shard_map/inters/pallas_call | solution.py:294
  194.0 2.9 %collective-permute-start.19 = (f32[2,256]{1,0:T(2,128)S(1)}, f32[2,256]{1,0:T(2,128)S(1)}, u32[]{:S(2)}, u32[]{:S(2)}) collective-permute-start(f32[2,256]{1,0:T(2,128)S(1)} %get-tuple-element.29), channel_id=1, source_target_pairs={{0,24},{8,0},{16,8},{24,16},{1,25},{9,1},{17,9},{25,17},{2,26},{10... | collective-permute-start | bytes 6152 | tf_op jit(solution)/shard_map/ppermute | solution.py:30
  197.5 2.0 constant_dynamic-slice_fusion
  200.9 1.8 collective-permute-start.26
  202.7 1.7 collective-permute-start.27
  207.8 1.7 collective-permute-start.23
  211.1 1.8 collective-permute-start.24
  212.9 3.3 %collective-permute-done.24 = f32[2,256]{1,0:T(2,128)S(1)} collective-permute-done((f32[2,256]{1,0:T(2,128)S(1)}, f32[2,256]{1,0:T(2,128)S(1)}, u32[]{:S(2)}, u32[]{:S(2)}) %collective-permute-start.24) | collective-permute-done | bytes 2080 | tf_op jit(solution)/shard_map/ppermute | solution.py:34
  217.7 2.7 %finish.1 = bf16[512,1024]{1,0:T(8,128)(2,1)} custom-call(s32[4]{0:T(128)} %pad_add_fusion.place, f32[2,256]{1,0:T(2,128)} %add_add_fusion.1.total, f32[1,1024]{1,0:T(1,128)} %bitcast.43, bf16[512,256]{1,0:T(8,128)(2,1)} %get-tuple-element.26.p0, bf16[512,256]{1,0:T(8,128)(2,1)} %copy-done.7, bf16[512,256]{1,0:T(8,128)(2,1)} %copy-done.8, ...), custom_call_target="tpu_custom_call" | custom-call | flops 4194304 | bytes 3145728 | tf_op jit(solution)/shard_map/finish/pallas_call | solution.py:318
  (119 shorter events, 34.9 us)
Async XLA Ops:
  6.5 133.9 %all-gather.2.cloned.1.call-start = ((), (), s32[]{:S(2)}) async-start(), calls=%async_computation | async-start | bytes 25952256 | tf_op jit(solution)/shard_map/all_gather | solution.py:232
  15.2 24.7 %collective-permute-start.7 = (bf16[384,768]{1,0:T(8,128)(2,1)}, bf16[384,768]{1,0:T(8,128)(2,1)S(1)}, u32[]{:S(2)}, u32[]{:S(2)}) collective-permute-start(bf16[384,768]{1,0:T(8,128)(2,1)} %copy.43), channel_id=1, source_target_pairs={{0,16},{1,17},{8,24},{9,25},{16,0},{17,1},{24,8},{25,9},{2,18},{3,... | collective-permute-start | bytes 1769480 | tf_op jit(solution)/shard_map/ppermute | solution.py:43
  21.4 37.4 %collective-permute-start.11 = (bf16[384,768]{1,0:T(8,128)(2,1)}, bf16[384,768]{1,0:T(8,128)(2,1)S(1)}, u32[]{:S(2)}, u32[]{:S(2)}) collective-permute-start(bf16[384,768]{1,0:T(8,128)(2,1)} %copy.44), channel_id=1, source_target_pairs={{0,24},{1,9},{8,0},{9,17},{16,8},{17,25},{24,16},{25,1},{2,26},{3,... | collective-permute-start | bytes 1769480 | tf_op jit(solution)/shard_map/ppermute | solution.py:43
  24.2 36.0 %collective-permute-start.3 = (bf16[384,768]{1,0:T(8,128)(2,1)}, bf16[384,768]{1,0:T(8,128)(2,1)S(1)}, u32[]{:S(2)}, u32[]{:S(2)}) collective-permute-start(bf16[384,768]{1,0:T(8,128)(2,1)} %copy.42), channel_id=1, source_target_pairs={{0,8},{1,25},{8,16},{9,1},{16,24},{17,9},{24,0},{25,17},{2,10},{3,... | collective-permute-start | bytes 1769480 | tf_op jit(solution)/shard_map/ppermute | solution.py:43
  25.8 101.0 %copy-start.1 = (bf16[384,768]{1,0:T(8,128)(2,1)}, bf16[384,768]{1,0:T(8,128)(2,1)S(1)}, u32[]{:S(2)}) copy-start(bf16[384,768]{1,0:T(8,128)(2,1)S(1)} %copy.46.refs_0_) | copy-start | bytes 1769476
  25.8 36.7 %collective-permute-start = (bf16[384,768]{1,0:T(8,128)(2,1)S(1)}, bf16[384,768]{1,0:T(8,128)(2,1)S(1)}, u32[]{:S(2)}, u32[]{:S(2)}) collective-permute-start(bf16[384,768]{1,0:T(8,128)(2,1)S(1)} %copy.46.refs_0_), channel_id=1, source_target_pairs={{0,32},{1,97},{32,64},{33,1},{64,96},{65,33},{96,0},{97,65},{2,34}... | collective-permute-start | bytes 1769480 | tf_op jit(solution)/shard_map/ppermute | solution.py:43
  39.9 86.9 %copy-start.2 = (bf16[384,768]{1,0:T(8,128)(2,1)}, bf16[384,768]{1,0:T(8,128)(2,1)S(1)}, u32[]{:S(2)}) copy-start(bf16[384,768]{1,0:T(8,128)(2,1)S(1)} %collective-permute-done.7.refs_8_) | copy-start | bytes 1769476
  39.9 24.0 %collective-permute-start.8 = (bf16[384,768]{1,0:T(8,128)(2,1)S(1)}, bf16[384,768]{1,0:T(8,128)(2,1)}, u32[]{:S(2)}, u32[]{:S(2)}) collective-permute-start(bf16[384,768]{1,0:T(8,128)(2,1)S(1)} %collective-permute-done.7.refs_8_), channel_id=1, source_target_pairs={{0,32},{1,97},{32,64},{33,1},{64,96},{65,33},{96,0},{97,65},{2,34}... | collective-permute-start | bytes 1769480 | tf_op jit(solution)/shard_map/ppermute | solution.py:43
  58.7 11.2 %collective-permute-start.12 = (bf16[384,768]{1,0:T(8,128)(2,1)S(1)}, bf16[384,768]{1,0:T(8,128)(2,1)}, u32[]{:S(2)}, u32[]{:S(2)}) collective-permute-start(bf16[384,768]{1,0:T(8,128)(2,1)S(1)} %collective-permute-done.11.refs_12_), channel_id=1, source_target_pairs={{0,32},{1,97},{32,64},{33,1},{64,96},{65,33},{96,0},{97,65},{2,34}... | collective-permute-start | bytes 1769480 | tf_op jit(solution)/shard_map/ppermute | solution.py:43
  60.3 15.9 %collective-permute-start.4 = (bf16[384,768]{1,0:T(8,128)(2,1)S(1)}, bf16[384,768]{1,0:T(8,128)(2,1)}, u32[]{:S(2)}, u32[]{:S(2)}) collective-permute-start(bf16[384,768]{1,0:T(8,128)(2,1)S(1)} %collective-permute-done.3.refs_4_), channel_id=1, source_target_pairs={{0,32},{1,97},{32,64},{33,1},{64,96},{65,33},{96,0},{97,65},{2,34}... | collective-permute-start | bytes 1769480 | tf_op jit(solution)/shard_map/ppermute | solution.py:43
  62.5 77.9 %copy-start.10 = (s32[8,256]{1,0:T(8,128)}, s32[8,256]{1,0:T(8,128)S(1)}, u32[]{:S(2)}) copy-start(s32[8,256]{1,0:T(8,128)S(1)} %get-tuple-element.18.docr) | copy-start | bytes 24580
  62.6 20.0 %collective-permute-start.1 = (bf16[384,768]{1,0:T(8,128)(2,1)S(1)}, bf16[384,768]{1,0:T(8,128)(2,1)}, u32[]{:S(2)}, u32[]{:S(2)}) collective-permute-start(bf16[384,768]{1,0:T(8,128)(2,1)S(1)} %collective-permute-done.refs_1_), channel_id=1, source_target_pairs={{0,32},{1,97},{32,64},{33,1},{64,96},{65,33},{96,0},{97,65},{2,34}... | collective-permute-start | bytes 1769480 | tf_op jit(solution)/shard_map/ppermute | solution.py:43
  63.9 24.9 %collective-permute-start.9 = (bf16[384,768]{1,0:T(8,128)(2,1)}, bf16[384,768]{1,0:T(8,128)(2,1)}, u32[]{:S(2)}, u32[]{:S(2)}) collective-permute-start(bf16[384,768]{1,0:T(8,128)(2,1)} %collective-permute-done.8.refs_9_), channel_id=1, source_target_pairs={{0,32},{1,97},{32,64},{33,1},{64,96},{65,33},{96,0},{97,65},{2,34}... | collective-permute-start | bytes 1769480 | tf_op jit(solution)/shard_map/ppermute | solution.py:43
  69.9 25.3 %collective-permute-start.13 = (bf16[384,768]{1,0:T(8,128)(2,1)}, bf16[384,768]{1,0:T(8,128)(2,1)}, u32[]{:S(2)}, u32[]{:S(2)}) collective-permute-start(bf16[384,768]{1,0:T(8,128)(2,1)} %collective-permute-done.12.refs_13_), channel_id=1, source_target_pairs={{0,32},{1,97},{32,64},{33,1},{64,96},{65,33},{96,0},{97,65},{2,34}... | collective-permute-start | bytes 1769480 | tf_op jit(solution)/shard_map/ppermute | solution.py:43
  76.2 25.3 %collective-permute-start.5 = (bf16[384,768]{1,0:T(8,128)(2,1)}, bf16[384,768]{1,0:T(8,128)(2,1)}, u32[]{:S(2)}, u32[]{:S(2)}) collective-permute-start(bf16[384,768]{1,0:T(8,128)(2,1)} %collective-permute-done.4.refs_5_), channel_id=1, source_target_pairs={{0,32},{1,97},{32,64},{33,1},{64,96},{65,33},{96,0},{97,65},{2,34}... | collective-permute-start | bytes 1769480 | tf_op jit(solution)/shard_map/ppermute | solution.py:43
  82.6 27.3 %collective-permute-start.2 = (bf16[384,768]{1,0:T(8,128)(2,1)}, bf16[384,768]{1,0:T(8,128)(2,1)}, u32[]{:S(2)}, u32[]{:S(2)}) collective-permute-start(bf16[384,768]{1,0:T(8,128)(2,1)} %collective-permute-done.1.refs_2_), channel_id=1, source_target_pairs={{0,32},{1,97},{32,64},{33,1},{64,96},{65,33},{96,0},{97,65},{2,34}... | collective-permute-start | bytes 1769480 | tf_op jit(solution)/shard_map/ppermute | solution.py:43
  88.9 25.3 %collective-permute-start.10 = (bf16[384,768]{1,0:T(8,128)(2,1)}, bf16[384,768]{1,0:T(8,128)(2,1)}, u32[]{:S(2)}, u32[]{:S(2)}) collective-permute-start(bf16[384,768]{1,0:T(8,128)(2,1)} %collective-permute-done.9.refs_10_), channel_id=1, source_target_pairs={{0,32},{1,97},{32,64},{33,1},{64,96},{65,33},{96,0},{97,65},{2,34}... | collective-permute-start | bytes 1769480 | tf_op jit(solution)/shard_map/ppermute | solution.py:43
  95.2 25.3 %collective-permute-start.14 = (bf16[384,768]{1,0:T(8,128)(2,1)}, bf16[384,768]{1,0:T(8,128)(2,1)}, u32[]{:S(2)}, u32[]{:S(2)}) collective-permute-start(bf16[384,768]{1,0:T(8,128)(2,1)} %collective-permute-done.13.refs_14_), channel_id=1, source_target_pairs={{0,32},{1,97},{32,64},{33,1},{64,96},{65,33},{96,0},{97,65},{2,34}... | collective-permute-start | bytes 1769480 | tf_op jit(solution)/shard_map/ppermute | solution.py:43
  101.5 25.3 %collective-permute-start.6 = (bf16[384,768]{1,0:T(8,128)(2,1)}, bf16[384,768]{1,0:T(8,128)(2,1)}, u32[]{:S(2)}, u32[]{:S(2)}) collective-permute-start(bf16[384,768]{1,0:T(8,128)(2,1)} %collective-permute-done.5.refs_6_), channel_id=1, source_target_pairs={{0,32},{1,97},{32,64},{33,1},{64,96},{65,33},{96,0},{97,65},{2,34}... | collective-permute-start | bytes 1769480 | tf_op jit(solution)/shard_map/ppermute | solution.py:43
  175.5 10.0 %collective-permute-start.15 = (bf16[2,128,128]{2,1,0:T(8,128)(2,1)}, bf16[2,128,128]{2,1,0:T(8,128)(2,1)S(1)}, u32[]{:S(2)}, u32[]{:S(2)}) collective-permute-start(bf16[2,128,128]{2,1,0:T(8,128)(2,1)} %get-tuple-element.10), channel_id=1, source_target_pairs={{0,32},{32,64},{64,96},{96,0},{1,33},{33,65},{65,97},{97,1},{2,34}... | collective-permute-start | bytes 196616 | tf_op jit(solution)/shard_map/ppermute | solution.py:26
  175.7 9.7 %collective-permute-start.16 = (bf16[2,128,128]{2,1,0:T(8,128)(2,1)}, bf16[2,128,128]{2,1,0:T(8,128)(2,1)S(1)}, u32[]{:S(2)}, u32[]{:S(2)}) collective-permute-start(bf16[2,128,128]{2,1,0:T(8,128)(2,1)} %get-tuple-element.10), channel_id=1, source_target_pairs={{0,64},{32,96},{64,0},{96,32},{1,65},{33,97},{65,1},{97,33},{2,66}... | collective-permute-start | bytes 196616 | tf_op jit(solution)/shard_map/ppermute | solution.py:26
  178.6 6.8 %collective-permute-start.17 = (bf16[2,128,128]{2,1,0:T(8,128)(2,1)}, bf16[2,128,128]{2,1,0:T(8,128)(2,1)S(1)}, u32[]{:S(2)}, u32[]{:S(2)}) collective-permute-start(bf16[2,128,128]{2,1,0:T(8,128)(2,1)} %get-tuple-element.10), channel_id=1, source_target_pairs={{0,96},{32,0},{64,32},{96,64},{1,97},{33,1},{65,33},{97,65},{2,98}... | collective-permute-start | bytes 196616 | tf_op jit(solution)/shard_map/ppermute | solution.py:26
  193.7 9.1 %collective-permute-start.18 = (f32[2,256]{1,0:T(2,128)S(1)}, f32[2,256]{1,0:T(2,128)S(1)}, u32[]{:S(2)}, u32[]{:S(2)}) collective-permute-start(f32[2,256]{1,0:T(2,128)S(1)} %get-tuple-element.27), channel_id=1, source_target_pairs={{0,8},{8,16},{16,24},{24,0},{1,9},{9,17},{17,25},{25,1},{2,10},{10... | collective-permute-start | bytes 6152 | tf_op jit(solution)/shard_map/ppermute | solution.py:30
  194.0 10.4 %collective-permute-start.19 = (f32[2,256]{1,0:T(2,128)S(1)}, f32[2,256]{1,0:T(2,128)S(1)}, u32[]{:S(2)}, u32[]{:S(2)}) collective-permute-start(f32[2,256]{1,0:T(2,128)S(1)} %get-tuple-element.29), channel_id=1, source_target_pairs={{0,24},{8,0},{16,8},{24,16},{1,25},{9,1},{17,9},{25,17},{2,26},{10... | collective-permute-start | bytes 6152 | tf_op jit(solution)/shard_map/ppermute | solution.py:30
  196.9 7.5 %collective-permute-start.20 = (f32[2,256]{1,0:T(2,128)S(1)}, f32[2,256]{1,0:T(2,128)S(1)}, u32[]{:S(2)}, u32[]{:S(2)}) collective-permute-start(f32[2,256]{1,0:T(2,128)S(1)} %get-tuple-element.28), channel_id=1, source_target_pairs={{0,16},{8,24},{16,0},{24,8},{1,17},{9,25},{17,1},{25,9},{2,18},{10... | collective-permute-start | bytes 6152 | tf_op jit(solution)/shard_map/ppermute | solution.py:30
  199.5 17.3 %collective-permute-start.25 = (bf16[512,256]{1,0:T(8,128)(2,1)S(1)}, bf16[512,256]{1,0:T(8,128)(2,1)S(1)}, u32[]{:S(2)}, u32[]{:S(2)}) collective-permute-start(bf16[512,256]{1,0:T(8,128)(2,1)S(1)} %get-tuple-element.25), channel_id=1, source_target_pairs={{0,8},{8,16},{16,24},{24,0},{1,9},{9,17},{17,25},{25,1},{2,10},{10... | collective-permute-start | bytes 786440 | tf_op jit(solution)/shard_map/ppermute | solution.py:30
  200.9 15.9 %collective-permute-start.26 = (bf16[512,256]{1,0:T(8,128)(2,1)S(1)}, bf16[512,256]{1,0:T(8,128)(2,1)S(1)}, u32[]{:S(2)}, u32[]{:S(2)}) collective-permute-start(bf16[512,256]{1,0:T(8,128)(2,1)S(1)} %get-tuple-element.24), channel_id=1, source_target_pairs={{0,24},{8,0},{16,8},{24,16},{1,25},{9,1},{17,9},{25,17},{2,26},{10... | collective-permute-start | bytes 786440 | tf_op jit(solution)/shard_map/ppermute | solution.py:30
  202.7 14.1 %collective-permute-start.27 = (bf16[512,256]{1,0:T(8,128)(2,1)S(1)}, bf16[512,256]{1,0:T(8,128)(2,1)S(1)}, u32[]{:S(2)}, u32[]{:S(2)}) collective-permute-start(bf16[512,256]{1,0:T(8,128)(2,1)S(1)} %get-tuple-element.23), channel_id=1, source_target_pairs={{0,16},{8,24},{16,0},{24,8},{1,17},{9,25},{17,1},{25,9},{2,18},{10... | collective-permute-start | bytes 786440 | tf_op jit(solution)/shard_map/ppermute | solution.py:30
  205.1 1.2 collective-permute-start.21
  206.3 4.8 %collective-permute-start.22 = (f32[2,256]{1,0:T(2,128)S(1)}, f32[2,256]{1,0:T(2,128)S(1)}, u32[]{:S(2)}, u32[]{:S(2)}) collective-permute-start(f32[2,256]{1,0:T(2,128)S(1)} %add.238), channel_id=1, source_target_pairs={{0,2},{2,4},{4,6},{6,0},{1,3},{3,5},{5,7},{7,1},{8,10},{10,12},{12... | collective-permute-start | bytes 6152 | tf_op jit(solution)/shard_map/ppermute | solution.py:34
  207.8 5.1 %collective-permute-start.23 = (f32[2,256]{1,0:T(2,128)S(1)}, f32[2,256]{1,0:T(2,128)S(1)}, u32[]{:S(2)}, u32[]{:S(2)}) collective-permute-start(f32[2,256]{1,0:T(2,128)S(1)} %add.238), channel_id=1, source_target_pairs={{0,6},{2,0},{4,2},{6,4},{1,7},{3,1},{5,3},{7,5},{8,14},{10,8},{12,... | collective-permute-start | bytes 6152 | tf_op jit(solution)/shard_map/ppermute | solution.py:34
  211.1 5.1 %collective-permute-start.24 = (f32[2,256]{1,0:T(2,128)S(1)}, f32[2,256]{1,0:T(2,128)S(1)}, u32[]{:S(2)}, u32[]{:S(2)}) collective-permute-start(f32[2,256]{1,0:T(2,128)S(1)} %add.238), channel_id=1, source_target_pairs={{0,4},{2,6},{4,0},{6,2},{1,5},{3,7},{5,1},{7,3},{8,12},{10,14},{12... | collective-permute-start | bytes 6152 | tf_op jit(solution)/shard_map/ppermute | solution.py:34
  (13 other events, 340.8 us)
Sparse Core Ops, SparseCore 0:
  9.6 114.7 all-gather.1
where the time goes:
time: 228 us; the launch traced here: 227 us
  waiting for transfers between devices  85.9 us (38%)
  Pallas kernels  63.3 us (28%)
  starting transfers between devices  34.6 us (15%)
  local copies, waits for them, and re-layouts  24.7 us (11%)
  between operations  13.8 us (6%)
  other arithmetic  4.87 us (2%)
    ppermute x15, waiting for transfers between devices, opposed(): return lax.ppermute(a, (axis, 'c'), perm)  79.9 us
    pallas_call x2, Pallas kernels, call_project(): pl.pallas_call(functools.partial(project, spans), out_shape=jax.ShapeDtyp...  43.7 us
    ppermute x15, starting transfers between devices, opposed(): return lax.ppermute(a, (axis, 'c'), perm)  16.1 us
    ppermute x6, starting transfers between devices, move_z(): return lax.ppermute(a, 'z', [(s, (s + d) % 4) for s in range(4)])  8.79 us
    reshape x4, local copies, waits for them, and re-layouts, per_device(): lax.dynamic_slice(wview, (0, 0, at, 0), (WROWS, 3, 1, HH * HDIM))  6.76 us
    pallas_call x1, Pallas kernels, per_device(): pl.pallas_call(inters, out_shape=(jax.ShapeDtypeStruct((GROUP, HH * HDIM)...  6.7 us
    unnamed x35, local copies, waits for them, and re-layouts  5.99 us
    pallas_call x1, Pallas kernels, per_device(): pl.pallas_call(intras, out_shape=jax.ShapeDtypeStruct((GROUP, HH * HDIM),...  5.35 us
  transfers between devices with their start and end apart: 29, of which 14 were waited for; matrix products, arithmetic and copies ran while one was open for 11% of the time, Pallas kernels for 8%

commit v1 on v0

v1 whole, which is shorter than its diff:
```python
import functools

import jax
import jax.numpy as jnp
from jax import lax
from jax.experimental import pallas as pl
from jax.experimental.pallas import tpu as pltpu
from jax.sharding import PartitionSpec as P

AXES = ("y", "z", "x", "c")
HEADS = 64
HDIM = 128
BLOCK = 256
SIDE = 4
SPAN = 512
DEPTH = 6144
WROWS = 384
HH = 2
COLS = 3 * HH * HDIM
GROUP = SIDE * SPAN
NB = GROUP // BLOCK
VMEM = pltpu.CompilerParams(vmem_limit_bytes=56 * 1024 * 1024)


def move_y(a, d):
    return lax.ppermute(a, "y", [(s, (s + d) % 4) for s in range(4)])


def move_z(a, d):
    return lax.ppermute(a, "z", [(s, (s + d) % 4) for s in range(4)])


def move_x(a, d):
    return lax.ppermute(a, "x", [(s, (s + d) % 4) for s in range(4)])


def swap(a):
    return lax.ppermute(a, "c", [(0, 1), (1, 0)])


def opposed(a, axis, d):
    perm = [(2 * s + c, 2 * ((s + d - 2 * d * c) % 4) + c) for s in range(4) for c in range(2)]
    return lax.ppermute(a, (axis, "c"), perm)


ORDER = (
    ("y00", ""),
    ("z1", ""),
    ("z3", ""),
    ("y01", ""),
    ("z2", "z1"),
    ("y02", "z2"),
    ("y10", "y01"),
    ("y30", "y02 z3"),
    ("y11", "y02"),
    ("y31", ""),
    ("y12", "y30"),
    ("y20", "y11"),
    ("y32", "y11"),
    ("y21", "y12"),
    ("y22", ""),
)


def spread_weights(weights):
    got = {"z0": weights[0]}
    for name, after in ORDER:
        if name[0] == "z":
            source = weights[int(name[1])]
        elif name[2] == "0":
            source = got["z" + name[1]]
        else:
            source = got["y" + name[1] + str(int(name[2]) - 1)]
        if after:
            source = lax.optimization_barrier((source, *[got[n] for n in after.split()]))[0]
        got[name] = opposed(source, name[0], int(name[1]) if name[0] == "z" else 1)
    return [
        got[n] for k in range(SIDE) for n in ["z%d" % k] + ["y%d%d" % (k, i) for i in range(3)]
    ]


def along(place, axis, steps):
    return lax.rem(place[axis] + SIDE + steps * (2 * place[3] - 1), SIDE)


def product(spans, place, x, wrefs, cols, wfull, acc, sem):
    step = pl.program_id(0)
    depth = SIDE * WROWS

    @pl.when(step == 0)
    def _():
        for i in range(SIDE):
            for k in range(SIDE):
                at = along(place, 1, i) * SIDE + along(place, 0, k)
                rows = pl.ds(pl.multiple_of(at * WROWS, WROWS), WROWS)
                pltpu.make_async_copy(
                    wrefs[SIDE * k + i].at[:, cols], wfull.at[rows], sem.at[at]
                ).start()
        for i in range(SIDE):
            for k in range(SIDE):
                rows = pl.ds((SIDE * i + k) * WROWS, WROWS)
                pltpu.make_async_copy(
                    wrefs[0].at[:, cols], wfull.at[rows], sem.at[SIDE * i + k]
                ).wait()
            part = jnp.dot(
                x[:, pl.ds(i * depth, depth)],
                wfull[pl.ds(i * depth, depth), :],
                preferred_element_type=jnp.float32,
            )
            if i == 0:
                acc[...] = part
            else:
                acc[...] += part

    if spans > 1:

        @pl.when(step > 0)
        def _():
            acc[...] = jnp.dot(x[...], wfull[...], preferred_element_type=jnp.float32)

    total = acc[...]
    return (total / (1.0 + jnp.exp(-total))).astype(jnp.bfloat16)


def span_of(spans, step, place):
    return place[0] if spans == 1 else lax.rem(place[0] + step + 1, SIDE)


def project_kv(spans, place, x, kf, suffix, before, *refs):
    wrefs = refs[: SIDE * SIDE]
    kv_out, block_out, sum_out, held, wfull, acc, sem = refs[-7:]
    step = pl.program_id(0)
    span = span_of(spans, step, place)
    kv_out[...] = product(
        spans, place, x, wrefs, pl.ds(HH * HDIM, 2 * HH * HDIM), wfull, acc, sem
    )

    @pl.when(step == 0)
    def _():
        held[...] = before[...]

    for b in range(SPAN // BLOCK):
        rows = pl.ds(b * BLOCK, BLOCK)
        for h in range(HH):
            k = kv_out[rows, pl.ds(h * HDIM, HDIM)].astype(jnp.float32)
            v = kv_out[rows, pl.ds((HH + h) * HDIM, HDIM)]
            kd = (k * kf[rows, pl.ds(h, 1)]).astype(jnp.bfloat16)
            kv = lax.dot_general(
                kd, v, (((0,), (0,)), ((), ())), preferred_element_type=jnp.float32
            )
            block_out[b, h] = kv
            held[h] += suffix[h, span * (SPAN // BLOCK) + b] * kv

    @pl.when(step == spans - 1)
    def _():
        sum_out[...] = held[...].astype(sum_out.dtype)


def project_q(spans, place, x, kv, decay, qf, *refs):
    wrefs = refs[: SIDE * SIDE]
    qd_out, intra_out, wfull, acc, sem = refs[-5:]
    q = product(spans, place, x, wrefs, pl.ds(0, HH * HDIM), wfull, acc, sem)
    for b in range(SPAN // BLOCK):
        rows = pl.ds(b * BLOCK, BLOCK)
        for h in range(HH):
            cols = pl.ds(h * HDIM, HDIM)
            qb = q[b * BLOCK : (b + 1) * BLOCK, h * HDIM : (h + 1) * HDIM]
            k = kv[rows, cols]
            v = kv[rows, pl.ds((HH + h) * HDIM, HDIM)]
            scores = lax.dot_general(
                qb, k, (((1,), (1,)), ((), ())), preferred_element_type=jnp.float32
            )
            weights = (scores * decay[b, h]).astype(jnp.bfloat16)
            intra_out[rows, cols] = jnp.dot(weights, v, preferred_element_type=jnp.float32)
            qd_out[rows, cols] = (qb.astype(jnp.float32) * qf[rows, pl.ds(h, 1)]).astype(
                jnp.bfloat16
            )


def call_project(place, rows, w, kf, qf, suffix, decay, before, held):
    spans = SIDE - 1 if held else 1
    near = SPAN // BLOCK
    square = (HDIM, HDIM)
    width = HH * HDIM
    hbm = pl.BlockSpec(memory_space=pl.ANY)
    smem = pl.BlockSpec(memory_space=pltpu.SMEM)

    def there(i, place):
        return (span_of(spans, i, place), 0)

    def blocks(i, place):
        return (span_of(spans, i, place), 0, 0, 0)

    def whole(i, place):
        return (0, 0, 0)

    xspec = pl.BlockSpec((SPAN, DEPTH), there if held else lambda i, place: (i, 0))
    column = pl.BlockSpec((SPAN, HH), there)
    nw = len(w)

    def scratch(cols):
        return [
            pltpu.VMEM((DEPTH, cols), jnp.bfloat16),
            pltpu.VMEM((SPAN, cols), jnp.float32),
            pltpu.SemaphoreType.DMA((SIDE * SIDE,)),
        ]

    def cost(cols):
        return pl.CostEstimate(
            flops=2 * spans * SPAN * DEPTH * cols,
            bytes_accessed=(6 + 8 * spans) << 20,
            transcendentals=0,
        )

    kv, states, total = pl.pallas_call(
        functools.partial(project_kv, spans),
        out_shape=(
            jax.ShapeDtypeStruct((GROUP, 2 * width), jnp.bfloat16),
            jax.ShapeDtypeStruct((NB, HH) + square, jnp.float32),
            jax.ShapeDtypeStruct((HH,) + square, jnp.bfloat16 if held else jnp.float32),
        ),
        grid_spec=pltpu.PrefetchScalarGridSpec(
            num_scalar_prefetch=1,
            grid=(spans,),
            in_specs=[xspec, column, smem, pl.BlockSpec((HH,) + square, whole)]
            + [hbm] * (nw + len(held[:2])),
            out_specs=(
                pl.BlockSpec((SPAN, 2 * width), there),
                pl.BlockSpec((near, HH) + square, blocks),
                pl.BlockSpec((HH,) + square, whole),
            ),
            scratch_shapes=[pltpu.VMEM((HH,) + square, jnp.float32)] + scratch(2 * width),
        ),
        input_output_aliases={5 + nw: 0, 6 + nw: 1} if held else {},
        cost_estimate=cost(2 * width),
        compiler_params=VMEM,
        name="kv_others" if held else "kv_own",
    )(place, rows, kf, suffix, before, *w, *held[:2])
    qd, intra = pl.pallas_call(
        functools.partial(project_q, spans),
        out_shape=(
            jax.ShapeDtypeStruct((GROUP, width), jnp.bfloat16),
            jax.ShapeDtypeStruct((GROUP, width), jnp.float32),
        ),
        grid_spec=pltpu.PrefetchScalarGridSpec(
            num_scalar_prefetch=1,
            grid=(spans,),
            in_specs=[
                xspec,
                pl.BlockSpec((SPAN, 2 * width), there),
                pl.BlockSpec((near, HH, BLOCK, BLOCK), blocks),
                column,
            ]
            + [hbm] * (nw + len(held[2:])),
            out_specs=(pl.BlockSpec((SPAN, width), there), pl.BlockSpec((SPAN, width), there)),
            scratch_shapes=scratch(width),
        ),
        input_output_aliases={5 + nw: 0, 6 + nw: 1} if held else {},
        cost_estimate=cost(width),
        compiler_params=VMEM,
        name="q_others" if held else "q_own",
    )(place, rows, kv, decay, qf, *w, *held[2:])
    return kv, states, total, qd, intra


def decays(cumr, cumc, docr, docc, out):
    row = lax.broadcasted_iota(jnp.int32, (BLOCK, BLOCK), 0)
    col = lax.broadcasted_iota(jnp.int32, (BLOCK, BLOCK), 1)
    mask = (row >= col) & (docc[...] == docr[0])
    for h in range(HH):
        diff = cumc[:, pl.ds(h, 1)] - cumr[0, pl.ds(h, 1), :]
        out[0, h] = jnp.where(mask, jnp.exp(jnp.where(mask, diff, 0.0)), 0.0)


def inters(place, qd, intra, states, passes, fac, s1, s2, s3, *refs):
    outs, squares_outs = refs[:SIDE], refs[SIDE : 2 * SIDE]
    state, att, squares, sem = refs[2 * SIDE :]
    b = pl.program_id(0)

    @pl.when(b == 0)
    def _():
        for h in range(HH):
            state[h] = (
                fac[h, 0] * s1[h].astype(jnp.float32)
                + fac[h, 1] * s2[h].astype(jnp.float32)
                + fac[h, 2] * s3[h].astype(jnp.float32)
            )

    near = SPAN // BLOCK
    span, part = b // near, lax.rem(b, near)
    rows = pl.ds(pl.multiple_of(part * BLOCK, BLOCK), BLOCK)
    sums = jnp.zeros((BLOCK, HDIM), jnp.float32)
    for h in range(HH):
        cols = pl.ds(h * HDIM, HDIM)
        value = intra[:, cols] + jnp.dot(
            qd[:, cols], state[h].astype(jnp.bfloat16), preferred_element_type=jnp.float32
        )
        sums += value * value
        att[span, rows, cols] = value.astype(jnp.bfloat16)
        state[h] = passes[h, b] * state[h] + states[0, h]
    ones = jnp.ones((8, HDIM), jnp.bfloat16)
    total = jnp.zeros((8, BLOCK), jnp.float32)
    for _ in range(3):
        piece = sums.astype(jnp.bfloat16)
        sums = sums - piece.astype(jnp.float32)
        total += lax.dot_general(
            ones, piece, (((1,), (1,)), ((), ())), preferred_element_type=jnp.float32
        )
    squares[span, part] = total

    @pl.when(b == NB - 1)
    def _():
        copies = []
        for i, d in enumerate((0, 1, 3, 2)):
            target = lax.rem(place[0] + d, SIDE)
            copies.append(pltpu.make_async_copy(att.at[target], outs[i], sem.at[2 * i]))
            copies.append(
                pltpu.make_async_copy(squares.at[target], squares_outs[i], sem.at[2 * i + 1])
            )
        for copy in copies:
            copy.start()
        for copy in copies:
            copy.wait()


def finish(place, total, gain, p0, p1, p2, p3, out):
    scale = lax.rsqrt(total[...] / (HEADS * HDIM) + 1e-05)
    for b in range(SPAN // BLOCK):
        rows = pl.ds(b * BLOCK, BLOCK)
        column = jnp.transpose(scale[b])[:, 0:1]
        for dz, piece in ((0, p0), (3, p1), (1, p2), (2, p3)):
            zz = lax.rem(place[0] + dz, SIDE)
            cols = pl.ds(pl.multiple_of(zz * (HH * HDIM), HH * HDIM), HH * HDIM)
            value = piece[rows, :].astype(jnp.float32) * column
            out[rows, cols] = (value * gain[0:1, cols]).astype(jnp.bfloat16)


def doc_of(points, ends):
    found = jnp.sum((points[..., None] >= ends).astype(jnp.int32), axis=-1)
    return jnp.where(points < 0, -1, found)


def per_device(tokens, w_qkv, log_decay, doc_lengths, norm_gain):
    y, z, x, c = [lax.axis_index(axis) for axis in AXES]
    place = jnp.stack([z, y, x, c]).astype(jnp.int32)

    mine = lax.dynamic_slice(tokens, ((2 * x + c) * 64, 0), (64, DEPTH))
    wview = w_qkv.reshape(WROWS, 3, SIDE, HH * HDIM)
    weights = []
    for d in range(SIDE):
        at = (z + d * (1 - 2 * c)) % SIDE
        weights.append(
            lax.dynamic_slice(wview, (0, 0, at, 0), (WROWS, 3, 1, HH * HDIM)).reshape(WROWS, COLS)
        )
    group = lax.all_gather(mine, ("z", "x", "c"), axis=0, tiled=True)
    w = spread_weights(weights)

    ends = jnp.cumsum(doc_lengths)
    nblocks = GROUP * SIDE // BLOCK
    logs = lax.dynamic_slice(log_decay, (HH * z, 0), (HH, GROUP * SIDE))
    cum_all = jnp.cumsum(logs.reshape(HH, nblocks, BLOCK), axis=2)
    starts = jnp.arange(nblocks, dtype=jnp.int32) * BLOCK
    before_all = doc_of(starts - 1, ends)
    last_all = doc_of(starts + (BLOCK - 1), ends)
    pass_all = jnp.where((before_all == last_all)[None], jnp.exp(cum_all[:, :, -1]), 0.0)
    gpass = jnp.prod(pass_all.reshape(HH, SIDE, NB), axis=2)
    f1 = jnp.where(y >= 1, 1.0, 0.0) * jnp.ones((HH,), jnp.float32)
    prev1 = lax.dynamic_index_in_dim(gpass, jnp.maximum(y - 1, 0), 1, keepdims=False)
    prev2 = lax.dynamic_index_in_dim(gpass, jnp.maximum(y - 2, 0), 1, keepdims=False)
    f2 = jnp.where(y >= 2, prev1, 0.0)
    f3 = jnp.where(y >= 3, prev1 * prev2, 0.0)
    fac = jnp.stack([f1, f2, f3], axis=1)
    passes = lax.dynamic_slice_in_dim(pass_all, NB * y, NB, 1)
    suffix = jnp.concatenate(
        [jnp.cumprod(passes[:, :0:-1], axis=1)[:, ::-1], jnp.ones((HH, 1), jnp.float32)], axis=1
    )
    cum = lax.dynamic_slice_in_dim(cum_all, NB * y, NB, 1)
    before = lax.dynamic_slice_in_dim(before_all, NB * y, NB, 0)
    last = lax.dynamic_slice_in_dim(last_all, NB * y, NB, 0)
    points = GROUP * y + jnp.arange(GROUP, dtype=jnp.int32).reshape(NB, BLOCK)
    doc = doc_of(points, ends)
    qfac = jnp.where((doc == before[:, None])[None], jnp.exp(cum), 0.0)
    kfac = jnp.where((doc == last[:, None])[None], jnp.exp(cum[:, :, -1:] - cum), 0.0)
    cumc = cum.reshape(HH, GROUP).T
    qf = qfac.reshape(HH, GROUP).T
    kf = kfac.reshape(HH, GROUP).T
    docc = doc.reshape(GROUP, 1)

    smem = pl.BlockSpec(memory_space=pltpu.SMEM)
    vmem = pl.BlockSpec(memory_space=pltpu.VMEM)
    hbm = pl.BlockSpec(memory_space=pl.ANY)
    square = (HDIM, HDIM)
    decay = pl.pallas_call(
        decays,
        out_shape=jax.ShapeDtypeStruct((NB, HH, BLOCK, BLOCK), jnp.float32),
        grid=(NB,),
        in_specs=[
            pl.BlockSpec((1, HH, BLOCK), lambda b: (b, 0, 0)),
            pl.BlockSpec((BLOCK, HH), lambda b: (b, 0)),
            pl.BlockSpec((1, 1, BLOCK), lambda b: (b, 0, 0)),
            pl.BlockSpec((BLOCK, 1), lambda b: (b, 0)),
        ],
        out_specs=pl.BlockSpec((1, HH, BLOCK, BLOCK), lambda b: (b, 0, 0, 0)),
        name="decays",
    )(jnp.transpose(cum, (1, 0, 2)), cumc, doc[:, None], docc)

    zero = jnp.zeros((HH,) + square, jnp.float32)
    kv, states, total, qd, intra = call_project(
        place, tokens, w, kf, qf, suffix, decay, zero, []
    )
    kv, states, total, qd, intra = call_project(
        place, group, w, kf, qf, suffix, decay, total, [kv, states, qd, intra]
    )
    s1, s2, s3 = move_y(total, 1), move_y(total, 2), move_y(total, 3)

    def block(b, place):
        return (b, 0)

    width = HH * HDIM
    near = SPAN // BLOCK
    summed = (near, 8, BLOCK)
    whole = pl.BlockSpec((HH,) + square, lambda b, place: (0, 0, 0))
    out = pl.pallas_call(
        inters,
        out_shape=[jax.ShapeDtypeStruct((SPAN, width), jnp.bfloat16)] * SIDE
        + [jax.ShapeDtypeStruct(summed, jnp.float32)] * SIDE,
        grid_spec=pltpu.PrefetchScalarGridSpec(
            num_scalar_prefetch=1,
            grid=(NB,),
            in_specs=[
                pl.BlockSpec((BLOCK, width), block),
                pl.BlockSpec((BLOCK, width), block),
                pl.BlockSpec((1, HH) + square, lambda b, place: (b, 0, 0, 0)),
                smem,
                smem,
                whole,
                whole,
                whole,
            ],
            out_specs=[hbm] * (2 * SIDE),
            scratch_shapes=[
                pltpu.VMEM((HH,) + square, jnp.float32),
                pltpu.VMEM((SIDE, SPAN, width), jnp.bfloat16),
                pltpu.VMEM((SIDE,) + summed, jnp.float32),
                pltpu.SemaphoreType.DMA((2 * SIDE,)),
            ],
        ),
        cost_estimate=pl.CostEstimate(flops=1 << 28, bytes_accessed=6 << 20, transcendentals=0),
        compiler_params=VMEM,
        name="inters",
    )(place, qd, intra, states, passes, fac, s1, s2, s3)

    part = out[SIDE]
    for i, d in enumerate((1, -1, 2)):
        part = part + move_z(out[SIDE + 1 + i], d)
    part = part + swap(part)
    part = part + move_x(part, 1) + move_x(part, -1) + move_x(part, 2)
    pieces = [out[0]] + [move_z(out[1 + i], d) for i, d in enumerate((1, -1, 2))]
    return pl.pallas_call(
        finish,
        out_shape=jax.ShapeDtypeStruct((SPAN, SIDE * width), jnp.bfloat16),
        in_specs=[smem] + [vmem] * 6,
        out_specs=vmem,
        cost_estimate=pl.CostEstimate(flops=1 << 22, bytes_accessed=3 << 20, transcendentals=0),
        compiler_params=VMEM,
        name="finish",
    )(place, part, norm_gain.reshape(1, -1), *pieces)


def solution(mesh):
    mesh = jax.sharding.Mesh(mesh.devices.reshape(SIDE, SIDE, SIDE, 2), AXES)
    in_specs = (
        P(("y", "z"), None),
        P(("y", "z"), None, ("x", "c")),
        P(("x", "c"), None),
        P(),
        P(("x", "c")),
    )
    out_specs = P(("y", "z"), ("x", "c"))
    return jax.shard_map(
        per_device, mesh=mesh, in_specs=in_specs, out_specs=out_specs, check_vma=False
    )
```

time: 228 us -> 248 us (1.088)
  Pallas kernels: 63.3 us -> 76.7 us
  starting transfers between devices: 34.6 us -> 47.1 us
  waiting for transfers between devices: 85.9 us -> 80.3 us
    pallas_call x6 -> x7, Pallas kernels: 63.3 us -> 76.7 us  [the longest x2 30.9 us: call_project(): pl.pallas_call(functools.partial(project_kv, spans), out_shape=(jax.Shape...]
    ppermute x15, starting transfers between devices: 16.1 us -> 28 us  [opposed(): return lax.ppermute(a, (axis, 'c'), perm)]
    ppermute x15, waiting for transfers between devices: 79.9 us -> 68.7 us  [opposed(): return lax.ppermute(a, (axis, 'c'), perm)]
    ppermute x6, waiting for transfers between devices: 0.02 us -> 7.01 us  [move_z(): return lax.ppermute(a, 'z', [(s, (s + d) % 4) for s in range(4)])]
    dynamic_slice x3 -> x1, local copies, waits for them, and re-layouts: 2.81 us -> 0.03 us  [per_device(): logs = lax.dynamic_slice(log_decay, (HH * z, 0), (HH, GROUP * SIDE))]
    reshape x4 -> x3, local copies, waits for them, and re-layouts: 6.76 us -> 4.61 us  [per_device(): lax.dynamic_slice(wview, (0, 0, at, 0), (WROWS, 3, 1, HH * HDIM))]
    unnamed x35 -> x39, local copies, waits for them, and re-layouts: 5.99 us -> 6.73 us
  transfers between devices with their start and end apart: 29 -> 29, of which waited for: 14 -> 16; matrix products, arithmetic and copies ran while one was open for 11% -> 9% of each run, Pallas kernels for 8% -> 19%
where the time goes in v1:
time: 248 us; the launch traced here: 246 us
  waiting for transfers between devices  80.3 us (32%)
  Pallas kernels  76.7 us (31%)
  starting transfers between devices  47.1 us (19%)
  local copies, waits for them, and re-layouts  22.8 us (9%)
  between operations  13.8 us (6%)
  other arithmetic  5.55 us (2%)
    ppermute x15, waiting for transfers between devices, opposed(): return lax.ppermute(a, (axis, 'c'), perm)  68.7 us
    pallas_call x2, Pallas kernels, call_project(): pl.pallas_call(functools.partial(project_kv, spans), out_shape=(jax.Shape...  30.9 us
    pallas_call x2, Pallas kernels, call_project(): pl.pallas_call(functools.partial(project_q, spans), out_shape=(jax.ShapeD...  28.3 us
    ppermute x15, starting transfers between devices, opposed(): return lax.ppermute(a, (axis, 'c'), perm)  28 us
    pallas_call x1, Pallas kernels, per_device(): pl.pallas_call(inters, out_shape=[jax.ShapeDtypeStruct((SPAN, width), jnp...  7.86 us
    ppermute x6, waiting for transfers between devices, move_z(): return lax.ppermute(a, 'z', [(s, (s + d) % 4) for s in range(4)])  7.01 us
    pallas_call x1, Pallas kernels, per_device(): pl.pallas_call(decays, out_shape=jax.ShapeDtypeStruct((NB, HH, BLOCK, BLO...  6.99 us
    ppermute x3, starting transfers between devices, move_y(): return lax.ppermute(a, 'y', [(s, (s + d) % 4) for s in range(4)])  6.73 us
  transfers between devices with their start and end apart: 29, of which 16 were waited for; matrix products, arithmetic and copies ran while one was open for 9% of the time, Pallas kernels for 19%

profile of v1, /device:TPU:0, one launch (start us, length us, event | category | flops | bytes accessed | tf_op | source)
XLA Modules:
  0.0 246.2 jit_solution(10002989035857714519)
XLA Ops:
  6.5 2.1 constant_dynamic-slice_fusion.10
  8.8 3.0 %copy.83 = bf16[384,3,1024]{0,2,1:T(8,128)(2,1)S(1)} copy(bf16[384,3,1024]{2,0,1:T(8,128)(2,1)} %param.6) | data formatting | bytes 4718592 | tf_op args[1]
  13.1 2.2 copy.85
  15.3 2.0 collective-permute-start.2
  21.4 2.1 collective-permute-start.7
  24.0 5.4 %collective-permute-done.2.refs_4_ = bf16[384,768]{1,0:T(8,128)(2,1)S(1)} collective-permute-done((bf16[384,768]{1,0:T(8,128)(2,1)}, bf16[384,768]{1,0:T(8,128)(2,1)S(1)}, u32[]{:S(2)}, u32[]{:S(2)}) %collective-permute-start.2) | collective-permute-done | bytes 589856 | tf_op jit(solution)/shard_map/ppermute | solution.py:43
  30.4 6.1 %collective-permute-start.3 = (bf16[384,768]{1,0:T(8,128)(2,1)}, bf16[384,768]{1,0:T(8,128)(2,1)S(1)}, u32[]{:S(2)}, u32[]{:S(2)}) collective-permute-start(bf16[384,768]{1,0:T(8,128)(2,1)} %copy.86), channel_id=1, source_target_pairs={{0,16},{1,17},{8,24},{9,25},{16,0},{17,1},{24,8},{25,9},{2,18},{3,... | collective-permute-start | bytes 1769480 | tf_op jit(solution)/shard_map/ppermute | solution.py:43
  36.5 6.7 %collective-permute-start.1 = (bf16[384,768]{1,0:T(8,128)(2,1)S(1)}, bf16[384,768]{1,0:T(8,128)(2,1)}, u32[]{:S(2)}, u32[]{:S(2)}) collective-permute-start(bf16[384,768]{1,0:T(8,128)(2,1)S(1)} %collective-permute-done.refs_1_), channel_id=1, source_target_pairs={{0,32},{1,97},{32,64},{33,1},{64,96},{65,33},{96,0},{97,65},{2,34}... | collective-permute-start | bytes 1769480 | tf_op jit(solution)/shard_map/ppermute | solution.py:43
  44.7 7.5 %collective-permute-done.1.refs_2_ = bf16[384,768]{1,0:T(8,128)(2,1)} collective-permute-done((bf16[384,768]{1,0:T(8,128)(2,1)S(1)}, bf16[384,768]{1,0:T(8,128)(2,1)}, u32[]{:S(2)}, u32[]{:S(2)}) %collective-permute-start.1) | collective-permute-done | bytes 589856 | tf_op jit(solution)/shard_map/ppermute | solution.py:43
  52.2 5.2 %collective-permute-done.3.refs_8_ = bf16[384,768]{1,0:T(8,128)(2,1)S(1)} collective-permute-done((bf16[384,768]{1,0:T(8,128)(2,1)}, bf16[384,768]{1,0:T(8,128)(2,1)S(1)}, u32[]{:S(2)}, u32[]{:S(2)}) %collective-permute-start.3) | collective-permute-done | bytes 589856 | tf_op jit(solution)/shard_map/ppermute | solution.py:43
  57.4 4.1 %collective-permute-start.4 = (bf16[384,768]{1,0:T(8,128)(2,1)}, bf16[384,768]{1,0:T(8,128)(2,1)}, u32[]{:S(2)}, u32[]{:S(2)}) collective-permute-start(bf16[384,768]{1,0:T(8,128)(2,1)} %collective-permute-done.1.refs_2_), channel_id=1, source_target_pairs={{0,32},{1,97},{32,64},{33,1},{64,96},{65,33},{96,0},{97,65},{2,34}... | collective-permute-start | bytes 1769480 | tf_op jit(solution)/shard_map/ppermute | solution.py:43
  63.5 7.3 %collective-permute-done.4.refs_3_ = bf16[384,768]{1,0:T(8,128)(2,1)} collective-permute-done((bf16[384,768]{1,0:T(8,128)(2,1)}, bf16[384,768]{1,0:T(8,128)(2,1)}, u32[]{:S(2)}, u32[]{:S(2)}) %collective-permute-start.4) | collective-permute-done | bytes 589856 | tf_op jit(solution)/shard_map/ppermute | solution.py:43
  70.8 6.3 %collective-permute-done.5.refs_5_ = bf16[384,768]{1,0:T(8,128)(2,1)} collective-permute-done((bf16[384,768]{1,0:T(8,128)(2,1)S(1)}, bf16[384,768]{1,0:T(8,128)(2,1)}, u32[]{:S(2)}, u32[]{:S(2)}) %collective-permute-start.5) | collective-permute-done | bytes 589856 | tf_op jit(solution)/shard_map/ppermute | solution.py:43
  79.6 8.9 %collective-permute-done.6.refs_6_ = bf16[384,768]{1,0:T(8,128)(2,1)} collective-permute-done((bf16[384,768]{1,0:T(8,128)(2,1)}, bf16[384,768]{1,0:T(8,128)(2,1)}, u32[]{:S(2)}, u32[]{:S(2)}) %collective-permute-start.6) | collective-permute-done | bytes 589856 | tf_op jit(solution)/shard_map/ppermute | solution.py:43
  88.5 6.2 %collective-permute-done.8.refs_13_ = bf16[384,768]{1,0:T(8,128)(2,1)S(1)} collective-permute-done((bf16[384,768]{1,0:T(8,128)(2,1)S(1)}, bf16[384,768]{1,0:T(8,128)(2,1)S(1)}, u32[]{:S(2)}, u32[]{:S(2)}) %collective-permute-start.8) | collective-permute-done | bytes 589856 | tf_op jit(solution)/shard_map/ppermute | solution.py:43
  97.2 4.0 %collective-permute-done.10.refs_9_ = bf16[384,768]{1,0:T(8,128)(2,1)} collective-permute-done((bf16[384,768]{1,0:T(8,128)(2,1)S(1)}, bf16[384,768]{1,0:T(8,128)(2,1)}, u32[]{:S(2)}, u32[]{:S(2)}) %collective-permute-start.10) | collective-permute-done | bytes 589856 | tf_op jit(solution)/shard_map/ppermute | solution.py:43
  101.2 6.3 %collective-permute-done.9.refs_7_ = bf16[384,768]{1,0:T(8,128)(2,1)} collective-permute-done((bf16[384,768]{1,0:T(8,128)(2,1)}, bf16[384,768]{1,0:T(8,128)(2,1)}, u32[]{:S(2)}, u32[]{:S(2)}) %collective-permute-start.9) | collective-permute-done | bytes 589856 | tf_op jit(solution)/shard_map/ppermute | solution.py:43
  108.5 5.3 %collective-permute-done.13.refs_14_ = bf16[384,768]{1,0:T(8,128)(2,1)} collective-permute-done((bf16[384,768]{1,0:T(8,128)(2,1)}, bf16[384,768]{1,0:T(8,128)(2,1)}, u32[]{:S(2)}, u32[]{:S(2)}) %collective-permute-start.13) | collective-permute-done | bytes 589856 | tf_op jit(solution)/shard_map/ppermute | solution.py:43
  113.8 6.3 %collective-permute-done.11.refs_10_ = bf16[384,768]{1,0:T(8,128)(2,1)} collective-permute-done((bf16[384,768]{1,0:T(8,128)(2,1)}, bf16[384,768]{1,0:T(8,128)(2,1)}, u32[]{:S(2)}, u32[]{:S(2)}) %collective-permute-start.11) | collective-permute-done | bytes 589856 | tf_op jit(solution)/shard_map/ppermute | solution.py:43
  126.8 7.0 %decays.1.decay = f32[8,2,256,256]{3,2,1,0:T(8,128)} custom-call(f32[8,2,256]{2,1,0:T(2,128)} %bitcast.45, f32[2048,2]{1,0:T(8,128)} %bitcast.39, s32[8,1,256]{2,1,0:T(1,128)} %compare_select_fusion.docr, s32[2048,1]{1,0:T(8,128)} %bitcast.40), custom_call_target="tpu_custom_call" | custom-call | tf_op jit(solution)/shard_map/decays/pallas_call | solution.py:393
  136.0 10.4 %kv_own.1 = (bf16[2048,512]{1,0:T(8,128)(2,1)}, f32[8,2,128,128]{3,2,1,0:T(8,128)}, f32[2,128,128]{2,1,0:T(8,128)}) custom-call(s32[4]{0:T(128)} %pad_add_fusion.place, bf16[512,6144]{1,0:T(8,128)(2,1)} %x.5, f32[2048,2]{1,0:T(8,128)} %bitcast.36, f32[2,8]{1,0:T(2,128)} %concatenate.3.suffix, f32[2,128,128]{2,1,0:T(8,128)} %broadcast_in_dim.73.before, ...), custom_call_target="tpu_custom_call" | custom-call | flops 3221225472 | bytes 14680064 | tf_op jit(solution)/shard_map/kv_own/pallas_call | solution.py:215
  146.4 10.3 %q_own.1 = (bf16[2048,256]{1,0:T(8,128)(2,1)}, f32[2048,256]{1,0:T(8,128)}) custom-call(s32[4]{0:T(128)} %pad_add_fusion.place, bf16[512,6144]{1,0:T(8,128)(2,1)} %x.5, bf16[2048,512]{1,0:T(8,128)(2,1)} %get-tuple-element.42.refs_16_.kv, f32[8,2,256,256]{3,2,1,0:T(8,128)} %decays.1.decay, f32[2048,2]{1,0:T(8,128)} %bitcast.34, bf16[384,768]{1,0:T(8,128)(2,1)} %copy-done.2, ...), custom_call_target="tpu_custom_call" | custom-call | flops 1610612736 | bytes 14680064 | tf_op jit(solution)/shard_map/q_own/pallas_call | solution.py:239
  156.8 20.5 %kv_others.1 = (bf16[2048,512]{1,0:T(8,128)(2,1)}, f32[8,2,128,128]{3,2,1,0:T(8,128)}, bf16[2,128,128]{2,1,0:T(8,128)(2,1)}) custom-call(s32[4]{0:T(128)} %pad_add_fusion.place, bf16[2048,6144]{1,0:T(8,128)(2,1)} %all-gather.2.cloned.1.call-done.x, f32[2048,2]{1,0:T(8,128)} %bitcast.37, ...), custom_call_target="tpu_custom_call", output_to_operand_aliasing={{0}: (21, {}), {1}: (22, {})} | custom-call | flops 9663676416 | bytes 31457280 | tf_op jit(solution)/shard_map/kv_others/pallas_call | solution.py:215
  177.3 5.8 %collective-permute-start.17 = (bf16[2,128,128]{2,1,0:T(8,128)(2,1)}, bf16[2,128,128]{2,1,0:T(8,128)(2,1)S(1)}, u32[]{:S(2)}, u32[]{:S(2)}) collective-permute-start(bf16[2,128,128]{2,1,0:T(8,128)(2,1)} %get-tuple-element.50), channel_id=1, source_target_pairs={{0,96},{32,0},{64,32},{96,64},{1,97},{33,1},{65,33},{97,65},{2,98}... | collective-permute-start | bytes 196616 | tf_op jit(solution)/shard_map/ppermute | solution.py:26
  184.0 17.9 %q_others.1 = (bf16[2048,256]{1,0:T(8,128)(2,1)}, f32[2048,256]{1,0:T(8,128)}) custom-call(s32[4]{0:T(128)} %pad_add_fusion.place, bf16[2048,6144]{1,0:T(8,128)(2,1)} %all-gather.2.cloned.1.call-done.x, bf16[2048,512]{1,0:T(8,128)(2,1)} %get-tuple-element.44.kv, f32[8,2,256,256]{3,2,1,0:T(8,128)} %decays.1.decay, ...), custom_call_target="tpu_custom_call", output_to_operand_aliasing={{0}: (21, {}), {1}: (22, {})} | custom-call | flops 4831838208 | bytes 31457280 | tf_op jit(solution)/shard_map/q_others/pallas_call | solution.py:239
  202.7 7.9 %inters.1 = (bf16[512,256]{1,0:T(8,128)(2,1)}, bf16[512,256]{1,0:T(8,128)(2,1)}, bf16[512,256]{1,0:T(8,128)(2,1)}, bf16[512,256]{1,0:T(8,128)(2,1)}, f32[2,8,256...) custom-call(s32[4]{0:T(128)} %pad_add_fusion.place, ...), custom_call_target="tpu_custom_call" | custom-call | flops 268435456 | bytes 6291456 | tf_op jit(solution)/shard_map/inters/pallas_call | solution.py:423
  210.7 3.2 %collective-permute-start.19 = (f32[2,8,256]{2,1,0:T(8,128)}, f32[2,8,256]{2,1,0:T(8,128)S(1)}, u32[]{:S(2)}, u32[]{:S(2)}) collective-permute-start(f32[2,8,256]{2,1,0:T(8,128)} %get-tuple-element.53), channel_id=1, source_target_pairs={{0,24},{8,0},{16,8},{24,16},{1,25},{9,1},{17,9},{25,17},{2,26},{10... | collective-permute-start | bytes 49160 | tf_op jit(solution)/shard_map/ppermute | solution.py:30
  215.8 3.5 %collective-permute-done.20 = f32[2,8,256]{2,1,0:T(8,128)S(1)} collective-permute-done((f32[2,8,256]{2,1,0:T(8,128)}, f32[2,8,256]{2,1,0:T(8,128)S(1)}, u32[]{:S(2)}, u32[]{:S(2)}) %collective-permute-start.20) | collective-permute-done | bytes 16416 | tf_op jit(solution)/shard_map/ppermute | solution.py:30
  220.1 3.2 %collective-permute-start.26 = (bf16[512,256]{1,0:T(8,128)(2,1)}, bf16[512,256]{1,0:T(8,128)(2,1)S(1)}, u32[]{:S(2)}, u32[]{:S(2)}) collective-permute-start(bf16[512,256]{1,0:T(8,128)(2,1)} %get-tuple-element.57), channel_id=1, source_target_pairs={{0,24},{8,0},{16,8},{24,16},{1,25},{9,1},{17,9},{25,17},{2,26},{10... | collective-permute-start | bytes 786440 | tf_op jit(solution)/shard_map/ppermute | solution.py:30
  223.4 3.1 %collective-permute-start.24 = (f32[2,8,256]{2,1,0:T(8,128)S(1)}, f32[2,8,256]{2,1,0:T(8,128)S(1)}, u32[]{:S(2)}, u32[]{:S(2)}) collective-permute-start(f32[2,8,256]{2,1,0:T(8,128)S(1)} %add.198), channel_id=1, source_target_pairs={{0,4},{2,6},{4,0},{6,2},{1,5},{3,7},{5,1},{7,3},{8,12},{10,14},{12... | collective-permute-start | bytes 49160 | tf_op jit(solution)/shard_map/ppermute | solution.py:34
  230.2 3.4 %collective-permute-done.22 = f32[2,8,256]{2,1,0:T(8,128)S(1)} collective-permute-done((f32[2,8,256]{2,1,0:T(8,128)S(1)}, f32[2,8,256]{2,1,0:T(8,128)S(1)}, u32[]{:S(2)}, u32[]{:S(2)}) %collective-permute-start.22) | collective-permute-done | bytes 16416 | tf_op jit(solution)/shard_map/ppermute | solution.py:34
  236.7 2.7 %finish.1 = bf16[512,1024]{1,0:T(8,128)(2,1)} custom-call(s32[4]{0:T(128)} %pad_add_fusion.place, f32[2,8,256]{2,1,0:T(8,128)} %add_add_fusion.total, f32[1,1024]{1,0:T(1,128)} %bitcast.48, bf16[512,256]{1,0:T(8,128)(2,1)} %get-tuple-element.55.p0, bf16[512,256]{1,0:T(8,128)(2,1)} %copy-done.10, bf16[512,256]{1,0:T(8,128)(2,1)} %copy-done.11, ...), custom_call_target="tpu_custom_call" | custom-call | flops 4194304 | bytes 3145728 | tf_op jit(solution)/shard_map/finish/pallas_call | solution.py:459
  (132 shorter events, 36.4 us)
Async XLA Ops:
  6.5 150.2 %all-gather.2.cloned.1.call-start = ((), (), s32[]{:S(2)}) async-start(), calls=%async_computation | async-start | bytes 25952256 | tf_op jit(solution)/shard_map/all_gather | solution.py:355
  15.3 14.0 %collective-permute-start.2 = (bf16[384,768]{1,0:T(8,128)(2,1)}, bf16[384,768]{1,0:T(8,128)(2,1)S(1)}, u32[]{:S(2)}, u32[]{:S(2)}) collective-permute-start(bf16[384,768]{1,0:T(8,128)(2,1)} %copy.85), channel_id=1, source_target_pairs={{0,8},{1,25},{8,16},{9,1},{16,24},{17,9},{24,0},{25,17},{2,10},{3,... | collective-permute-start | bytes 1769480 | tf_op jit(solution)/shard_map/ppermute | solution.py:43
  18.6 103.1 %copy-start.2 = (bf16[384,768]{1,0:T(8,128)(2,1)}, bf16[384,768]{1,0:T(8,128)(2,1)S(1)}, u32[]{:S(2)}) copy-start(bf16[384,768]{1,0:T(8,128)(2,1)S(1)} %copy.88.refs_0_) | copy-start | bytes 1769476
  18.6 17.9 %collective-permute-start = (bf16[384,768]{1,0:T(8,128)(2,1)S(1)}, bf16[384,768]{1,0:T(8,128)(2,1)S(1)}, u32[]{:S(2)}, u32[]{:S(2)}) collective-permute-start(bf16[384,768]{1,0:T(8,128)(2,1)S(1)} %copy.88.refs_0_), channel_id=1, source_target_pairs={{0,32},{1,97},{32,64},{33,1},{64,96},{65,33},{96,0},{97,65},{2,34}... | collective-permute-start | bytes 1769480 | tf_op jit(solution)/shard_map/ppermute | solution.py:43
  21.4 56.6 %collective-permute-start.7 = (bf16[384,768]{1,0:T(8,128)(2,1)}, bf16[384,768]{1,0:T(8,128)(2,1)S(1)}, u32[]{:S(2)}, u32[]{:S(2)}) collective-permute-start(bf16[384,768]{1,0:T(8,128)(2,1)} %copy.87), channel_id=1, source_target_pairs={{0,24},{1,9},{8,0},{9,17},{16,8},{17,25},{24,16},{25,1},{2,26},{3,... | collective-permute-start | bytes 1769480 | tf_op jit(solution)/shard_map/ppermute | solution.py:43
  29.3 96.1 %copy-start.3 = (bf16[384,768]{1,0:T(8,128)(2,1)}, bf16[384,768]{1,0:T(8,128)(2,1)S(1)}, u32[]{:S(2)}) copy-start(bf16[384,768]{1,0:T(8,128)(2,1)S(1)} %collective-permute-done.2.refs_4_) | copy-start | bytes 1769476
  30.4 27.0 %collective-permute-start.3 = (bf16[384,768]{1,0:T(8,128)(2,1)}, bf16[384,768]{1,0:T(8,128)(2,1)S(1)}, u32[]{:S(2)}, u32[]{:S(2)}) collective-permute-start(bf16[384,768]{1,0:T(8,128)(2,1)} %copy.86), channel_id=1, source_target_pairs={{0,16},{1,17},{8,24},{9,25},{16,0},{17,1},{24,8},{25,9},{2,18},{3,... | collective-permute-start | bytes 1769480 | tf_op jit(solution)/shard_map/ppermute | solution.py:43
  36.5 90.3 %copy-start.4 = (bf16[384,768]{1,0:T(8,128)(2,1)}, bf16[384,768]{1,0:T(8,128)(2,1)S(1)}, u32[]{:S(2)}) copy-start(bf16[384,768]{1,0:T(8,128)(2,1)S(1)} %collective-permute-done.refs_1_) | copy-start | bytes 1769476
  36.5 15.7 %collective-permute-start.1 = (bf16[384,768]{1,0:T(8,128)(2,1)S(1)}, bf16[384,768]{1,0:T(8,128)(2,1)}, u32[]{:S(2)}, u32[]{:S(2)}) collective-permute-start(bf16[384,768]{1,0:T(8,128)(2,1)S(1)} %collective-permute-done.refs_1_), channel_id=1, source_target_pairs={{0,32},{1,97},{32,64},{33,1},{64,96},{65,33},{96,0},{97,65},{2,34}... | collective-permute-start | bytes 1769480 | tf_op jit(solution)/shard_map/ppermute | solution.py:43
  57.4 13.4 %collective-permute-start.4 = (bf16[384,768]{1,0:T(8,128)(2,1)}, bf16[384,768]{1,0:T(8,128)(2,1)}, u32[]{:S(2)}, u32[]{:S(2)}) collective-permute-start(bf16[384,768]{1,0:T(8,128)(2,1)} %collective-permute-done.1.refs_2_), channel_id=1, source_target_pairs={{0,32},{1,97},{32,64},{33,1},{64,96},{65,33},{96,0},{97,65},{2,34}... | collective-permute-start | bytes 1769480 | tf_op jit(solution)/shard_map/ppermute | solution.py:43
  61.5 15.6 %collective-permute-start.5 = (bf16[384,768]{1,0:T(8,128)(2,1)S(1)}, bf16[384,768]{1,0:T(8,128)(2,1)}, u32[]{:S(2)}, u32[]{:S(2)}) collective-permute-start(bf16[384,768]{1,0:T(8,128)(2,1)S(1)} %collective-permute-done.2.refs_4_), channel_id=1, source_target_pairs={{0,32},{1,97},{32,64},{33,1},{64,96},{65,33},{96,0},{97,65},{2,34}... | collective-permute-start | bytes 1769480 | tf_op jit(solution)/shard_map/ppermute | solution.py:43
  77.1 11.4 %collective-permute-start.6 = (bf16[384,768]{1,0:T(8,128)(2,1)}, bf16[384,768]{1,0:T(8,128)(2,1)}, u32[]{:S(2)}, u32[]{:S(2)}) collective-permute-start(bf16[384,768]{1,0:T(8,128)(2,1)} %collective-permute-done.5.refs_5_), channel_id=1, source_target_pairs={{0,32},{1,97},{32,64},{33,1},{64,96},{65,33},{96,0},{97,65},{2,34}... | collective-permute-start | bytes 1769480 | tf_op jit(solution)/shard_map/ppermute | solution.py:43
  78.0 16.7 %collective-permute-start.8 = (bf16[384,768]{1,0:T(8,128)(2,1)S(1)}, bf16[384,768]{1,0:T(8,128)(2,1)S(1)}, u32[]{:S(2)}, u32[]{:S(2)}) collective-permute-start(bf16[384,768]{1,0:T(8,128)(2,1)S(1)} %collective-permute-done.7.refs_12_), channel_id=1, source_target_pairs={{0,32},{1,97},{32,64},{33,1},{64,96},{65,33},{96,0},{97,65},{2,34}... | collective-permute-start | bytes 1769480 | tf_op jit(solution)/shard_map/ppermute | solution.py:43
  88.5 12.6 %collective-permute-start.10 = (bf16[384,768]{1,0:T(8,128)(2,1)S(1)}, bf16[384,768]{1,0:T(8,128)(2,1)}, u32[]{:S(2)}, u32[]{:S(2)}) collective-permute-start(bf16[384,768]{1,0:T(8,128)(2,1)S(1)} %collective-permute-done.3.refs_8_), channel_id=1, source_target_pairs={{0,32},{1,97},{32,64},{33,1},{64,96},{65,33},{96,0},{97,65},{2,34}... | collective-permute-start | bytes 1769480 | tf_op jit(solution)/shard_map/ppermute | solution.py:43
  95.6 11.9 %collective-permute-start.9 = (bf16[384,768]{1,0:T(8,128)(2,1)}, bf16[384,768]{1,0:T(8,128)(2,1)}, u32[]{:S(2)}, u32[]{:S(2)}) collective-permute-start(bf16[384,768]{1,0:T(8,128)(2,1)} %collective-permute-done.6.refs_6_), channel_id=1, source_target_pairs={{0,32},{1,97},{32,64},{33,1},{64,96},{65,33},{96,0},{97,65},{2,34}... | collective-permute-start | bytes 1769480 | tf_op jit(solution)/shard_map/ppermute | solution.py:43
  95.9 17.9 %collective-permute-start.13 = (bf16[384,768]{1,0:T(8,128)(2,1)}, bf16[384,768]{1,0:T(8,128)(2,1)}, u32[]{:S(2)}, u32[]{:S(2)}) collective-permute-start(bf16[384,768]{1,0:T(8,128)(2,1)} %copy-done.7), channel_id=1, source_target_pairs={{0,32},{1,97},{32,64},{33,1},{64,96},{65,33},{96,0},{97,65},{2,34}... | collective-permute-start | bytes 1769480 | tf_op jit(solution)/shard_map/ppermute | solution.py:43
  107.5 12.6 %collective-permute-start.11 = (bf16[384,768]{1,0:T(8,128)(2,1)}, bf16[384,768]{1,0:T(8,128)(2,1)}, u32[]{:S(2)}, u32[]{:S(2)}) collective-permute-start(bf16[384,768]{1,0:T(8,128)(2,1)} %collective-permute-done.10.refs_9_), channel_id=1, source_target_pairs={{0,32},{1,97},{32,64},{33,1},{64,96},{65,33},{96,0},{97,65},{2,34}... | collective-permute-start | bytes 1769480 | tf_op jit(solution)/shard_map/ppermute | solution.py:43
  113.8 21.5 %collective-permute-start.14 = (bf16[384,768]{1,0:T(8,128)(2,1)}, bf16[384,768]{1,0:T(8,128)(2,1)}, u32[]{:S(2)}, u32[]{:S(2)}) collective-permute-start(bf16[384,768]{1,0:T(8,128)(2,1)} %collective-permute-done.13.refs_14_), channel_id=1, source_target_pairs={{0,32},{1,97},{32,64},{33,1},{64,96},{65,33},{96,0},{97,65},{2,34}... | collective-permute-start | bytes 1769480 | tf_op jit(solution)/shard_map/ppermute | solution.py:43
  120.1 15.2 %collective-permute-start.12 = (bf16[384,768]{1,0:T(8,128)(2,1)}, bf16[384,768]{1,0:T(8,128)(2,1)}, u32[]{:S(2)}, u32[]{:S(2)}) collective-permute-start(bf16[384,768]{1,0:T(8,128)(2,1)} %collective-permute-done.11.refs_10_), channel_id=1, source_target_pairs={{0,32},{1,97},{32,64},{33,1},{64,96},{65,33},{96,0},{97,65},{2,34}... | collective-permute-start | bytes 1769480 | tf_op jit(solution)/shard_map/ppermute | solution.py:43
  177.3 24.7 %collective-permute-start.17 = (bf16[2,128,128]{2,1,0:T(8,128)(2,1)}, bf16[2,128,128]{2,1,0:T(8,128)(2,1)S(1)}, u32[]{:S(2)}, u32[]{:S(2)}) collective-permute-start(bf16[2,128,128]{2,1,0:T(8,128)(2,1)} %get-tuple-element.50), channel_id=1, source_target_pairs={{0,96},{32,0},{64,32},{96,64},{1,97},{33,1},{65,33},{97,65},{2,98}... | collective-permute-start | bytes 196616 | tf_op jit(solution)/shard_map/ppermute | solution.py:26
  183.1 18.9 %collective-permute-start.16 = (bf16[2,128,128]{2,1,0:T(8,128)(2,1)}, bf16[2,128,128]{2,1,0:T(8,128)(2,1)S(1)}, u32[]{:S(2)}, u32[]{:S(2)}) collective-permute-start(bf16[2,128,128]{2,1,0:T(8,128)(2,1)} %get-tuple-element.50), channel_id=1, source_target_pairs={{0,64},{32,96},{64,0},{96,32},{1,65},{33,97},{65,1},{97,33},{2,66}... | collective-permute-start | bytes 196616 | tf_op jit(solution)/shard_map/ppermute | solution.py:26
  183.1 18.9 %collective-permute-start.15 = (bf16[2,128,128]{2,1,0:T(8,128)(2,1)}, bf16[2,128,128]{2,1,0:T(8,128)(2,1)S(1)}, u32[]{:S(2)}, u32[]{:S(2)}) collective-permute-start(bf16[2,128,128]{2,1,0:T(8,128)(2,1)} %get-tuple-element.50), channel_id=1, source_target_pairs={{0,32},{32,64},{64,96},{96,0},{1,33},{33,65},{65,97},{97,1},{2,34}... | collective-permute-start | bytes 196616 | tf_op jit(solution)/shard_map/ppermute | solution.py:26
  210.5 5.2 %collective-permute-start.18 = (f32[2,8,256]{2,1,0:T(8,128)}, f32[2,8,256]{2,1,0:T(8,128)S(1)}, u32[]{:S(2)}, u32[]{:S(2)}) collective-permute-start(f32[2,8,256]{2,1,0:T(8,128)} %get-tuple-element.52), channel_id=1, source_target_pairs={{0,8},{8,16},{16,24},{24,0},{1,9},{9,17},{17,25},{25,1},{2,10},{10... | collective-permute-start | bytes 49160 | tf_op jit(solution)/shard_map/ppermute | solution.py:30
  210.7 5.1 %collective-permute-start.19 = (f32[2,8,256]{2,1,0:T(8,128)}, f32[2,8,256]{2,1,0:T(8,128)S(1)}, u32[]{:S(2)}, u32[]{:S(2)}) collective-permute-start(f32[2,8,256]{2,1,0:T(8,128)} %get-tuple-element.53), channel_id=1, source_target_pairs={{0,24},{8,0},{16,8},{24,16},{1,25},{9,1},{17,9},{25,17},{2,26},{10... | collective-permute-start | bytes 49160 | tf_op jit(solution)/shard_map/ppermute | solution.py:30
  213.8 5.5 %collective-permute-start.20 = (f32[2,8,256]{2,1,0:T(8,128)}, f32[2,8,256]{2,1,0:T(8,128)S(1)}, u32[]{:S(2)}, u32[]{:S(2)}) collective-permute-start(f32[2,8,256]{2,1,0:T(8,128)} %get-tuple-element.54), channel_id=1, source_target_pairs={{0,16},{8,24},{16,0},{24,8},{1,17},{9,25},{17,1},{25,9},{2,18},{10... | collective-permute-start | bytes 49160 | tf_op jit(solution)/shard_map/ppermute | solution.py:30
  220.0 3.3 %collective-permute-start.21 = (f32[2,8,256]{2,1,0:T(8,128)S(1)}, f32[2,8,256]{2,1,0:T(8,128)S(1)}, u32[]{:S(2)}, u32[]{:S(2)}) collective-permute-start(f32[2,8,256]{2,1,0:T(8,128)S(1)} %add_add_fusion.1), channel_id=1, source_target_pairs={{0,1},{1,0},{2,3},{3,2},{4,5},{5,4},{6,7},{7,6},{8,9},{9,8},{10,11... | collective-permute-start | bytes 49160 | tf_op jit(solution)/shard_map/ppermute | solution.py:38
  220.0 15.8 %collective-permute-start.25 = (bf16[512,256]{1,0:T(8,128)(2,1)}, bf16[512,256]{1,0:T(8,128)(2,1)S(1)}, u32[]{:S(2)}, u32[]{:S(2)}) collective-permute-start(bf16[512,256]{1,0:T(8,128)(2,1)} %get-tuple-element.56), channel_id=1, source_target_pairs={{0,8},{8,16},{16,24},{24,0},{1,9},{9,17},{17,25},{25,1},{2,10},{10... | collective-permute-start | bytes 786440 | tf_op jit(solution)/shard_map/ppermute | solution.py:30
  220.1 15.7 %collective-permute-start.26 = (bf16[512,256]{1,0:T(8,128)(2,1)}, bf16[512,256]{1,0:T(8,128)(2,1)S(1)}, u32[]{:S(2)}, u32[]{:S(2)}) collective-permute-start(bf16[512,256]{1,0:T(8,128)(2,1)} %get-tuple-element.57), channel_id=1, source_target_pairs={{0,24},{8,0},{16,8},{24,16},{1,25},{9,1},{17,9},{25,17},{2,26},{10... | collective-permute-start | bytes 786440 | tf_op jit(solution)/shard_map/ppermute | solution.py:30
  223.3 12.5 %collective-permute-start.27 = (bf16[512,256]{1,0:T(8,128)(2,1)}, bf16[512,256]{1,0:T(8,128)(2,1)S(1)}, u32[]{:S(2)}, u32[]{:S(2)}) collective-permute-start(bf16[512,256]{1,0:T(8,128)(2,1)} %get-tuple-element.58), channel_id=1, source_target_pairs={{0,16},{8,24},{16,0},{24,8},{1,17},{9,25},{17,1},{25,9},{2,18},{10... | collective-permute-start | bytes 786440 | tf_op jit(solution)/shard_map/ppermute | solution.py:30
  223.4 5.3 %collective-permute-start.24 = (f32[2,8,256]{2,1,0:T(8,128)S(1)}, f32[2,8,256]{2,1,0:T(8,128)S(1)}, u32[]{:S(2)}, u32[]{:S(2)}) collective-permute-start(f32[2,8,256]{2,1,0:T(8,128)S(1)} %add.198), channel_id=1, source_target_pairs={{0,4},{2,6},{4,0},{6,2},{1,5},{3,7},{5,1},{7,3},{8,12},{10,14},{12... | collective-permute-start | bytes 49160 | tf_op jit(solution)/shard_map/ppermute | solution.py:34
  226.5 3.7 %collective-permute-start.23 = (f32[2,8,256]{2,1,0:T(8,128)S(1)}, f32[2,8,256]{2,1,0:T(8,128)S(1)}, u32[]{:S(2)}, u32[]{:S(2)}) collective-permute-start(f32[2,8,256]{2,1,0:T(8,128)S(1)} %add.198), channel_id=1, source_target_pairs={{0,6},{2,0},{4,2},{6,4},{1,7},{3,1},{5,3},{7,5},{8,14},{10,8},{12,... | collective-permute-start | bytes 49160 | tf_op jit(solution)/shard_map/ppermute | solution.py:34
  228.7 4.9 %collective-permute-start.22 = (f32[2,8,256]{2,1,0:T(8,128)S(1)}, f32[2,8,256]{2,1,0:T(8,128)S(1)}, u32[]{:S(2)}, u32[]{:S(2)}) collective-permute-start(f32[2,8,256]{2,1,0:T(8,128)S(1)} %add.198), channel_id=1, source_target_pairs={{0,2},{2,4},{4,6},{6,0},{1,3},{3,5},{5,7},{7,1},{8,10},{10,12},{12... | collective-permute-start | bytes 49160 | tf_op jit(solution)/shard_map/ppermute | solution.py:34
  (15 other events, 253.9 us)
Sparse Core Ops, SparseCore 0:
  9.6 114.6 all-gather.1

commit v2 on v0

v2 whole, which is shorter than its diff:
```python
import functools

import jax
import jax.numpy as jnp
from jax import lax
from jax.experimental import pallas as pl
from jax.experimental.pallas import tpu as pltpu
from jax.sharding import PartitionSpec as P

AXES = ("y", "z", "x", "c")
HEADS = 64
HDIM = 128
BLOCK = 256
SIDE = 4
SPAN = 512
DEPTH = 6144
WROWS = 384
HH = 2
COLS = 3 * HH * HDIM
GROUP = SIDE * SPAN
NB = GROUP // BLOCK
VMEM = pltpu.CompilerParams(vmem_limit_bytes=58 * 1024 * 1024)
SMALL = pltpu.CompilerParams(vmem_limit_bytes=24 * 1024 * 1024)


def move_y(a, d):
    return lax.ppermute(a, "y", [(s, (s + d) % 4) for s in range(4)])


def move_z(a, d):
    return lax.ppermute(a, "z", [(s, (s + d) % 4) for s in range(4)])


def move_x(a, d):
    return lax.ppermute(a, "x", [(s, (s + d) % 4) for s in range(4)])


def swap(a):
    return lax.ppermute(a, "c", [(0, 1), (1, 0)])


def opposed(a, axis, d):
    perm = [(2 * s + c, 2 * ((s + d - 2 * d * c) % 4) + c) for s in range(4) for c in range(2)]
    return lax.ppermute(a, (axis, "c"), perm)


ORDER = (
    ("y00", ""),
    ("z1", ""),
    ("z3", ""),
    ("z2", ""),
    ("y10", ""),
    ("y01", "z1"),
    ("y30", "y00"),
    ("y02", "z3"),
    ("y11", ""),
    ("y31", ""),
    ("y12", ""),
    ("y20", "y11 y02 early"),
    ("y32", ""),
    ("y21", ""),
    ("y22", ""),
)


def spread_weights(weights, early):
    got = {"z0": weights[0], "early": early}
    for name, after in ORDER:
        if name[0] == "z":
            source = weights[int(name[1])]
        elif name[2] == "0":
            source = got["z" + name[1]]
        else:
            source = got["y" + name[1] + str(int(name[2]) - 1)]
        if after:
            source = lax.optimization_barrier((source, *[got[n] for n in after.split()]))[0]
        got[name] = opposed(source, name[0], int(name[1]) if name[0] == "z" else 1)
    pieces = [
        got[n] for k in range(SIDE) for n in ["z%d" % k] + ["y%d%d" % (k, i) for i in range(3)]
    ]
    return pieces, (got["z1"], got["z3"])


def along(place, axis, steps):
    return lax.rem(place[axis] + SIDE + steps * (2 * place[3] - 1), SIDE)


def silu(total):
    return (total / (1.0 + jnp.exp(-total))).astype(jnp.bfloat16)


def project(others, place, x, *refs):
    wrefs = refs[: SIDE * SIDE]
    out, xbuf, wfull, acc, result, wsem, xsem, osem = refs[-8:]
    depth = SIDE * WROWS
    count = SIDE - 1 if others else 1
    spans = [lax.rem(place[0] + (j + 1 if others else 0), SIDE) for j in range(count)]
    tiles = [pl.ds(i * depth, depth) for i in range(SIDE)]

    def fetch_w(i):
        for k in range(SIDE):
            zz = along(place, 0, k)
            rows = pl.ds(pl.multiple_of(i * depth + zz * WROWS, WROWS), WROWS)
            n = SIDE * k + i
            yield pltpu.make_async_copy(wrefs[n], wfull.at[rows], wsem.at[n])

    def fetch_x(j, i):
        source = x.at[spans[j]] if others else x
        cols = pl.ds(pl.multiple_of(along(place, 1, i) * depth, depth), depth)
        return pltpu.make_async_copy(
            source.at[:, cols], xbuf.at[j, :, tiles[i]], xsem.at[SIDE * j + i]
        )

    def start(i):
        for copy in fetch_w(i):
            copy.start()
        fetch_x(0, i).start()

    start(0)
    for i in range(SIDE):
        if i + 1 < SIDE:
            start(i + 1)
        else:
            for j in range(1, count):
                for t in range(SIDE):
                    fetch_x(j, t).start()
        for copy in fetch_w(i):
            copy.wait()
        fetch_x(0, i).wait()
        part = jnp.dot(
            xbuf[0, :, tiles[i]], wfull[tiles[i], :], preferred_element_type=jnp.float32
        )
        if i == 0:
            acc[...] = part
        elif i + 1 < SIDE:
            acc[...] += part
        else:
            result[0] = silu(acc[...] + part)
    pltpu.make_async_copy(result.at[0], out.at[spans[0]], osem.at[0]).start()
    for j in range(1, count):
        for i in range(SIDE):
            fetch_x(j, i).wait()
        for m in range(0, SPAN, BLOCK):
            rows = pl.ds(m, BLOCK)
            result[j, rows, :] = silu(
                jnp.dot(xbuf[j, rows, :], wfull[...], preferred_element_type=jnp.float32)
            )
        pltpu.make_async_copy(result.at[j], out.at[spans[j]], osem.at[j]).start()
    for j in range(count):
        pltpu.make_async_copy(result.at[j], out.at[spans[j]], osem.at[j]).wait()


def call_project(place, x, w, held):
    count = SIDE - 1 if held else 1
    smem = pl.BlockSpec(memory_space=pltpu.SMEM)
    hbm = pl.BlockSpec(memory_space=pl.ANY)
    return pl.pallas_call(
        functools.partial(project, bool(held)),
        out_shape=jax.ShapeDtypeStruct((SIDE, SPAN, COLS), jnp.bfloat16),
        in_specs=[smem] + [hbm] * (1 + len(w) + len(held)),
        out_specs=hbm,
        scratch_shapes=[
            pltpu.VMEM((count, SPAN, DEPTH), jnp.bfloat16),
            pltpu.VMEM((DEPTH, COLS), jnp.bfloat16),
            pltpu.VMEM((SPAN, COLS), jnp.float32),
            pltpu.VMEM((count, SPAN, COLS), jnp.bfloat16),
            pltpu.SemaphoreType.DMA((SIDE * SIDE,)),
            pltpu.SemaphoreType.DMA((SIDE * count,)),
            pltpu.SemaphoreType.DMA((count,)),
        ],
        input_output_aliases={2 + len(w): 0} if held else {},
        cost_estimate=pl.CostEstimate(
            flops=2 * count * SPAN * DEPTH * COLS,
            bytes_accessed=(10 + 7 * count) << 20,
            transcendentals=0,
        ),
        compiler_params=VMEM,
        name="project_others" if held else "project_own",
    )(place, x, *w, *held)


def decays(cumr, cumc, docr, docc, out):
    row = lax.broadcasted_iota(jnp.int32, (BLOCK, BLOCK), 0)
    col = lax.broadcasted_iota(jnp.int32, (BLOCK, BLOCK), 1)
    mask = (row >= col) & (docc[...] == docr[0])
    for h in range(HH):
        diff = cumc[:, pl.ds(h, 1)] - cumr[0, pl.ds(h, 1), :]
        out[0, h] = jnp.where(mask, jnp.exp(jnp.where(mask, diff, 0.0)), 0.0)


def block_states(keys, values, kf, suffix, states, total):
    for h in range(HH):
        held = jnp.zeros((HDIM, HDIM), jnp.float32)
        for b in range(NB):
            rows = pl.ds(b * BLOCK, BLOCK)
            k = keys[rows, pl.ds(h * HDIM, HDIM)].astype(jnp.float32)
            v = values[rows, pl.ds(h * HDIM, HDIM)]
            kd = (k * kf[rows, pl.ds(h, 1)]).astype(jnp.bfloat16)
            state = lax.dot_general(
                kd, v, (((0,), (0,)), ((), ())), preferred_element_type=jnp.float32
            )
            states[b, h] = state
            held += suffix[h, b] * state
        total[h] = held.astype(jnp.bfloat16)


def intras(proj, decay, qf, qd_out, out):
    for h in range(HH):
        cols = pl.ds(h * HDIM, HDIM)
        q = proj[:, cols]
        k = proj[:, pl.ds((HH + h) * HDIM, HDIM)]
        v = proj[:, pl.ds((2 * HH + h) * HDIM, HDIM)]
        scores = lax.dot_general(
            q, k, (((1,), (1,)), ((), ())), preferred_element_type=jnp.float32
        )
        weights = (scores * decay[0, h]).astype(jnp.bfloat16)
        out[:, cols] = jnp.dot(weights, v, preferred_element_type=jnp.float32)
        qd_out[:, cols] = (q.astype(jnp.float32) * qf[:, pl.ds(h, 1)]).astype(jnp.bfloat16)


def inters(place, qd, intra, states, passes, fac, s1, s2, s3, *refs):
    outs, squares_outs = refs[:SIDE], refs[SIDE : 2 * SIDE]
    att, squares, sem = refs[2 * SIDE :]
    near = SPAN // BLOCK
    ones = jnp.ones((8, HDIM), jnp.bfloat16)
    state = [
        fac[h, 0] * s1[h].astype(jnp.float32)
        + fac[h, 1] * s2[h].astype(jnp.float32)
        + fac[h, 2] * s3[h].astype(jnp.float32)
        for h in range(HH)
    ]
    for b in range(NB):
        rows = pl.ds(b * BLOCK, BLOCK)
        sums = jnp.zeros((BLOCK, HDIM), jnp.float32)
        for h in range(HH):
            cols = pl.ds(h * HDIM, HDIM)
            value = intra[rows, cols] + jnp.dot(
                qd[rows, cols], state[h].astype(jnp.bfloat16), preferred_element_type=jnp.float32
            )
            sums += value * value
            att[b // near, pl.ds((b % near) * BLOCK, BLOCK), cols] = value.astype(jnp.bfloat16)
            state[h] = passes[h, b] * state[h] + states[b, h]
        total = jnp.zeros((8, BLOCK), jnp.float32)
        for _ in range(3):
            piece = sums.astype(jnp.bfloat16)
            sums = sums - piece.astype(jnp.float32)
            total += lax.dot_general(
                ones, piece, (((1,), (1,)), ((), ())), preferred_element_type=jnp.float32
            )
        squares[b // near, b % near] = total
    copies = []
    for i, d in enumerate((0, 1, 3, 2)):
        target = lax.rem(place[0] + d, SIDE)
        copies.append(pltpu.make_async_copy(squares.at[target], squares_outs[i], sem.at[2 * i]))
        copies.append(pltpu.make_async_copy(att.at[target], outs[i], sem.at[2 * i + 1]))
    for copy in copies:
        copy.start()
    for copy in copies:
        copy.wait()


def finish(place, total, gain, p0, p1, p2, p3, out):
    scale = lax.rsqrt(total[...] / (HEADS * HDIM) + 1e-05)
    for b in range(SPAN // BLOCK):
        rows = pl.ds(b * BLOCK, BLOCK)
        column = jnp.transpose(scale[b])[:, 0:1]
        for dz, piece in ((0, p0), (3, p1), (1, p2), (2, p3)):
            zz = lax.rem(place[0] + dz, SIDE)
            cols = pl.ds(pl.multiple_of(zz * (HH * HDIM), HH * HDIM), HH * HDIM)
            value = piece[rows, :].astype(jnp.float32) * column
            out[rows, cols] = (value * gain[0:1, cols]).astype(jnp.bfloat16)


def doc_of(points, ends):
    found = jnp.sum((points[..., None] >= ends).astype(jnp.int32), axis=-1)
    return jnp.where(points < 0, -1, found)


def per_device(tokens, w_qkv, log_decay, doc_lengths, norm_gain):
    y, z, x, c = [lax.axis_index(axis) for axis in AXES]
    place = jnp.stack([z, y, x, c]).astype(jnp.int32)

    ends = jnp.cumsum(doc_lengths)
    nblocks = GROUP * SIDE // BLOCK
    logs = lax.dynamic_slice(log_decay, (HH * z, 0), (HH, GROUP * SIDE))
    cum_all = jnp.cumsum(logs.reshape(HH, nblocks, BLOCK), axis=2)
    starts = jnp.arange(nblocks, dtype=jnp.int32) * BLOCK
    before_all = doc_of(starts - 1, ends)
    last_all = doc_of(starts + (BLOCK - 1), ends)
    pass_all = jnp.where((before_all == last_all)[None], jnp.exp(cum_all[:, :, -1]), 0.0)
    gpass = jnp.prod(pass_all.reshape(HH, SIDE, NB), axis=2)
    f1 = jnp.where(y >= 1, 1.0, 0.0) * jnp.ones((HH,), jnp.float32)
    prev1 = lax.dynamic_index_in_dim(gpass, jnp.maximum(y - 1, 0), 1, keepdims=False)
    prev2 = lax.dynamic_index_in_dim(gpass, jnp.maximum(y - 2, 0), 1, keepdims=False)
    f2 = jnp.where(y >= 2, prev1, 0.0)
    f3 = jnp.where(y >= 3, prev1 * prev2, 0.0)
    fac = jnp.stack([f1, f2, f3], axis=1)
    passes = lax.dynamic_slice_in_dim(pass_all, NB * y, NB, 1)
    suffix = jnp.concatenate(
        [jnp.cumprod(passes[:, :0:-1], axis=1)[:, ::-1], jnp.ones((HH, 1), jnp.float32)], axis=1
    )
    cum = lax.dynamic_slice_in_dim(cum_all, NB * y, NB, 1)
    before = lax.dynamic_slice_in_dim(before_all, NB * y, NB, 0)
    last = lax.dynamic_slice_in_dim(last_all, NB * y, NB, 0)
    points = GROUP * y + jnp.arange(GROUP, dtype=jnp.int32).reshape(NB, BLOCK)
    doc = doc_of(points, ends)
    qfac = jnp.where((doc == before[:, None])[None], jnp.exp(cum), 0.0)
    kfac = jnp.where((doc == last[:, None])[None], jnp.exp(cum[:, :, -1:] - cum), 0.0)
    cumc = cum.reshape(HH, GROUP).T
    qf = qfac.reshape(HH, GROUP).T
    kf = kfac.reshape(HH, GROUP).T
    docc = doc.reshape(GROUP, 1)

    smem = pl.BlockSpec(memory_space=pltpu.SMEM)
    vmem = pl.BlockSpec(memory_space=pltpu.VMEM)
    hbm = pl.BlockSpec(memory_space=pl.ANY)
    square = (HDIM, HDIM)
    width = HH * HDIM
    near = SPAN // BLOCK
    summed = (near, 8, BLOCK)
    decay = pl.pallas_call(
        decays,
        out_shape=jax.ShapeDtypeStruct((NB, HH, BLOCK, BLOCK), jnp.float32),
        grid=(NB,),
        in_specs=[
            pl.BlockSpec((1, HH, BLOCK), lambda b: (b, 0, 0)),
            pl.BlockSpec((BLOCK, HH), lambda b: (b, 0)),
            pl.BlockSpec((1, 1, BLOCK), lambda b: (b, 0, 0)),
            pl.BlockSpec((BLOCK, 1), lambda b: (b, 0)),
        ],
        out_specs=pl.BlockSpec((1, HH, BLOCK, BLOCK), lambda b: (b, 0, 0, 0)),
        compiler_params=SMALL,
        name="decays",
    )(jnp.transpose(cum, (1, 0, 2)), cumc, doc[:, None], docc)

    wview = w_qkv.reshape(WROWS, 3, SIDE, width)
    weights = []
    for d in range(SIDE):
        at = (z + d * (1 - 2 * c)) % SIDE
        weights.append(
            lax.dynamic_slice(wview, (0, 0, at, 0), (WROWS, 3, 1, width)).reshape(WROWS, COLS)
        )
    w, first = spread_weights(weights, (decay, kf, qf, suffix, passes, fac))
    mine = lax.dynamic_slice(tokens, ((2 * x + c) * 64, 0), (64, DEPTH))
    mine = lax.optimization_barrier((mine, *first))[0]
    group = lax.all_gather(mine, ("z", "x", "c"), axis=0, tiled=True)

    proj = call_project(place, tokens, w, [])
    proj = call_project(place, group.reshape(SIDE, SPAN, DEPTH), w, [proj])
    proj = proj.reshape(GROUP, COLS)
    states, total = pl.pallas_call(
        block_states,
        out_shape=(
            jax.ShapeDtypeStruct((NB, HH) + square, jnp.float32),
            jax.ShapeDtypeStruct((HH,) + square, jnp.bfloat16),
        ),
        grid=(1,),
        in_specs=[
            pl.BlockSpec((GROUP, width), lambda i: (0, 1)),
            pl.BlockSpec((GROUP, width), lambda i: (0, 2)),
            vmem,
            smem,
        ],
        out_specs=(vmem, vmem),
        cost_estimate=pl.CostEstimate(flops=1 << 27, bytes_accessed=4 << 20, transcendentals=0),
        compiler_params=SMALL,
        name="states",
    )(proj, proj, kf, suffix)
    s1, s2, s3 = move_y(total, 1), move_y(total, 2), move_y(total, 3)

    def block(b):
        return (b, 0)

    qd, intra = pl.pallas_call(
        intras,
        out_shape=(
            jax.ShapeDtypeStruct((GROUP, width), jnp.bfloat16),
            jax.ShapeDtypeStruct((GROUP, width), jnp.float32),
        ),
        grid=(NB,),
        in_specs=[
            pl.BlockSpec((BLOCK, COLS), block),
            pl.BlockSpec((1, HH, BLOCK, BLOCK), lambda b: (b, 0, 0, 0)),
            pl.BlockSpec((BLOCK, HH), block),
        ],
        out_specs=(pl.BlockSpec((BLOCK, width), block), pl.BlockSpec((BLOCK, width), block)),
        cost_estimate=pl.CostEstimate(flops=1 << 30, bytes_accessed=8 << 20, transcendentals=0),
        compiler_params=SMALL,
        name="intras",
    )(proj, decay, qf)
    out = pl.pallas_call(
        inters,
        out_shape=[jax.ShapeDtypeStruct((SPAN, width), jnp.bfloat16)] * SIDE
        + [jax.ShapeDtypeStruct(summed, jnp.float32)] * SIDE,
        in_specs=[smem, vmem, vmem, vmem, smem, smem, vmem, vmem, vmem],
        out_specs=[hbm] * (2 * SIDE),
        scratch_shapes=[
            pltpu.VMEM((SIDE, SPAN, width), jnp.bfloat16),
            pltpu.VMEM((SIDE,) + summed, jnp.float32),
            pltpu.SemaphoreType.DMA((2 * SIDE,)),
        ],
        cost_estimate=pl.CostEstimate(flops=1 << 28, bytes_accessed=6 << 20, transcendentals=0),
        compiler_params=SMALL,
        name="inters",
    )(place, qd, intra, states, passes, fac, s1, s2, s3)

    part = out[SIDE]
    for i, d in enumerate((1, -1, 2)):
        part = part + move_z(out[SIDE + 1 + i], d)
    part = part + swap(part)
    part = part + move_x(part, 1) + move_x(part, -1) + move_x(part, 2)
    pieces = [out[0]] + [move_z(out[1 + i], d) for i, d in enumerate((1, -1, 2))]
    return pl.pallas_call(
        finish,
        out_shape=jax.ShapeDtypeStruct((SPAN, SIDE * width), jnp.bfloat16),
        in_specs=[smem] + [vmem] * 6,
        out_specs=vmem,
        cost_estimate=pl.CostEstimate(flops=1 << 22, bytes_accessed=3 << 20, transcendentals=0),
        compiler_params=SMALL,
        name="finish",
    )(place, part, norm_gain.reshape(1, -1), *pieces)


def solution(mesh):
    mesh = jax.sharding.Mesh(mesh.devices.reshape(SIDE, SIDE, SIDE, 2), AXES)
    in_specs = (
        P(("y", "z"), None),
        P(("y", "z"), None, ("x", "c")),
        P(("x", "c"), None),
        P(),
        P(("x", "c")),
    )
    out_specs = P(("y", "z"), ("x", "c"))
    return jax.shard_map(
        per_device, mesh=mesh, in_specs=in_specs, out_specs=out_specs, check_vma=False
    )
```

time: 228 us -> 202 us (0.89)
  Pallas kernels: 63.3 us -> 49 us
  starting transfers between devices: 34.6 us -> 30 us
  local copies, waits for them, and re-layouts: 24.7 us -> 20.1 us
    pallas_call x6 -> x7, Pallas kernels: 63.3 us -> 49 us  [the longest x2 36.3 us: call_project(): pl.pallas_call(functools.partial(project, bool(held)), out_shape=jax.Shap...]
    ppermute x15, waiting for transfers between devices: 79.9 us -> 73.5 us  [opposed(): return lax.ppermute(a, (axis, 'c'), perm)]
    ppermute x6, waiting for transfers between devices: 0.02 us -> 6.22 us  [move_z(): return lax.ppermute(a, 'z', [(s, (s + d) % 4) for s in range(4)])]
    reshape x5 -> x6, local copies, waits for them, and re-layouts: 8.12 us -> 4.12 us  [the longest x4 4.03 us: per_device(): lax.dynamic_slice(wview, (0, 0, at, 0), (WROWS, 3, 1, width))]
    ppermute x15, starting transfers between devices: 16.1 us -> 12.7 us  [opposed(): return lax.ppermute(a, (axis, 'c'), perm)]
    unnamed x35 -> x45, local copies, waits for them, and re-layouts: 5.99 us -> 8.98 us
    dynamic_slice x4 -> x2, local copies, waits for them, and re-layouts: 4.07 us -> 1.35 us  [the longest x1 1.32 us: per_device(): lax.dynamic_slice(wview, (0, 0, at, 0), (WROWS, 3, 1, width))]
  transfers between devices with their start and end apart: 29 -> 29, of which waited for: 14 -> 20; matrix products, arithmetic and copies ran while one was open for 11% -> 6% of each run, Pallas kernels for 8% -> 9%
where the time goes in v2:
time: 202 us; the launch traced here: 201 us
  waiting for transfers between devices  85.5 us (42%)
  Pallas kernels  49 us (24%)
  starting transfers between devices  30 us (15%)
  local copies, waits for them, and re-layouts  20.1 us (10%)
  between operations  13.8 us (7%)
  other arithmetic  3.12 us (2%)
    ppermute x15, waiting for transfers between devices, opposed(): return lax.ppermute(a, (axis, 'c'), perm)  73.5 us
    pallas_call x2, Pallas kernels, call_project(): pl.pallas_call(functools.partial(project, bool(held)), out_shape=jax.Shap...  36.3 us
    ppermute x15, starting transfers between devices, opposed(): return lax.ppermute(a, (axis, 'c'), perm)  12.7 us
    unnamed x45, local copies, waits for them, and re-layouts  8.98 us
    ppermute x6, starting transfers between devices, move_z(): return lax.ppermute(a, 'z', [(s, (s + d) % 4) for s in range(4)])  7.59 us
    ppermute x6, waiting for transfers between devices, move_z(): return lax.ppermute(a, 'z', [(s, (s + d) % 4) for s in range(4)])  6.22 us
    ppermute x3, starting transfers between devices, move_x(): return lax.ppermute(a, 'x', [(s, (s + d) % 4) for s in range(4)])  5.63 us
    ppermute x3, waiting for transfers between devices, move_x(): return lax.ppermute(a, 'x', [(s, (s + d) % 4) for s in range(4)])  4.64 us
  transfers between devices with their start and end apart: 29, of which 20 were waited for; matrix products, arithmetic and copies ran while one was open for 6% of the time, Pallas kernels for 9%

profile of v2, /device:TPU:0, one launch (start us, length us, event | category | flops | bytes accessed | tf_op | source)
XLA Modules:
  0.0 201.5 jit_solution(10863897533716624886)
XLA Ops:
  6.5 3.0 %copy.69 = bf16[384,3,1024]{0,2,1:T(8,128)(2,1)S(1)} copy(bf16[384,3,1024]{2,0,1:T(8,128)(2,1)} %param.6) | data formatting | bytes 4718592 | tf_op args[1]
  12.3 2.1 %collective-permute-start = (bf16[384,768]{1,0:T(8,128)(2,1)S(1)}, bf16[384,768]{1,0:T(8,128)(2,1)}, u32[]{:S(2)}, u32[]{:S(2)}) collective-permute-start(bf16[384,768]{1,0:T(8,128)(2,1)S(1)} %copy.70), channel_id=1, source_target_pairs={{0,8},{1,25},{8,16},{9,1},{16,24},{17,9},{24,0},{25,17},{2,10},{3,... | collective-permute-start | bytes 1769480 | tf_op jit(solution)/shard_map/ppermute | solution.py:44
  15.7 2.2 %collective-permute-start.1 = (bf16[384,768]{1,0:T(8,128)(2,1)S(1)}, bf16[384,768]{1,0:T(8,128)(2,1)S(1)}, u32[]{:S(2)}, u32[]{:S(2)}) collective-permute-start(bf16[384,768]{1,0:T(8,128)(2,1)S(1)} %copy.71), channel_id=1, source_target_pairs={{0,24},{1,9},{8,0},{9,17},{16,8},{17,25},{24,16},{25,1},{2,26},{3,... | collective-permute-start | bytes 1769480 | tf_op jit(solution)/shard_map/ppermute | solution.py:44
  17.9 2.1 %constant_dynamic-slice_fusion.10 = bf16[64,6144]{1,0:T(8,128)(2,1)} fusion(bf16[512,6144]{1,0:T(8,128)(2,1)} %x.3, s32[]{:T(128)S(6)} %select_n.133), kind=kLoop, calls=%fused_computation.27 | loop fusion | bytes 1572868 | tf_op jit(solution)/shard_map/dynamic_slice | solution.py:344
  20.0 7.5 %collective-permute-done.refs_4_ = bf16[384,768]{1,0:T(8,128)(2,1)} collective-permute-done((bf16[384,768]{1,0:T(8,128)(2,1)S(1)}, bf16[384,768]{1,0:T(8,128)(2,1)}, u32[]{:S(2)}, u32[]{:S(2)}) %collective-permute-start) | collective-permute-done | bytes 589856 | tf_op jit(solution)/shard_map/ppermute | solution.py:44
  33.0 3.3 %collective-permute-start.8 = (bf16[384,768]{1,0:T(8,128)(2,1)}, bf16[384,768]{1,0:T(8,128)(2,1)}, u32[]{:S(2)}, u32[]{:S(2)}) collective-permute-start(bf16[384,768]{1,0:T(8,128)(2,1)} %copy.73), channel_id=1, source_target_pairs={{0,16},{1,17},{8,24},{9,25},{16,0},{17,1},{24,8},{25,9},{2,18},{3,... | collective-permute-start | bytes 1769480 | tf_op jit(solution)/shard_map/ppermute | solution.py:44
  39.0 2.5 %collective-permute-done.2.refs_1_ = bf16[384,768]{1,0:T(8,128)(2,1)} collective-permute-done((bf16[384,768]{1,0:T(8,128)(2,1)S(1)}, bf16[384,768]{1,0:T(8,128)(2,1)}, u32[]{:S(2)}, u32[]{:S(2)}) %collective-permute-start.2) | collective-permute-done | bytes 589856 | tf_op jit(solution)/shard_map/ppermute | solution.py:44
  48.7 2.0 copy-done.3
  50.7 2.1 %collective-permute-done.3.refs_2_ = bf16[384,768]{1,0:T(8,128)(2,1)} collective-permute-done((bf16[384,768]{1,0:T(8,128)(2,1)}, bf16[384,768]{1,0:T(8,128)(2,1)}, u32[]{:S(2)}, u32[]{:S(2)}) %collective-permute-start.3) | collective-permute-done | bytes 589856 | tf_op jit(solution)/shard_map/ppermute | solution.py:44
  52.9 6.3 %collective-permute-done.5.refs_5_ = bf16[384,768]{1,0:T(8,128)(2,1)} collective-permute-done((bf16[384,768]{1,0:T(8,128)(2,1)}, bf16[384,768]{1,0:T(8,128)(2,1)}, u32[]{:S(2)}, u32[]{:S(2)}) %collective-permute-start.5) | collective-permute-done | bytes 589856 | tf_op jit(solution)/shard_map/ppermute | solution.py:44
  60.2 11.5 %collective-permute-done.6.refs_6_ = bf16[384,768]{1,0:T(8,128)(2,1)S(1)} collective-permute-done((bf16[384,768]{1,0:T(8,128)(2,1)}, bf16[384,768]{1,0:T(8,128)(2,1)S(1)}, u32[]{:S(2)}, u32[]{:S(2)}) %collective-permute-start.6) | collective-permute-done | bytes 589856 | tf_op jit(solution)/shard_map/ppermute | solution.py:44
  71.8 6.2 %collective-permute-done.12.refs_13_ = bf16[384,768]{1,0:T(8,128)(2,1)S(1)} collective-permute-done((bf16[384,768]{1,0:T(8,128)(2,1)S(1)}, bf16[384,768]{1,0:T(8,128)(2,1)S(1)}, u32[]{:S(2)}, u32[]{:S(2)}) %collective-permute-start.12) | collective-permute-done | bytes 589856 | tf_op jit(solution)/shard_map/ppermute | solution.py:44
  78.1 6.3 %collective-permute-done.9.refs_9_ = bf16[384,768]{1,0:T(8,128)(2,1)S(1)} collective-permute-done((bf16[384,768]{1,0:T(8,128)(2,1)}, bf16[384,768]{1,0:T(8,128)(2,1)S(1)}, u32[]{:S(2)}, u32[]{:S(2)}) %collective-permute-start.9) | collective-permute-done | bytes 589856 | tf_op jit(solution)/shard_map/ppermute | solution.py:44
  85.1 5.6 %collective-permute-done.13.refs_14_ = bf16[384,768]{1,0:T(8,128)(2,1)S(1)} collective-permute-done((bf16[384,768]{1,0:T(8,128)(2,1)S(1)}, bf16[384,768]{1,0:T(8,128)(2,1)S(1)}, u32[]{:S(2)}, u32[]{:S(2)}) %collective-permute-start.13) | collective-permute-done | bytes 589856 | tf_op jit(solution)/shard_map/ppermute | solution.py:44
  90.7 6.3 %collective-permute-done.10.refs_10_ = bf16[384,768]{1,0:T(8,128)(2,1)S(1)} collective-permute-done((bf16[384,768]{1,0:T(8,128)(2,1)S(1)}, bf16[384,768]{1,0:T(8,128)(2,1)S(1)}, u32[]{:S(2)}, u32[]{:S(2)}) %collective-permute-start.10) | collective-permute-done | bytes 589856 | tf_op jit(solution)/shard_map/ppermute | solution.py:44
  97.7 5.6 %collective-permute-done.7.refs_7_ = bf16[384,768]{1,0:T(8,128)(2,1)S(1)} collective-permute-done((bf16[384,768]{1,0:T(8,128)(2,1)S(1)}, bf16[384,768]{1,0:T(8,128)(2,1)S(1)}, u32[]{:S(2)}, u32[]{:S(2)}) %collective-permute-start.7) | collective-permute-done | bytes 589856 | tf_op jit(solution)/shard_map/ppermute | solution.py:44
  103.3 6.3 %collective-permute-done.14.refs_15_ = bf16[384,768]{1,0:T(8,128)(2,1)S(1)} collective-permute-done((bf16[384,768]{1,0:T(8,128)(2,1)S(1)}, bf16[384,768]{1,0:T(8,128)(2,1)S(1)}, u32[]{:S(2)}, u32[]{:S(2)}) %collective-permute-start.14) | collective-permute-done | bytes 589856 | tf_op jit(solution)/shard_map/ppermute | solution.py:44
  110.5 5.6 %collective-permute-done.11.refs_11_ = bf16[384,768]{1,0:T(8,128)(2,1)} collective-permute-done((bf16[384,768]{1,0:T(8,128)(2,1)S(1)}, bf16[384,768]{1,0:T(8,128)(2,1)}, u32[]{:S(2)}, u32[]{:S(2)}) %collective-permute-start.11) | collective-permute-done | bytes 589856 | tf_op jit(solution)/shard_map/ppermute | solution.py:44
  116.1 12.6 %project_own.1.refs_16_ = bf16[4,512,768]{2,1,0:T(8,128)(2,1)} custom-call(s32[4]{0:T(128)} %pad_add_fusion.place, bf16[512,6144]{1,0:T(8,128)(2,1)} %x.3, bf16[384,768]{1,0:T(8,128)(2,1)} %copy-done.8, bf16[384,768]{1,0:T(8,128)(2,1)} %collective-permute-done.2.refs_1_, bf16[384,768]{1,0:T(8,128)(2,1)} %collective-permute-done.3.refs_2_, ...), custom_call_target="tpu_custom_call" | custom-call | flops 4831838208 | bytes 17825792 | tf_op jit(solution)/shard_map/project_own/pallas_call | solution.py:157
  128.7 23.7 %project_others.1 = bf16[4,512,768]{2,1,0:T(8,128)(2,1)} custom-call(s32[4]{0:T(128)} %pad_add_fusion.place, bf16[4,512,6144]{2,1,0:T(8,128)(2,1)} %bitcast.55, bf16[384,768]{1,0:T(8,128)(2,1)} %copy-done.8, bf16[384,768]{1,0:T(8,128)(2,1)} %collective-permute-done.2.refs_1_, ...), custom_call_target="tpu_custom_call", output_to_operand_aliasing={{}: (18, {})} | custom-call | flops 14495514624 | bytes 32505856 | tf_op jit(solution)/shard_map/project_others/pallas_call | solution.py:157
  152.5 1.9 copy-done.2
  154.4 2.4 %states.1 = (f32[8,2,128,128]{3,2,1,0:T(8,128)S(1)}, bf16[2,128,128]{2,1,0:T(8,128)(2,1)S(1)}) custom-call(bf16[2048,768]{1,0:T(8,128)(2,1)S(1)} %bitcast.37, bf16[2048,768]{1,0:T(8,128)(2,1)S(1)} %bitcast.38, f32[2048,2]{1,0:T(8,128)S(1)} %bitcast.40, f32[2,8]{1,0:T(2,128)S(1)} %concatenate.3.suffix), custom_call_target="tpu_custom_call" | custom-call | flops 134217728 | bytes 4194304 | tf_op jit(solution)/shard_map/states/pallas_call | solution.py:351
  156.8 2.4 %collective-permute-start.17 = (bf16[2,128,128]{2,1,0:T(8,128)(2,1)S(1)}, bf16[2,128,128]{2,1,0:T(8,128)(2,1)S(1)}, u32[]{:S(2)}, u32[]{:S(2)}) collective-permute-start(bf16[2,128,128]{2,1,0:T(8,128)(2,1)S(1)} %get-tuple-element.30), channel_id=1, source_target_pairs={{0,96},{32,0},{64,32},{96,64},{1,97},{33,1},{65,33},{97,65},{2,98}... | collective-permute-start | bytes 196616 | tf_op jit(solution)/shard_map/ppermute | solution.py:27
  160.9 4.2 %intras.1 = (bf16[2048,256]{1,0:T(8,128)(2,1)S(1)}, f32[2048,256]{1,0:T(8,128)S(1)}) custom-call(bf16[2048,768]{1,0:T(8,128)(2,1)S(1)} %bitcast.39, f32[8,2,256,256]{3,2,1,0:T(8,128)S(1)} %copy-done.4, f32[2048,2]{1,0:T(8,128)S(1)} %bitcast.43), custom_call_target="tpu_custom_call" | custom-call | flops 1073741824 | bytes 8388608 | tf_op jit(solution)/shard_map/intras/pallas_call | solution.py:374
  166.2 2.2 %inters.1 = (bf16[512,256]{1,0:T(8,128)(2,1)S(1)}, bf16[512,256]{1,0:T(8,128)(2,1)S(1)}, bf16[512,256]{1,0:T(8,128)(2,1)S(1)}, bf16[512,256]{1,0:T(8,128)(2,1)S(...) custom-call(s32[4]{0:T(128)S(1)} %copy-done.6, ...), custom_call_target="tpu_custom_call" | custom-call | flops 268435456 | bytes 6291456 | tf_op jit(solution)/shard_map/inters/pallas_call | solution.py:391
  169.2 2.6 %collective-permute-start.19 = (f32[2,8,256]{2,1,0:T(8,128)S(1)}, f32[2,8,256]{2,1,0:T(8,128)S(1)}, u32[]{:S(2)}, u32[]{:S(2)}) collective-permute-start(f32[2,8,256]{2,1,0:T(8,128)S(1)} %get-tuple-element.33), channel_id=1, source_target_pairs={{0,24},{8,0},{16,8},{24,16},{1,25},{9,1},{17,9},{25,17},{2,26},{10... | collective-permute-start | bytes 49160 | tf_op jit(solution)/shard_map/ppermute | solution.py:31
  173.5 3.5 %collective-permute-done.20 = f32[2,8,256]{2,1,0:T(8,128)S(1)} collective-permute-done((f32[2,8,256]{2,1,0:T(8,128)S(1)}, f32[2,8,256]{2,1,0:T(8,128)S(1)}, u32[]{:S(2)}, u32[]{:S(2)}) %collective-permute-start.20) | collective-permute-done | bytes 16416 | tf_op jit(solution)/shard_map/ppermute | solution.py:31
  177.1 3.2 %collective-permute-start.26 = (bf16[512,256]{1,0:T(8,128)(2,1)S(1)}, bf16[512,256]{1,0:T(8,128)(2,1)S(1)}, u32[]{:S(2)}, u32[]{:S(2)}) collective-permute-start(bf16[512,256]{1,0:T(8,128)(2,1)S(1)} %get-tuple-element.37), channel_id=1, source_target_pairs={{0,24},{8,0},{16,8},{24,16},{1,25},{9,1},{17,9},{25,17},{2,26},{10... | collective-permute-start | bytes 786440 | tf_op jit(solution)/shard_map/ppermute | solution.py:31
  180.4 3.0 %collective-permute-start.24 = (f32[2,8,256]{2,1,0:T(8,128)S(1)}, f32[2,8,256]{2,1,0:T(8,128)S(1)}, u32[]{:S(2)}, u32[]{:S(2)}) collective-permute-start(f32[2,8,256]{2,1,0:T(8,128)S(1)} %add.198), channel_id=1, source_target_pairs={{0,4},{2,6},{4,0},{6,2},{1,5},{3,7},{5,1},{7,3},{8,12},{10,14},{12... | collective-permute-start | bytes 49160 | tf_op jit(solution)/shard_map/ppermute | solution.py:35
  187.1 3.5 %collective-permute-done.22 = f32[2,8,256]{2,1,0:T(8,128)S(1)} collective-permute-done((f32[2,8,256]{2,1,0:T(8,128)S(1)}, f32[2,8,256]{2,1,0:T(8,128)S(1)}, u32[]{:S(2)}, u32[]{:S(2)}) %collective-permute-start.22) | collective-permute-done | bytes 16416 | tf_op jit(solution)/shard_map/ppermute | solution.py:35
  190.7 2.0 collective-permute-done.25.p1
  192.6 2.0 %finish.1 = bf16[512,1024]{1,0:T(8,128)(2,1)} custom-call(s32[4]{0:T(128)S(1)} %copy-done.6, f32[2,8,256]{2,1,0:T(8,128)S(1)} %add_add_fusion.total, f32[1,1024]{1,0:T(1,128)S(1)} %bitcast.45, bf16[512,256]{1,0:T(8,128)(2,1)S(1)} %get-tuple-element.35.p0, bf16[512,256]{1,0:T(8,128)(2,1)S(1)} %collective-permute-done.25.p1, ...), custom_call_target="tpu_custom_call" | custom-call | flops 4194304 | bytes 3145728 | tf_op jit(solution)/shard_map/finish/pallas_call | solution.py:413
  (137 shorter events, 31.7 us)
Async XLA Ops:
  6.5 122.2 %all-gather.2.cloned.1.call-start = ((), (), s32[]{:S(2)}) async-start(), calls=%async_computation | async-start | bytes 25952256 | tf_op jit(solution)/shard_map/all_gather | solution.py:346
  12.3 15.2 %collective-permute-start = (bf16[384,768]{1,0:T(8,128)(2,1)S(1)}, bf16[384,768]{1,0:T(8,128)(2,1)}, u32[]{:S(2)}, u32[]{:S(2)}) collective-permute-start(bf16[384,768]{1,0:T(8,128)(2,1)S(1)} %copy.70), channel_id=1, source_target_pairs={{0,8},{1,25},{8,16},{9,1},{16,24},{17,9},{24,0},{25,17},{2,10},{3,... | collective-permute-start | bytes 1769480 | tf_op jit(solution)/shard_map/ppermute | solution.py:44
  15.7 13.4 %collective-permute-start.1 = (bf16[384,768]{1,0:T(8,128)(2,1)S(1)}, bf16[384,768]{1,0:T(8,128)(2,1)S(1)}, u32[]{:S(2)}, u32[]{:S(2)}) collective-permute-start(bf16[384,768]{1,0:T(8,128)(2,1)S(1)} %copy.71), channel_id=1, source_target_pairs={{0,24},{1,9},{8,0},{9,17},{16,8},{17,25},{24,16},{25,1},{2,26},{3,... | collective-permute-start | bytes 1769480 | tf_op jit(solution)/shard_map/ppermute | solution.py:44
  30.2 11.3 %collective-permute-start.2 = (bf16[384,768]{1,0:T(8,128)(2,1)S(1)}, bf16[384,768]{1,0:T(8,128)(2,1)}, u32[]{:S(2)}, u32[]{:S(2)}) collective-permute-start(bf16[384,768]{1,0:T(8,128)(2,1)S(1)} %copy.85.refs_0_), channel_id=1, source_target_pairs={{0,32},{1,97},{32,64},{33,1},{64,96},{65,33},{96,0},{97,65},{2,34}... | collective-permute-start | bytes 1769480 | tf_op jit(solution)/shard_map/ppermute | solution.py:44
  33.0 27.3 %collective-permute-start.8 = (bf16[384,768]{1,0:T(8,128)(2,1)}, bf16[384,768]{1,0:T(8,128)(2,1)}, u32[]{:S(2)}, u32[]{:S(2)}) collective-permute-start(bf16[384,768]{1,0:T(8,128)(2,1)} %copy.73), channel_id=1, source_target_pairs={{0,16},{1,17},{8,24},{9,25},{16,0},{17,1},{24,8},{25,9},{2,18},{3,... | collective-permute-start | bytes 1769480 | tf_op jit(solution)/shard_map/ppermute | solution.py:44
  41.5 11.4 %collective-permute-start.3 = (bf16[384,768]{1,0:T(8,128)(2,1)}, bf16[384,768]{1,0:T(8,128)(2,1)}, u32[]{:S(2)}, u32[]{:S(2)}) collective-permute-start(bf16[384,768]{1,0:T(8,128)(2,1)} %collective-permute-done.2.refs_1_), channel_id=1, source_target_pairs={{0,32},{1,97},{32,64},{33,1},{64,96},{65,33},{96,0},{97,65},{2,34}... | collective-permute-start | bytes 1769480 | tf_op jit(solution)/shard_map/ppermute | solution.py:44
  41.8 17.4 %collective-permute-start.5 = (bf16[384,768]{1,0:T(8,128)(2,1)}, bf16[384,768]{1,0:T(8,128)(2,1)}, u32[]{:S(2)}, u32[]{:S(2)}) collective-permute-start(bf16[384,768]{1,0:T(8,128)(2,1)} %collective-permute-done.refs_4_), channel_id=1, source_target_pairs={{0,32},{1,97},{32,64},{33,1},{64,96},{65,33},{96,0},{97,65},{2,34}... | collective-permute-start | bytes 1769480 | tf_op jit(solution)/shard_map/ppermute | solution.py:44
  52.9 18.9 %collective-permute-start.4 = (bf16[384,768]{1,0:T(8,128)(2,1)}, bf16[384,768]{1,0:T(8,128)(2,1)S(1)}, u32[]{:S(2)}, u32[]{:S(2)}) collective-permute-start(bf16[384,768]{1,0:T(8,128)(2,1)} %collective-permute-done.3.refs_2_), channel_id=1, source_target_pairs={{0,32},{1,97},{32,64},{33,1},{64,96},{65,33},{96,0},{97,65},{2,34}... | collective-permute-start | bytes 1769480 | tf_op jit(solution)/shard_map/ppermute | solution.py:44
  59.2 12.5 %collective-permute-start.6 = (bf16[384,768]{1,0:T(8,128)(2,1)}, bf16[384,768]{1,0:T(8,128)(2,1)S(1)}, u32[]{:S(2)}, u32[]{:S(2)}) collective-permute-start(bf16[384,768]{1,0:T(8,128)(2,1)} %collective-permute-done.5.refs_5_), channel_id=1, source_target_pairs={{0,32},{1,97},{32,64},{33,1},{64,96},{65,33},{96,0},{97,65},{2,34}... | collective-permute-start | bytes 1769480 | tf_op jit(solution)/shard_map/ppermute | solution.py:44
  59.5 18.6 %collective-permute-start.12 = (bf16[384,768]{1,0:T(8,128)(2,1)S(1)}, bf16[384,768]{1,0:T(8,128)(2,1)S(1)}, u32[]{:S(2)}, u32[]{:S(2)}) collective-permute-start(bf16[384,768]{1,0:T(8,128)(2,1)S(1)} %copy-done.11), channel_id=1, source_target_pairs={{0,32},{1,97},{32,64},{33,1},{64,96},{65,33},{96,0},{97,65},{2,34}... | collective-permute-start | bytes 1769480 | tf_op jit(solution)/shard_map/ppermute | solution.py:44
  71.7 44.3 %copy-start.13 = (bf16[384,768]{1,0:T(8,128)(2,1)}, bf16[384,768]{1,0:T(8,128)(2,1)S(1)}, u32[]{:S(2)}) copy-start(bf16[384,768]{1,0:T(8,128)(2,1)S(1)} %collective-permute-done.6.refs_6_) | copy-start | bytes 1769476
  71.7 44.3 %copy-start.12 = (bf16[384,768]{1,0:T(8,128)(2,1)}, bf16[384,768]{1,0:T(8,128)(2,1)S(1)}, u32[]{:S(2)}) copy-start(bf16[384,768]{1,0:T(8,128)(2,1)S(1)} %collective-permute-done.4.refs_3_) | copy-start | bytes 1769476
  71.7 12.6 %collective-permute-start.9 = (bf16[384,768]{1,0:T(8,128)(2,1)}, bf16[384,768]{1,0:T(8,128)(2,1)S(1)}, u32[]{:S(2)}, u32[]{:S(2)}) collective-permute-start(bf16[384,768]{1,0:T(8,128)(2,1)} %collective-permute-done.8.refs_8_), channel_id=1, source_target_pairs={{0,32},{1,97},{32,64},{33,1},{64,96},{65,33},{96,0},{97,65},{2,34}... | collective-permute-start | bytes 1769480 | tf_op jit(solution)/shard_map/ppermute | solution.py:44
  78.0 38.0 %copy-start.14 = (bf16[384,768]{1,0:T(8,128)(2,1)}, bf16[384,768]{1,0:T(8,128)(2,1)S(1)}, u32[]{:S(2)}) copy-start(bf16[384,768]{1,0:T(8,128)(2,1)S(1)} %collective-permute-done.12.refs_13_) | copy-start | bytes 1769476
  78.0 12.6 %collective-permute-start.13 = (bf16[384,768]{1,0:T(8,128)(2,1)S(1)}, bf16[384,768]{1,0:T(8,128)(2,1)S(1)}, u32[]{:S(2)}, u32[]{:S(2)}) collective-permute-start(bf16[384,768]{1,0:T(8,128)(2,1)S(1)} %collective-permute-done.12.refs_13_), channel_id=1, source_target_pairs={{0,32},{1,97},{32,64},{33,1},{64,96},{65,33},{96,0},{97,65},{2,34}... | collective-permute-start | bytes 1769480 | tf_op jit(solution)/shard_map/ppermute | solution.py:44
  84.4 12.6 %collective-permute-start.10 = (bf16[384,768]{1,0:T(8,128)(2,1)S(1)}, bf16[384,768]{1,0:T(8,128)(2,1)S(1)}, u32[]{:S(2)}, u32[]{:S(2)}) collective-permute-start(bf16[384,768]{1,0:T(8,128)(2,1)S(1)} %collective-permute-done.9.refs_9_), channel_id=1, source_target_pairs={{0,32},{1,97},{32,64},{33,1},{64,96},{65,33},{96,0},{97,65},{2,34}... | collective-permute-start | bytes 1769480 | tf_op jit(solution)/shard_map/ppermute | solution.py:44
  84.4 19.0 %collective-permute-start.7 = (bf16[384,768]{1,0:T(8,128)(2,1)S(1)}, bf16[384,768]{1,0:T(8,128)(2,1)S(1)}, u32[]{:S(2)}, u32[]{:S(2)}) collective-permute-start(bf16[384,768]{1,0:T(8,128)(2,1)S(1)} %collective-permute-done.6.refs_6_), channel_id=1, source_target_pairs={{0,32},{1,97},{32,64},{33,1},{64,96},{65,33},{96,0},{97,65},{2,34}... | collective-permute-start | bytes 1769480 | tf_op jit(solution)/shard_map/ppermute | solution.py:44
  90.7 19.0 %collective-permute-start.14 = (bf16[384,768]{1,0:T(8,128)(2,1)S(1)}, bf16[384,768]{1,0:T(8,128)(2,1)S(1)}, u32[]{:S(2)}, u32[]{:S(2)}) collective-permute-start(bf16[384,768]{1,0:T(8,128)(2,1)S(1)} %collective-permute-done.13.refs_14_), channel_id=1, source_target_pairs={{0,32},{1,97},{32,64},{33,1},{64,96},{65,33},{96,0},{97,65},{2,34}... | collective-permute-start | bytes 1769480 | tf_op jit(solution)/shard_map/ppermute | solution.py:44
  97.0 19.1 %collective-permute-start.11 = (bf16[384,768]{1,0:T(8,128)(2,1)S(1)}, bf16[384,768]{1,0:T(8,128)(2,1)}, u32[]{:S(2)}, u32[]{:S(2)}) collective-permute-start(bf16[384,768]{1,0:T(8,128)(2,1)S(1)} %collective-permute-done.10.refs_10_), channel_id=1, source_target_pairs={{0,32},{1,97},{32,64},{33,1},{64,96},{65,33},{96,0},{97,65},{2,34}... | collective-permute-start | bytes 1769480 | tf_op jit(solution)/shard_map/ppermute | solution.py:44
  156.8 8.3 %collective-permute-start.17 = (bf16[2,128,128]{2,1,0:T(8,128)(2,1)S(1)}, bf16[2,128,128]{2,1,0:T(8,128)(2,1)S(1)}, u32[]{:S(2)}, u32[]{:S(2)}) collective-permute-start(bf16[2,128,128]{2,1,0:T(8,128)(2,1)S(1)} %get-tuple-element.30), channel_id=1, source_target_pairs={{0,96},{32,0},{64,32},{96,64},{1,97},{33,1},{65,33},{97,65},{2,98}... | collective-permute-start | bytes 196616 | tf_op jit(solution)/shard_map/ppermute | solution.py:27
  159.2 6.4 %collective-permute-start.16 = (bf16[2,128,128]{2,1,0:T(8,128)(2,1)S(1)}, bf16[2,128,128]{2,1,0:T(8,128)(2,1)S(1)}, u32[]{:S(2)}, u32[]{:S(2)}) collective-permute-start(bf16[2,128,128]{2,1,0:T(8,128)(2,1)S(1)} %get-tuple-element.30), channel_id=1, source_target_pairs={{0,64},{32,96},{64,0},{96,32},{1,65},{33,97},{65,1},{97,33},{2,66}... | collective-permute-start | bytes 196616 | tf_op jit(solution)/shard_map/ppermute | solution.py:27
  160.0 6.2 %collective-permute-start.15 = (bf16[2,128,128]{2,1,0:T(8,128)(2,1)S(1)}, bf16[2,128,128]{2,1,0:T(8,128)(2,1)S(1)}, u32[]{:S(2)}, u32[]{:S(2)}) collective-permute-start(bf16[2,128,128]{2,1,0:T(8,128)(2,1)S(1)} %get-tuple-element.30), channel_id=1, source_target_pairs={{0,32},{32,64},{64,96},{96,0},{1,33},{33,65},{65,97},{97,1},{2,34}... | collective-permute-start | bytes 196616 | tf_op jit(solution)/shard_map/ppermute | solution.py:27
  168.5 5.0 %collective-permute-start.18 = (f32[2,8,256]{2,1,0:T(8,128)S(1)}, f32[2,8,256]{2,1,0:T(8,128)S(1)}, u32[]{:S(2)}, u32[]{:S(2)}) collective-permute-start(f32[2,8,256]{2,1,0:T(8,128)S(1)} %get-tuple-element.32), channel_id=1, source_target_pairs={{0,8},{8,16},{16,24},{24,0},{1,9},{9,17},{17,25},{25,1},{2,10},{10... | collective-permute-start | bytes 49160 | tf_op jit(solution)/shard_map/ppermute | solution.py:31
  169.2 4.3 %collective-permute-start.19 = (f32[2,8,256]{2,1,0:T(8,128)S(1)}, f32[2,8,256]{2,1,0:T(8,128)S(1)}, u32[]{:S(2)}, u32[]{:S(2)}) collective-permute-start(f32[2,8,256]{2,1,0:T(8,128)S(1)} %get-tuple-element.33), channel_id=1, source_target_pairs={{0,24},{8,0},{16,8},{24,16},{1,25},{9,1},{17,9},{25,17},{2,26},{10... | collective-permute-start | bytes 49160 | tf_op jit(solution)/shard_map/ppermute | solution.py:31
  171.8 5.2 %collective-permute-start.20 = (f32[2,8,256]{2,1,0:T(8,128)S(1)}, f32[2,8,256]{2,1,0:T(8,128)S(1)}, u32[]{:S(2)}, u32[]{:S(2)}) collective-permute-start(f32[2,8,256]{2,1,0:T(8,128)S(1)} %get-tuple-element.34), channel_id=1, source_target_pairs={{0,16},{8,24},{16,0},{24,8},{1,17},{9,25},{17,1},{25,9},{2,18},{10... | collective-permute-start | bytes 49160 | tf_op jit(solution)/shard_map/ppermute | solution.py:31
  177.0 3.3 %collective-permute-start.21 = (f32[2,8,256]{2,1,0:T(8,128)S(1)}, f32[2,8,256]{2,1,0:T(8,128)S(1)}, u32[]{:S(2)}, u32[]{:S(2)}) collective-permute-start(f32[2,8,256]{2,1,0:T(8,128)S(1)} %add_add_fusion.1), channel_id=1, source_target_pairs={{0,1},{1,0},{2,3},{3,2},{4,5},{5,4},{6,7},{7,6},{8,9},{9,8},{10,11... | collective-permute-start | bytes 49160 | tf_op jit(solution)/shard_map/ppermute | solution.py:39
  177.1 15.6 %collective-permute-start.25 = (bf16[512,256]{1,0:T(8,128)(2,1)S(1)}, bf16[512,256]{1,0:T(8,128)(2,1)S(1)}, u32[]{:S(2)}, u32[]{:S(2)}) collective-permute-start(bf16[512,256]{1,0:T(8,128)(2,1)S(1)} %get-tuple-element.36), channel_id=1, source_target_pairs={{0,8},{8,16},{16,24},{24,0},{1,9},{9,17},{17,25},{25,1},{2,10},{10... | collective-permute-start | bytes 786440 | tf_op jit(solution)/shard_map/ppermute | solution.py:31
  177.1 15.5 %collective-permute-start.26 = (bf16[512,256]{1,0:T(8,128)(2,1)S(1)}, bf16[512,256]{1,0:T(8,128)(2,1)S(1)}, u32[]{:S(2)}, u32[]{:S(2)}) collective-permute-start(bf16[512,256]{1,0:T(8,128)(2,1)S(1)} %get-tuple-element.37), channel_id=1, source_target_pairs={{0,24},{8,0},{16,8},{24,16},{1,25},{9,1},{17,9},{25,17},{2,26},{10... | collective-permute-start | bytes 786440 | tf_op jit(solution)/shard_map/ppermute | solution.py:31
  180.4 12.3 %collective-permute-start.27 = (bf16[512,256]{1,0:T(8,128)(2,1)S(1)}, bf16[512,256]{1,0:T(8,128)(2,1)S(1)}, u32[]{:S(2)}, u32[]{:S(2)}) collective-permute-start(bf16[512,256]{1,0:T(8,128)(2,1)S(1)} %get-tuple-element.38), channel_id=1, source_target_pairs={{0,16},{8,24},{16,0},{24,8},{1,17},{9,25},{17,1},{25,9},{2,18},{10... | collective-permute-start | bytes 786440 | tf_op jit(solution)/shard_map/ppermute | solution.py:31
  180.4 5.3 %collective-permute-start.24 = (f32[2,8,256]{2,1,0:T(8,128)S(1)}, f32[2,8,256]{2,1,0:T(8,128)S(1)}, u32[]{:S(2)}, u32[]{:S(2)}) collective-permute-start(f32[2,8,256]{2,1,0:T(8,128)S(1)} %add.198), channel_id=1, source_target_pairs={{0,4},{2,6},{4,0},{6,2},{1,5},{3,7},{5,1},{7,3},{8,12},{10,14},{12... | collective-permute-start | bytes 49160 | tf_op jit(solution)/shard_map/ppermute | solution.py:35
  183.4 3.7 %collective-permute-start.23 = (f32[2,8,256]{2,1,0:T(8,128)S(1)}, f32[2,8,256]{2,1,0:T(8,128)S(1)}, u32[]{:S(2)}, u32[]{:S(2)}) collective-permute-start(f32[2,8,256]{2,1,0:T(8,128)S(1)} %add.198), channel_id=1, source_target_pairs={{0,6},{2,0},{4,2},{6,4},{1,7},{3,1},{5,3},{7,5},{8,14},{10,8},{12,... | collective-permute-start | bytes 49160 | tf_op jit(solution)/shard_map/ppermute | solution.py:35
  185.7 4.9 %collective-permute-start.22 = (f32[2,8,256]{2,1,0:T(8,128)S(1)}, f32[2,8,256]{2,1,0:T(8,128)S(1)}, u32[]{:S(2)}, u32[]{:S(2)}) collective-permute-start(f32[2,8,256]{2,1,0:T(8,128)S(1)} %add.198), channel_id=1, source_target_pairs={{0,2},{2,4},{4,6},{6,0},{1,3},{3,5},{5,7},{7,1},{8,10},{10,12},{12... | collective-permute-start | bytes 49160 | tf_op jit(solution)/shard_map/ppermute | solution.py:35
  (18 other events, 269.9 us)
Sparse Core Ops, SparseCore 0:
  29.2 99.0 all-gather.1

commit v3 on v2

--- a/solution.py
+++ b/solution.py
@@ -86,97 +86,119 @@
 
 
 def silu(total):
-    return (total / (1.0 + jnp.exp(-total))).astype(jnp.bfloat16)
-
-
-def project(others, place, x, *refs):
+    half = 0.5 * total
+    return (half + half * jnp.tanh(half)).astype(jnp.bfloat16)
+
+
+def project_own(place, x, *refs):
     wrefs = refs[: SIDE * SIDE]
-    out, xbuf, wfull, acc, result, wsem, xsem, osem = refs[-8:]
-    depth = SIDE * WROWS
-    count = SIDE - 1 if others else 1
-    spans = [lax.rem(place[0] + (j + 1 if others else 0), SIDE) for j in range(count)]
-    tiles = [pl.ds(i * depth, depth) for i in range(SIDE)]
-
-    def fetch_w(i):
-        for k in range(SIDE):
-            zz = along(place, 0, k)
-            rows = pl.ds(pl.multiple_of(i * depth + zz * WROWS, WROWS), WROWS)
+    out, wout, xbuf, wfull, result, wsem, xsem, osem = refs[-8:]
+    copies = [pltpu.make_async_copy(x, xbuf, xsem.at[0])]
+    for k in range(SIDE):
+        for i in range(SIDE):
+            at = along(place, 1, i) * SIDE + along(place, 0, k)
+            rows = pl.ds(pl.multiple_of(at * WROWS, WROWS), WROWS)
             n = SIDE * k + i
-            yield pltpu.make_async_copy(wrefs[n], wfull.at[rows], wsem.at[n])
-
-    def fetch_x(j, i):
-        source = x.at[spans[j]] if others else x
-        cols = pl.ds(pl.multiple_of(along(place, 1, i) * depth, depth), depth)
-        return pltpu.make_async_copy(
-            source.at[:, cols], xbuf.at[j, :, tiles[i]], xsem.at[SIDE * j + i]
+            copies.append(pltpu.make_async_copy(wrefs[n], wfull.at[rows], wsem.at[n]))
+    for copy in copies:
+        copy.start()
+    for copy in copies:
+        copy.wait()
+    outs = [pltpu.make_async_copy(wfull, wout, osem.at[0])]
+    outs[0].start()
+    for m in range(0, SPAN, BLOCK):
+        rows = pl.ds(m, BLOCK)
+        result[rows, :] = silu(
+            jnp.dot(xbuf[rows, :], wfull[...], preferred_element_type=jnp.float32)
         )
-
-    def start(i):
-        for copy in fetch_w(i):
+    outs.append(pltpu.make_async_copy(result, out.at[place[0]], osem.at[1]))
+    outs[1].start()
+    for copy in outs:
+        copy.wait()
+
+
+def project_others(place, x, w, own, out, wfull, sem):
+    depth = DEPTH // SIDE
+    step = pl.program_id(0)
+
+    @pl.when(step == 0)
+    def _():
+        tiles = [pl.ds(i * depth, depth) for i in range(SIDE)]
+        copies = [
+            pltpu.make_async_copy(w.at[t], wfull.at[t], sem.at[i]) for i, t in enumerate(tiles)
+        ]
+        for copy in copies:
             copy.start()
-        fetch_x(0, i).start()
-
-    start(0)
-    for i in range(SIDE):
-        if i + 1 < SIDE:
-            start(i + 1)
-        else:
-            for j in range(1, count):
-                for t in range(SIDE):
-                    fetch_x(j, t).start()
-        for copy in fetch_w(i):
+        total = None
+        for copy, t in zip(copies, tiles):
             copy.wait()
-        fetch_x(0, i).wait()
-        part = jnp.dot(
-            xbuf[0, :, tiles[i]], wfull[tiles[i], :], preferred_element_type=jnp.float32
-        )
-        if i == 0:
-            acc[...] = part
-        elif i + 1 < SIDE:
-            acc[...] += part
-        else:
-            result[0] = silu(acc[...] + part)
-    pltpu.make_async_copy(result.at[0], out.at[spans[0]], osem.at[0]).start()
-    for j in range(1, count):
-        for i in range(SIDE):
-            fetch_x(j, i).wait()
-        for m in range(0, SPAN, BLOCK):
-            rows = pl.ds(m, BLOCK)
-            result[j, rows, :] = silu(
-                jnp.dot(xbuf[j, rows, :], wfull[...], preferred_element_type=jnp.float32)
-            )
-        pltpu.make_async_copy(result.at[j], out.at[spans[j]], osem.at[j]).start()
-    for j in range(count):
-        pltpu.make_async_copy(result.at[j], out.at[spans[j]], osem.at[j]).wait()
-
-
-def call_project(place, x, w, held):
-    count = SIDE - 1 if held else 1
+            part = jnp.dot(x[0, :, t], wfull[t, :], preferred_element_type=jnp.float32)
+            total = part if total is None else total + part
+        out[0] = silu(total)
+
+    @pl.when(step > 0)
+    def _():
+        out[0] = silu(jnp.dot(x[0], wfull[...], preferred_element_type=jnp.float32))
+
+
+def call_project(place, tokens, group, w):
     smem = pl.BlockSpec(memory_space=pltpu.SMEM)
     hbm = pl.BlockSpec(memory_space=pl.ANY)
-    return pl.pallas_call(
-        functools.partial(project, bool(held)),
-        out_shape=jax.ShapeDtypeStruct((SIDE, SPAN, COLS), jnp.bfloat16),
-        in_specs=[smem] + [hbm] * (1 + len(w) + len(held)),
-        out_specs=hbm,
-        scratch_shapes=[
-            pltpu.VMEM((count, SPAN, DEPTH), jnp.bfloat16),
-            pltpu.VMEM((DEPTH, COLS), jnp.bfloat16),
-            pltpu.VMEM((SPAN, COLS), jnp.float32),
-            pltpu.VMEM((count, SPAN, COLS), jnp.bfloat16),
-            pltpu.SemaphoreType.DMA((SIDE * SIDE,)),
-            pltpu.SemaphoreType.DMA((SIDE * count,)),
-            pltpu.SemaphoreType.DMA((count,)),
-        ],
-        input_output_aliases={2 + len(w): 0} if held else {},
-        cost_estimate=pl.CostEstimate(
+    shape = jax.ShapeDtypeStruct((SIDE, SPAN, COLS), jnp.bfloat16)
+    whole = (DEPTH, COLS)
+
+    def cost(count):
+        return pl.CostEstimate(
             flops=2 * count * SPAN * DEPTH * COLS,
             bytes_accessed=(10 + 7 * count) << 20,
             transcendentals=0,
+        )
+
+    own, wfull = pl.pallas_call(
+        project_own,
+        out_shape=(shape, jax.ShapeDtypeStruct(whole, jnp.bfloat16)),
+        in_specs=[smem] + [hbm] * (1 + len(w)),
+        out_specs=(hbm, hbm),
+        scratch_shapes=[
+            pltpu.VMEM((SPAN, DEPTH), jnp.bfloat16),
+            pltpu.VMEM(whole, jnp.bfloat16),
+            pltpu.VMEM((SPAN, COLS), jnp.bfloat16),
+            pltpu.SemaphoreType.DMA((SIDE * SIDE,)),
+            pltpu.SemaphoreType.DMA((1,)),
+            pltpu.SemaphoreType.DMA((2,)),
+        ],
+        cost_estimate=cost(1),
+        compiler_params=VMEM,
+        name="project_own",
+    )(place, tokens, *w)
+    count = SIDE - 1
+    parts = SPAN // BLOCK
+
+    def there(i, place):
+        return (lax.rem(place[0] + i // parts + 1, SIDE), i % parts, 0)
+
+    return pl.pallas_call(
+        project_others,
+        out_shape=shape,
+        grid_spec=pltpu.PrefetchScalarGridSpec(
+            num_scalar_prefetch=1,
+            grid=(count * parts,),
+            in_specs=[
+                pl.BlockSpec((1, BLOCK, DEPTH), there),
+                hbm,
+                hbm,
+            ],
+            out_specs=pl.BlockSpec((1, BLOCK, COLS), there),
+            scratch_shapes=[
+                pltpu.VMEM(whole, jnp.bfloat16),
+                pltpu.SemaphoreType.DMA((SIDE,)),
+            ],
         ),
+        input_output_aliases={3: 0},
+        cost_estimate=cost(count),
         compiler_params=VMEM,
-        name="project_others" if held else "project_own",
-    )(place, x, *w, *held)
+        name="project_others",
+    )(place, group, wfull, own)
 
 
 def decays(cumr, cumc, docr, docc, out):
@@ -345,8 +367,7 @@
     mine = lax.optimization_barrier((mine, *first))[0]
     group = lax.all_gather(mine, ("z", "x", "c"), axis=0, tiled=True)
 
-    proj = call_project(place, tokens, w, [])
-    proj = call_project(place, group.reshape(SIDE, SPAN, DEPTH), w, [proj])
+    proj = call_project(place, tokens, group.reshape(SIDE, SPAN, DEPTH), w)
     proj = proj.reshape(GROUP, COLS)
     states, total = pl.pallas_call(
         block_states,
@@ -404,12 +425,14 @@
         name="inters",
     )(place, qd, intra, states, passes, fac, s1, s2, s3)
 
-    part = out[SIDE]
+    pieces, part = list(out[:SIDE]), out[SIDE]
+    pieces[1], pieces[2] = move_z(pieces[1], 1), move_z(pieces[2], -1)
     for i, d in enumerate((1, -1, 2)):
         part = part + move_z(out[SIDE + 1 + i], d)
     part = part + swap(part)
+    part = lax.optimization_barrier((part, pieces[1], pieces[2]))[0]
+    pieces[3] = move_z(pieces[3], 2)
     part = part + move_x(part, 1) + move_x(part, -1) + move_x(part, 2)
-    pieces = [out[0]] + [move_z(out[1 + i], d) for i, d in enumerate((1, -1, 2))]
     return pl.pallas_call(
         finish,
         out_shape=jax.ShapeDtypeStruct((SPAN, SIDE * width), jnp.bfloat16),

time: 202 us -> 201 us (level)
  starting transfers between devices: 30 us -> 37.7 us
  waiting for transfers between devices: 85.5 us -> 78 us
    ppermute x15, starting transfers between devices: 12.7 us -> 17.1 us  [opposed(): return lax.ppermute(a, (axis, 'c'), perm)]
    ppermute x15, waiting for transfers between devices: 73.5 us -> 69.7 us  [opposed(): return lax.ppermute(a, (axis, 'c'), perm)]
    ppermute x3, starting transfers between devices: 5.63 us -> 7.86 us  [move_x(): return lax.ppermute(a, 'x', [(s, (s + d) % 4) for s in range(4)])]
    ppermute x6, waiting for transfers between devices: 6.22 us -> 4.1 us  [move_z(): return lax.ppermute(a, 'z', [(s, (s + d) % 4) for s in range(4)])]
    unnamed x45 -> x41, local copies, waits for them, and re-layouts: 8.98 us -> 8.15 us
  transfers between devices with their start and end apart: 29 -> 29, of which waited for: 20 -> 17; matrix products, arithmetic and copies ran while one was open for 6% -> 6% of each run, Pallas kernels for 9% -> 9%
where the time goes in v3:
time: 201 us
  waiting for transfers between devices  78 us (39%)
  Pallas kernels  48 us (24%)
  starting transfers between devices  37.7 us (19%)
  local copies, waits for them, and re-layouts  20.1 us (10%)
  between operations  13.8 us (7%)
  other arithmetic  3 us (1%)
    ppermute x15, waiting for transfers between devices, opposed(): return lax.ppermute(a, (axis, 'c'), perm)  69.7 us
    pallas_call x1, Pallas kernels, call_project(): pl.pallas_call(project_others, out_shape=shape, grid_spec=pltpu.PrefetchS...  22.9 us
    ppermute x15, starting transfers between devices, opposed(): return lax.ppermute(a, (axis, 'c'), perm)  17.1 us
    pallas_call x1, Pallas kernels, call_project(): pl.pallas_call(project_own, out_shape=(shape, jax.ShapeDtypeStruct(whole,...  12.5 us
    unnamed x41, local copies, waits for them, and re-layouts  8.15 us
    ppermute x3, starting transfers between devices, move_x(): return lax.ppermute(a, 'x', [(s, (s + d) % 4) for s in range(4)])  7.86 us
    ppermute x6, starting transfers between devices, move_z(): return lax.ppermute(a, 'z', [(s, (s + d) % 4) for s in range(4)])  7.69 us
    ppermute x3, starting transfers between devices, move_y(): return lax.ppermute(a, 'y', [(s, (s + d) % 4) for s in range(4)])  5.01 us
  transfers between devices with their start and end apart: 29, of which 17 were waited for; matrix products, arithmetic and copies ran while one was open for 6% of the time, Pallas kernels for 9%

profile of v3, /device:TPU:0, one launch (start us, length us, event | category | flops | bytes accessed | tf_op | source)
XLA Modules:
  0.0 200.5 jit_solution(2774332751848137044)
XLA Ops:
  6.5 3.0 %copy.66 = bf16[384,3,1024]{0,2,1:T(8,128)(2,1)S(1)} copy(bf16[384,3,1024]{2,0,1:T(8,128)(2,1)} %param.6) | data formatting | bytes 4718592 | tf_op args[1]
  12.3 2.1 %collective-permute-start = (bf16[384,768]{1,0:T(8,128)(2,1)S(1)}, bf16[384,768]{1,0:T(8,128)(2,1)S(1)}, u32[]{:S(2)}, u32[]{:S(2)}) collective-permute-start(bf16[384,768]{1,0:T(8,128)(2,1)S(1)} %copy.67), channel_id=1, source_target_pairs={{0,8},{1,25},{8,16},{9,1},{16,24},{17,9},{24,0},{25,17},{2,10},{3,... | collective-permute-start | bytes 1769480 | tf_op jit(solution)/shard_map/ppermute | solution.py:44
  15.7 2.2 %collective-permute-start.1 = (bf16[384,768]{1,0:T(8,128)(2,1)S(1)}, bf16[384,768]{1,0:T(8,128)(2,1)}, u32[]{:S(2)}, u32[]{:S(2)}) collective-permute-start(bf16[384,768]{1,0:T(8,128)(2,1)S(1)} %copy.68), channel_id=1, source_target_pairs={{0,24},{1,9},{8,0},{9,17},{16,8},{17,25},{24,16},{25,1},{2,26},{3,... | collective-permute-start | bytes 1769480 | tf_op jit(solution)/shard_map/ppermute | solution.py:44
  17.9 2.1 %constant_dynamic-slice_fusion.10 = bf16[64,6144]{1,0:T(8,128)(2,1)} fusion(bf16[512,6144]{1,0:T(8,128)(2,1)} %x.3, s32[]{:T(128)S(6)} %select_n.133), kind=kLoop, calls=%fused_computation.27 | loop fusion | bytes 1572868 | tf_op jit(solution)/shard_map/dynamic_slice | solution.py:366
  19.9 7.5 %collective-permute-done.refs_4_ = bf16[384,768]{1,0:T(8,128)(2,1)S(1)} collective-permute-done((bf16[384,768]{1,0:T(8,128)(2,1)S(1)}, bf16[384,768]{1,0:T(8,128)(2,1)S(1)}, u32[]{:S(2)}, u32[]{:S(2)}) %collective-permute-start) | collective-permute-done | bytes 589856 | tf_op jit(solution)/shard_map/ppermute | solution.py:44
  32.8 3.2 %collective-permute-start.8 = (bf16[384,768]{1,0:T(8,128)(2,1)}, bf16[384,768]{1,0:T(8,128)(2,1)}, u32[]{:S(2)}, u32[]{:S(2)}) collective-permute-start(bf16[384,768]{1,0:T(8,128)(2,1)} %copy.70), channel_id=1, source_target_pairs={{0,16},{1,17},{8,24},{9,25},{16,0},{17,1},{24,8},{25,9},{2,18},{3,... | collective-permute-start | bytes 1769480 | tf_op jit(solution)/shard_map/ppermute | solution.py:44
  45.2 1.7 decays.1.decay
  46.9 2.0 copy-done.3
  48.9 4.3 %collective-permute-done.3.refs_2_ = bf16[384,768]{1,0:T(8,128)(2,1)} collective-permute-done((bf16[384,768]{1,0:T(8,128)(2,1)}, bf16[384,768]{1,0:T(8,128)(2,1)}, u32[]{:S(2)}, u32[]{:S(2)}) %collective-permute-start.3) | collective-permute-done | bytes 589856 | tf_op jit(solution)/shard_map/ppermute | solution.py:44
  53.6 5.9 %collective-permute-done.5.refs_5_ = bf16[384,768]{1,0:T(8,128)(2,1)} collective-permute-done((bf16[384,768]{1,0:T(8,128)(2,1)}, bf16[384,768]{1,0:T(8,128)(2,1)}, u32[]{:S(2)}, u32[]{:S(2)}) %collective-permute-start.5) | collective-permute-done | bytes 589856 | tf_op jit(solution)/shard_map/ppermute | solution.py:44
  61.5 4.3 %collective-permute-done.4.refs_3_ = bf16[384,768]{1,0:T(8,128)(2,1)S(1)} collective-permute-done((bf16[384,768]{1,0:T(8,128)(2,1)}, bf16[384,768]{1,0:T(8,128)(2,1)S(1)}, u32[]{:S(2)}, u32[]{:S(2)}) %collective-permute-start.4) | collective-permute-done | bytes 589856 | tf_op jit(solution)/shard_map/ppermute | solution.py:44
  65.7 6.3 %collective-permute-done.6.refs_6_ = bf16[384,768]{1,0:T(8,128)(2,1)S(1)} collective-permute-done((bf16[384,768]{1,0:T(8,128)(2,1)}, bf16[384,768]{1,0:T(8,128)(2,1)S(1)}, u32[]{:S(2)}, u32[]{:S(2)}) %collective-permute-start.6) | collective-permute-done | bytes 589856 | tf_op jit(solution)/shard_map/ppermute | solution.py:44
  72.4 5.9 %collective-permute-done.12.refs_13_ = bf16[384,768]{1,0:T(8,128)(2,1)S(1)} collective-permute-done((bf16[384,768]{1,0:T(8,128)(2,1)}, bf16[384,768]{1,0:T(8,128)(2,1)S(1)}, u32[]{:S(2)}, u32[]{:S(2)}) %collective-permute-start.12) | collective-permute-done | bytes 589856 | tf_op jit(solution)/shard_map/ppermute | solution.py:44
  78.7 5.9 %collective-permute-done.9.refs_9_ = bf16[384,768]{1,0:T(8,128)(2,1)S(1)} collective-permute-done((bf16[384,768]{1,0:T(8,128)(2,1)}, bf16[384,768]{1,0:T(8,128)(2,1)S(1)}, u32[]{:S(2)}, u32[]{:S(2)}) %collective-permute-start.9) | collective-permute-done | bytes 589856 | tf_op jit(solution)/shard_map/ppermute | solution.py:44
  86.3 4.7 %collective-permute-done.13.refs_14_ = bf16[384,768]{1,0:T(8,128)(2,1)S(1)} collective-permute-done((bf16[384,768]{1,0:T(8,128)(2,1)S(1)}, bf16[384,768]{1,0:T(8,128)(2,1)S(1)}, u32[]{:S(2)}, u32[]{:S(2)}) %collective-permute-start.13) | collective-permute-done | bytes 589856 | tf_op jit(solution)/shard_map/ppermute | solution.py:44
  91.4 5.9 %collective-permute-done.10.refs_10_ = bf16[384,768]{1,0:T(8,128)(2,1)S(1)} collective-permute-done((bf16[384,768]{1,0:T(8,128)(2,1)S(1)}, bf16[384,768]{1,0:T(8,128)(2,1)S(1)}, u32[]{:S(2)}, u32[]{:S(2)}) %collective-permute-start.10) | collective-permute-done | bytes 589856 | tf_op jit(solution)/shard_map/ppermute | solution.py:44
  98.3 11.7 %collective-permute-done.14.refs_15_ = bf16[384,768]{1,0:T(8,128)(2,1)S(1)} collective-permute-done((bf16[384,768]{1,0:T(8,128)(2,1)S(1)}, bf16[384,768]{1,0:T(8,128)(2,1)S(1)}, u32[]{:S(2)}, u32[]{:S(2)}) %collective-permute-start.14) | collective-permute-done | bytes 589856 | tf_op jit(solution)/shard_map/ppermute | solution.py:44
  110.8 5.6 %collective-permute-done.11.refs_11_ = bf16[384,768]{1,0:T(8,128)(2,1)} collective-permute-done((bf16[384,768]{1,0:T(8,128)(2,1)S(1)}, bf16[384,768]{1,0:T(8,128)(2,1)}, u32[]{:S(2)}, u32[]{:S(2)}) %collective-permute-start.11) | collective-permute-done | bytes 589856 | tf_op jit(solution)/shard_map/ppermute | solution.py:44
  116.4 12.5 %project_own.1 = (bf16[4,512,768]{2,1,0:T(8,128)(2,1)}, bf16[6144,768]{1,0:T(8,128)(2,1)}) custom-call(s32[4]{0:T(128)} %pad_add_fusion.place, bf16[512,6144]{1,0:T(8,128)(2,1)} %x.3, bf16[384,768]{1,0:T(8,128)(2,1)} %copy.81.refs_0_, bf16[384,768]{1,0:T(8,128)(2,1)} %collective-permute-done.2.refs_1_, bf16[384,768]{1,0:T(8,128)(2,1)} %collective-permute-done.3.refs_2_, ...), custom_call_target="tpu_custom_call" | custom-call | flops 4831838208 | bytes 17825792 | tf_op jit(solution)/shard_map/project_own/pallas_call | solution.py:157
  129.0 22.9 %project_others.1 = bf16[4,512,768]{2,1,0:T(8,128)(2,1)} custom-call(s32[4]{0:T(128)} %pad_add_fusion.place, bf16[4,512,6144]{2,1,0:T(8,128)(2,1)} %bitcast.55, bf16[6144,768]{1,0:T(8,128)(2,1)} %get-tuple-element.30.w, bf16[4,512,768]{2,1,0:T(8,128)(2,1)} %get-tuple-element.31.own), custom_call_target="tpu_custom_call", output_to_operand_aliasing={{}: (3, {})} | custom-call | flops 14495514624 | bytes 32505856 | tf_op jit(solution)/shard_map/project_others/pallas_call | solution.py:180
  151.8 1.9 copy-done.2
  153.7 2.4 %states.1 = (f32[8,2,128,128]{3,2,1,0:T(8,128)S(1)}, bf16[2,128,128]{2,1,0:T(8,128)(2,1)S(1)}) custom-call(bf16[2048,768]{1,0:T(8,128)(2,1)S(1)} %bitcast.37, bf16[2048,768]{1,0:T(8,128)(2,1)S(1)} %bitcast.38, f32[2048,2]{1,0:T(8,128)S(1)} %bitcast.40, f32[2,8]{1,0:T(2,128)S(1)} %concatenate.3.suffix), custom_call_target="tpu_custom_call" | custom-call | flops 134217728 | bytes 4194304 | tf_op jit(solution)/shard_map/states/pallas_call | solution.py:372
  157.0 2.7 %collective-permute-start.16 = (bf16[2,128,128]{2,1,0:T(8,128)(2,1)S(1)}, bf16[2,128,128]{2,1,0:T(8,128)(2,1)S(1)}, u32[]{:S(2)}, u32[]{:S(2)}) collective-permute-start(bf16[2,128,128]{2,1,0:T(8,128)(2,1)S(1)} %get-tuple-element.35), channel_id=1, source_target_pairs={{0,64},{32,96},{64,0},{96,32},{1,65},{33,97},{65,1},{97,33},{2,66}... | collective-permute-start | bytes 196616 | tf_op jit(solution)/shard_map/ppermute | solution.py:27
  161.2 4.3 %intras.1 = (bf16[2048,256]{1,0:T(8,128)(2,1)S(1)}, f32[2048,256]{1,0:T(8,128)S(1)}) custom-call(bf16[2048,768]{1,0:T(8,128)(2,1)S(1)} %bitcast.39, f32[8,2,256,256]{3,2,1,0:T(8,128)S(1)} %copy-done.4, f32[2048,2]{1,0:T(8,128)S(1)} %bitcast.43), custom_call_target="tpu_custom_call" | custom-call | flops 1073741824 | bytes 8388608 | tf_op jit(solution)/shard_map/intras/pallas_call | solution.py:395
  165.5 2.2 %inters.1 = (bf16[512,256]{1,0:T(8,128)(2,1)S(1)}, bf16[512,256]{1,0:T(8,128)(2,1)S(1)}, bf16[512,256]{1,0:T(8,128)(2,1)S(1)}, bf16[512,256]{1,0:T(8,128)(2,1)S(...) custom-call(s32[4]{0:T(128)S(1)} %copy-done.6, ...), custom_call_target="tpu_custom_call" | custom-call | flops 268435456 | bytes 6291456 | tf_op jit(solution)/shard_map/inters/pallas_call | solution.py:412
  168.7 2.4 %collective-permute-start.23 = (bf16[512,256]{1,0:T(8,128)(2,1)S(1)}, bf16[512,256]{1,0:T(8,128)(2,1)S(1)}, u32[]{:S(2)}, u32[]{:S(2)}) collective-permute-start(bf16[512,256]{1,0:T(8,128)(2,1)S(1)} %get-tuple-element.41), channel_id=1, source_target_pairs={{0,24},{8,0},{16,8},{24,16},{1,25},{9,1},{17,9},{25,17},{2,26},{10... | collective-permute-start | bytes 786440 | tf_op jit(solution)/shard_map/ppermute | solution.py:31
  171.1 3.2 %collective-permute-start.19 = (f32[2,8,256]{2,1,0:T(8,128)S(1)}, f32[2,8,256]{2,1,0:T(8,128)S(1)}, u32[]{:S(2)}, u32[]{:S(2)}) collective-permute-start(f32[2,8,256]{2,1,0:T(8,128)S(1)} %get-tuple-element.38), channel_id=1, source_target_pairs={{0,24},{8,0},{16,8},{24,16},{1,25},{9,1},{17,9},{25,17},{2,26},{10... | collective-permute-start | bytes 49160 | tf_op jit(solution)/shard_map/ppermute | solution.py:31
  174.3 2.9 %collective-permute-done.18 = f32[2,8,256]{2,1,0:T(8,128)S(1)} collective-permute-done((f32[2,8,256]{2,1,0:T(8,128)S(1)}, f32[2,8,256]{2,1,0:T(8,128)S(1)}, u32[]{:S(2)}, u32[]{:S(2)}) %collective-permute-start.18) | collective-permute-done | bytes 16416 | tf_op jit(solution)/shard_map/ppermute | solution.py:31
  180.8 4.3 %collective-permute-start.24 = (f32[2,8,256]{2,1,0:T(8,128)S(1)}, f32[2,8,256]{2,1,0:T(8,128)S(1)}, u32[]{:S(2)}, u32[]{:S(2)}) collective-permute-start(f32[2,8,256]{2,1,0:T(8,128)S(1)} %add.198), channel_id=1, source_target_pairs={{0,2},{2,4},{4,6},{6,0},{1,3},{3,5},{5,7},{7,1},{8,10},{10,12},{12... | collective-permute-start | bytes 49160 | tf_op jit(solution)/shard_map/ppermute | solution.py:35
  186.4 2.2 %collective-permute-start.26 = (f32[2,8,256]{2,1,0:T(8,128)S(1)}, f32[2,8,256]{2,1,0:T(8,128)S(1)}, u32[]{:S(2)}, u32[]{:S(2)}) collective-permute-start(f32[2,8,256]{2,1,0:T(8,128)S(1)} %add.198), channel_id=1, source_target_pairs={{0,4},{2,6},{4,0},{6,2},{1,5},{3,7},{5,1},{7,3},{8,12},{10,14},{12... | collective-permute-start | bytes 49160 | tf_op jit(solution)/shard_map/ppermute | solution.py:35
  188.8 2.8 %collective-permute-done.26 = f32[2,8,256]{2,1,0:T(8,128)S(1)} collective-permute-done((f32[2,8,256]{2,1,0:T(8,128)S(1)}, f32[2,8,256]{2,1,0:T(8,128)S(1)}, u32[]{:S(2)}, u32[]{:S(2)}) %collective-permute-start.26) | collective-permute-done | bytes 16416 | tf_op jit(solution)/shard_map/ppermute | solution.py:35
  191.7 2.0 %finish.1 = bf16[512,1024]{1,0:T(8,128)(2,1)} custom-call(s32[4]{0:T(128)S(1)} %copy-done.6, f32[2,8,256]{2,1,0:T(8,128)S(1)} %add_add_fusion.total, f32[1,1024]{1,0:T(1,128)S(1)} %bitcast.45, bf16[512,256]{1,0:T(8,128)(2,1)S(1)} %get-tuple-element.43.p0, bf16[512,256]{1,0:T(8,128)(2,1)S(1)} %collective-permute-done.22.p1, ...), custom_call_target="tpu_custom_call" | custom-call | flops 4194304 | bytes 3145728 | tf_op jit(solution)/shard_map/finish/pallas_call | solution.py:436
  (133 shorter events, 33.7 us)
Async XLA Ops:
  6.5 122.4 %all-gather.2.cloned.1.call-start = ((), (), s32[]{:S(2)}) async-start(), calls=%async_computation | async-start | bytes 25952256 | tf_op jit(solution)/shard_map/all_gather | solution.py:368
  12.3 15.1 %collective-permute-start = (bf16[384,768]{1,0:T(8,128)(2,1)S(1)}, bf16[384,768]{1,0:T(8,128)(2,1)S(1)}, u32[]{:S(2)}, u32[]{:S(2)}) collective-permute-start(bf16[384,768]{1,0:T(8,128)(2,1)S(1)} %copy.67), channel_id=1, source_target_pairs={{0,8},{1,25},{8,16},{9,1},{16,24},{17,9},{24,0},{25,17},{2,10},{3,... | collective-permute-start | bytes 1769480 | tf_op jit(solution)/shard_map/ppermute | solution.py:44
  15.7 13.4 %collective-permute-start.1 = (bf16[384,768]{1,0:T(8,128)(2,1)S(1)}, bf16[384,768]{1,0:T(8,128)(2,1)}, u32[]{:S(2)}, u32[]{:S(2)}) collective-permute-start(bf16[384,768]{1,0:T(8,128)(2,1)S(1)} %copy.68), channel_id=1, source_target_pairs={{0,24},{1,9},{8,0},{9,17},{16,8},{17,25},{24,16},{25,1},{2,26},{3,... | collective-permute-start | bytes 1769480 | tf_op jit(solution)/shard_map/ppermute | solution.py:44
  30.2 11.6 %collective-permute-start.2 = (bf16[384,768]{1,0:T(8,128)(2,1)}, bf16[384,768]{1,0:T(8,128)(2,1)}, u32[]{:S(2)}, u32[]{:S(2)}) collective-permute-start(bf16[384,768]{1,0:T(8,128)(2,1)} %copy.81.refs_0_), channel_id=1, source_target_pairs={{0,32},{1,97},{32,64},{33,1},{64,96},{65,33},{96,0},{97,65},{2,34}... | collective-permute-start | bytes 1769480 | tf_op jit(solution)/shard_map/ppermute | solution.py:44
  32.8 28.7 %collective-permute-start.8 = (bf16[384,768]{1,0:T(8,128)(2,1)}, bf16[384,768]{1,0:T(8,128)(2,1)}, u32[]{:S(2)}, u32[]{:S(2)}) collective-permute-start(bf16[384,768]{1,0:T(8,128)(2,1)} %copy.70), channel_id=1, source_target_pairs={{0,16},{1,17},{8,24},{9,25},{16,0},{17,1},{24,8},{25,9},{2,18},{3,... | collective-permute-start | bytes 1769480 | tf_op jit(solution)/shard_map/ppermute | solution.py:44
  41.8 11.4 %collective-permute-start.3 = (bf16[384,768]{1,0:T(8,128)(2,1)}, bf16[384,768]{1,0:T(8,128)(2,1)}, u32[]{:S(2)}, u32[]{:S(2)}) collective-permute-start(bf16[384,768]{1,0:T(8,128)(2,1)} %collective-permute-done.2.refs_1_), channel_id=1, source_target_pairs={{0,32},{1,97},{32,64},{33,1},{64,96},{65,33},{96,0},{97,65},{2,34}... | collective-permute-start | bytes 1769480 | tf_op jit(solution)/shard_map/ppermute | solution.py:44
  43.4 16.1 %collective-permute-start.5 = (bf16[384,768]{1,0:T(8,128)(2,1)}, bf16[384,768]{1,0:T(8,128)(2,1)}, u32[]{:S(2)}, u32[]{:S(2)}) collective-permute-start(bf16[384,768]{1,0:T(8,128)(2,1)} %copy-done.9), channel_id=1, source_target_pairs={{0,32},{1,97},{32,64},{33,1},{64,96},{65,33},{96,0},{97,65},{2,34}... | collective-permute-start | bytes 1769480 | tf_op jit(solution)/shard_map/ppermute | solution.py:44
  53.2 12.5 %collective-permute-start.4 = (bf16[384,768]{1,0:T(8,128)(2,1)}, bf16[384,768]{1,0:T(8,128)(2,1)S(1)}, u32[]{:S(2)}, u32[]{:S(2)}) collective-permute-start(bf16[384,768]{1,0:T(8,128)(2,1)} %collective-permute-done.3.refs_2_), channel_id=1, source_target_pairs={{0,32},{1,97},{32,64},{33,1},{64,96},{65,33},{96,0},{97,65},{2,34}... | collective-permute-start | bytes 1769480 | tf_op jit(solution)/shard_map/ppermute | solution.py:44
  59.5 12.5 %collective-permute-start.6 = (bf16[384,768]{1,0:T(8,128)(2,1)}, bf16[384,768]{1,0:T(8,128)(2,1)S(1)}, u32[]{:S(2)}, u32[]{:S(2)}) collective-permute-start(bf16[384,768]{1,0:T(8,128)(2,1)} %collective-permute-done.5.refs_5_), channel_id=1, source_target_pairs={{0,32},{1,97},{32,64},{33,1},{64,96},{65,33},{96,0},{97,65},{2,34}... | collective-permute-start | bytes 1769480 | tf_op jit(solution)/shard_map/ppermute | solution.py:44
  60.2 18.2 %collective-permute-start.12 = (bf16[384,768]{1,0:T(8,128)(2,1)}, bf16[384,768]{1,0:T(8,128)(2,1)S(1)}, u32[]{:S(2)}, u32[]{:S(2)}) collective-permute-start(bf16[384,768]{1,0:T(8,128)(2,1)} %collective-permute-done.1.refs_12_), channel_id=1, source_target_pairs={{0,32},{1,97},{32,64},{33,1},{64,96},{65,33},{96,0},{97,65},{2,34}... | collective-permute-start | bytes 1769480 | tf_op jit(solution)/shard_map/ppermute | solution.py:44
  65.7 50.7 %copy-start.10 = (bf16[384,768]{1,0:T(8,128)(2,1)}, bf16[384,768]{1,0:T(8,128)(2,1)S(1)}, u32[]{:S(2)}) copy-start(bf16[384,768]{1,0:T(8,128)(2,1)S(1)} %collective-permute-done.4.refs_3_) | copy-start | bytes 1769476
  72.0 44.3 %copy-start.11 = (bf16[384,768]{1,0:T(8,128)(2,1)}, bf16[384,768]{1,0:T(8,128)(2,1)S(1)}, u32[]{:S(2)}) copy-start(bf16[384,768]{1,0:T(8,128)(2,1)S(1)} %collective-permute-done.6.refs_6_) | copy-start | bytes 1769476
  72.1 12.6 %collective-permute-start.9 = (bf16[384,768]{1,0:T(8,128)(2,1)}, bf16[384,768]{1,0:T(8,128)(2,1)S(1)}, u32[]{:S(2)}, u32[]{:S(2)}) collective-permute-start(bf16[384,768]{1,0:T(8,128)(2,1)} %collective-permute-done.8.refs_8_), channel_id=1, source_target_pairs={{0,32},{1,97},{32,64},{33,1},{64,96},{65,33},{96,0},{97,65},{2,34}... | collective-permute-start | bytes 1769480 | tf_op jit(solution)/shard_map/ppermute | solution.py:44
  78.4 38.0 %copy-start.12 = (bf16[384,768]{1,0:T(8,128)(2,1)}, bf16[384,768]{1,0:T(8,128)(2,1)S(1)}, u32[]{:S(2)}) copy-start(bf16[384,768]{1,0:T(8,128)(2,1)S(1)} %collective-permute-done.12.refs_13_) | copy-start | bytes 1769476
  78.4 12.6 %collective-permute-start.13 = (bf16[384,768]{1,0:T(8,128)(2,1)S(1)}, bf16[384,768]{1,0:T(8,128)(2,1)S(1)}, u32[]{:S(2)}, u32[]{:S(2)}) collective-permute-start(bf16[384,768]{1,0:T(8,128)(2,1)S(1)} %collective-permute-done.12.refs_13_), channel_id=1, source_target_pairs={{0,32},{1,97},{32,64},{33,1},{64,96},{65,33},{96,0},{97,65},{2,34}... | collective-permute-start | bytes 1769480 | tf_op jit(solution)/shard_map/ppermute | solution.py:44
  84.7 12.6 %collective-permute-start.10 = (bf16[384,768]{1,0:T(8,128)(2,1)S(1)}, bf16[384,768]{1,0:T(8,128)(2,1)S(1)}, u32[]{:S(2)}, u32[]{:S(2)}) collective-permute-start(bf16[384,768]{1,0:T(8,128)(2,1)S(1)} %collective-permute-done.9.refs_9_), channel_id=1, source_target_pairs={{0,32},{1,97},{32,64},{33,1},{64,96},{65,33},{96,0},{97,65},{2,34}... | collective-permute-start | bytes 1769480 | tf_op jit(solution)/shard_map/ppermute | solution.py:44
  85.1 24.9 %collective-permute-start.7 = (bf16[384,768]{1,0:T(8,128)(2,1)S(1)}, bf16[384,768]{1,0:T(8,128)(2,1)S(1)}, u32[]{:S(2)}, u32[]{:S(2)}) collective-permute-start(bf16[384,768]{1,0:T(8,128)(2,1)S(1)} %collective-permute-done.6.refs_6_), channel_id=1, source_target_pairs={{0,32},{1,97},{32,64},{33,1},{64,96},{65,33},{96,0},{97,65},{2,34}... | collective-permute-start | bytes 1769480 | tf_op jit(solution)/shard_map/ppermute | solution.py:44
  91.0 19.0 %collective-permute-start.14 = (bf16[384,768]{1,0:T(8,128)(2,1)S(1)}, bf16[384,768]{1,0:T(8,128)(2,1)S(1)}, u32[]{:S(2)}, u32[]{:S(2)}) collective-permute-start(bf16[384,768]{1,0:T(8,128)(2,1)S(1)} %collective-permute-done.13.refs_14_), channel_id=1, source_target_pairs={{0,32},{1,97},{32,64},{33,1},{64,96},{65,33},{96,0},{97,65},{2,34}... | collective-permute-start | bytes 1769480 | tf_op jit(solution)/shard_map/ppermute | solution.py:44
  97.3 19.1 %collective-permute-start.11 = (bf16[384,768]{1,0:T(8,128)(2,1)S(1)}, bf16[384,768]{1,0:T(8,128)(2,1)}, u32[]{:S(2)}, u32[]{:S(2)}) collective-permute-start(bf16[384,768]{1,0:T(8,128)(2,1)S(1)} %collective-permute-done.10.refs_10_), channel_id=1, source_target_pairs={{0,32},{1,97},{32,64},{33,1},{64,96},{65,33},{96,0},{97,65},{2,34}... | collective-permute-start | bytes 1769480 | tf_op jit(solution)/shard_map/ppermute | solution.py:44
  156.2 9.3 %collective-permute-start.15 = (bf16[2,128,128]{2,1,0:T(8,128)(2,1)S(1)}, bf16[2,128,128]{2,1,0:T(8,128)(2,1)S(1)}, u32[]{:S(2)}, u32[]{:S(2)}) collective-permute-start(bf16[2,128,128]{2,1,0:T(8,128)(2,1)S(1)} %get-tuple-element.35), channel_id=1, source_target_pairs={{0,32},{32,64},{64,96},{96,0},{1,33},{33,65},{65,97},{97,1},{2,34}... | collective-permute-start | bytes 196616 | tf_op jit(solution)/shard_map/ppermute | solution.py:27
  157.0 8.4 %collective-permute-start.16 = (bf16[2,128,128]{2,1,0:T(8,128)(2,1)S(1)}, bf16[2,128,128]{2,1,0:T(8,128)(2,1)S(1)}, u32[]{:S(2)}, u32[]{:S(2)}) collective-permute-start(bf16[2,128,128]{2,1,0:T(8,128)(2,1)S(1)} %get-tuple-element.35), channel_id=1, source_target_pairs={{0,64},{32,96},{64,0},{96,32},{1,65},{33,97},{65,1},{97,33},{2,66}... | collective-permute-start | bytes 196616 | tf_op jit(solution)/shard_map/ppermute | solution.py:27
  159.7 5.7 %collective-permute-start.17 = (bf16[2,128,128]{2,1,0:T(8,128)(2,1)S(1)}, bf16[2,128,128]{2,1,0:T(8,128)(2,1)S(1)}, u32[]{:S(2)}, u32[]{:S(2)}) collective-permute-start(bf16[2,128,128]{2,1,0:T(8,128)(2,1)S(1)} %get-tuple-element.35), channel_id=1, source_target_pairs={{0,96},{32,0},{64,32},{96,64},{1,97},{33,1},{65,33},{97,65},{2,98}... | collective-permute-start | bytes 196616 | tf_op jit(solution)/shard_map/ppermute | solution.py:27
  167.8 13.0 %collective-permute-start.22 = (bf16[512,256]{1,0:T(8,128)(2,1)S(1)}, bf16[512,256]{1,0:T(8,128)(2,1)S(1)}, u32[]{:S(2)}, u32[]{:S(2)}) collective-permute-start(bf16[512,256]{1,0:T(8,128)(2,1)S(1)} %get-tuple-element.40), channel_id=1, source_target_pairs={{0,8},{8,16},{16,24},{24,0},{1,9},{9,17},{17,25},{25,1},{2,10},{10... | collective-permute-start | bytes 786440 | tf_op jit(solution)/shard_map/ppermute | solution.py:31
  168.7 12.1 %collective-permute-start.23 = (bf16[512,256]{1,0:T(8,128)(2,1)S(1)}, bf16[512,256]{1,0:T(8,128)(2,1)S(1)}, u32[]{:S(2)}, u32[]{:S(2)}) collective-permute-start(bf16[512,256]{1,0:T(8,128)(2,1)S(1)} %get-tuple-element.41), channel_id=1, source_target_pairs={{0,24},{8,0},{16,8},{24,16},{1,25},{9,1},{17,9},{25,17},{2,26},{10... | collective-permute-start | bytes 786440 | tf_op jit(solution)/shard_map/ppermute | solution.py:31
  171.1 6.1 %collective-permute-start.18 = (f32[2,8,256]{2,1,0:T(8,128)S(1)}, f32[2,8,256]{2,1,0:T(8,128)S(1)}, u32[]{:S(2)}, u32[]{:S(2)}) collective-permute-start(f32[2,8,256]{2,1,0:T(8,128)S(1)} %get-tuple-element.37), channel_id=1, source_target_pairs={{0,8},{8,16},{16,24},{24,0},{1,9},{9,17},{17,25},{25,1},{2,10},{10... | collective-permute-start | bytes 49160 | tf_op jit(solution)/shard_map/ppermute | solution.py:31
  171.1 7.3 %collective-permute-start.19 = (f32[2,8,256]{2,1,0:T(8,128)S(1)}, f32[2,8,256]{2,1,0:T(8,128)S(1)}, u32[]{:S(2)}, u32[]{:S(2)}) collective-permute-start(f32[2,8,256]{2,1,0:T(8,128)S(1)} %get-tuple-element.38), channel_id=1, source_target_pairs={{0,24},{8,0},{16,8},{24,16},{1,25},{9,1},{17,9},{25,17},{2,26},{10... | collective-permute-start | bytes 49160 | tf_op jit(solution)/shard_map/ppermute | solution.py:31
  174.3 5.2 %collective-permute-start.20 = (f32[2,8,256]{2,1,0:T(8,128)S(1)}, f32[2,8,256]{2,1,0:T(8,128)S(1)}, u32[]{:S(2)}, u32[]{:S(2)}) collective-permute-start(f32[2,8,256]{2,1,0:T(8,128)S(1)} %get-tuple-element.39), channel_id=1, source_target_pairs={{0,16},{8,24},{16,0},{24,8},{1,17},{9,25},{17,1},{25,9},{2,18},{10... | collective-permute-start | bytes 49160 | tf_op jit(solution)/shard_map/ppermute | solution.py:31
  177.2 14.5 %collective-permute-start.27 = (bf16[512,256]{1,0:T(8,128)(2,1)S(1)}, bf16[512,256]{1,0:T(8,128)(2,1)S(1)}, u32[]{:S(2)}, u32[]{:S(2)}) collective-permute-start(bf16[512,256]{1,0:T(8,128)(2,1)S(1)} %get-tuple-element.44), channel_id=1, source_target_pairs={{0,16},{8,24},{16,0},{24,8},{1,17},{9,25},{17,1},{25,9},{2,18},{10... | collective-permute-start | bytes 786440 | tf_op jit(solution)/shard_map/ppermute | solution.py:31
  179.6 1.2 collective-permute-start.21
  180.8 7.9 %collective-permute-start.24 = (f32[2,8,256]{2,1,0:T(8,128)S(1)}, f32[2,8,256]{2,1,0:T(8,128)S(1)}, u32[]{:S(2)}, u32[]{:S(2)}) collective-permute-start(f32[2,8,256]{2,1,0:T(8,128)S(1)} %add.198), channel_id=1, source_target_pairs={{0,2},{2,4},{4,6},{6,0},{1,3},{3,5},{5,7},{7,1},{8,10},{10,12},{12... | collective-permute-start | bytes 49160 | tf_op jit(solution)/shard_map/ppermute | solution.py:35
  185.1 3.7 %collective-permute-start.25 = (f32[2,8,256]{2,1,0:T(8,128)S(1)}, f32[2,8,256]{2,1,0:T(8,128)S(1)}, u32[]{:S(2)}, u32[]{:S(2)}) collective-permute-start(f32[2,8,256]{2,1,0:T(8,128)S(1)} %add.198), channel_id=1, source_target_pairs={{0,6},{2,0},{4,2},{6,4},{1,7},{3,1},{5,3},{7,5},{8,14},{10,8},{12,... | collective-permute-start | bytes 49160 | tf_op jit(solution)/shard_map/ppermute | solution.py:35
  186.4 5.2 %collective-permute-start.26 = (f32[2,8,256]{2,1,0:T(8,128)S(1)}, f32[2,8,256]{2,1,0:T(8,128)S(1)}, u32[]{:S(2)}, u32[]{:S(2)}) collective-permute-start(f32[2,8,256]{2,1,0:T(8,128)S(1)} %add.198), channel_id=1, source_target_pairs={{0,4},{2,6},{4,0},{6,2},{1,5},{3,7},{5,1},{7,3},{8,12},{10,14},{12... | collective-permute-start | bytes 49160 | tf_op jit(solution)/shard_map/ppermute | solution.py:35
  (16 other events, 248.7 us)
Sparse Core Ops, SparseCore 0:
  29.2 99.0 all-gather.1

commit v4 on v3

--- a/solution.py
+++ b/solution.py
@@ -117,28 +117,8 @@
         copy.wait()
 
 
-def project_others(place, x, w, own, out, wfull, sem):
-    depth = DEPTH // SIDE
-    step = pl.program_id(0)
-
-    @pl.when(step == 0)
-    def _():
-        tiles = [pl.ds(i * depth, depth) for i in range(SIDE)]
-        copies = [
-            pltpu.make_async_copy(w.at[t], wfull.at[t], sem.at[i]) for i, t in enumerate(tiles)
-        ]
-        for copy in copies:
-            copy.start()
-        total = None
-        for copy, t in zip(copies, tiles):
-            copy.wait()
-            part = jnp.dot(x[0, :, t], wfull[t, :], preferred_element_type=jnp.float32)
-            total = part if total is None else total + part
-        out[0] = silu(total)
-
-    @pl.when(step > 0)
-    def _():
-        out[0] = silu(jnp.dot(x[0], wfull[...], preferred_element_type=jnp.float32))
+def project_others(place, x, w, own, out):
+    out[0] = silu(jnp.dot(x[0], w[...], preferred_element_type=jnp.float32))
 
 
 def call_project(place, tokens, group, w):
@@ -185,14 +165,10 @@
             grid=(count * parts,),
             in_specs=[
                 pl.BlockSpec((1, BLOCK, DEPTH), there),
-                hbm,
+                pl.BlockSpec(whole, lambda i, place: (0, 0), pipeline_mode=pl.Buffered(1)),
                 hbm,
             ],
             out_specs=pl.BlockSpec((1, BLOCK, COLS), there),
-            scratch_shapes=[
-                pltpu.VMEM(whole, jnp.bfloat16),
-                pltpu.SemaphoreType.DMA((SIDE,)),
-            ],
         ),
         input_output_aliases={3: 0},
         cost_estimate=cost(count),
@@ -355,12 +331,11 @@
         name="decays",
     )(jnp.transpose(cum, (1, 0, 2)), cumc, doc[:, None], docc)
 
-    wview = w_qkv.reshape(WROWS, 3, SIDE, width)
     weights = []
     for d in range(SIDE):
         at = (z + d * (1 - 2 * c)) % SIDE
         weights.append(
-            lax.dynamic_slice(wview, (0, 0, at, 0), (WROWS, 3, 1, width)).reshape(WROWS, COLS)
+            lax.dynamic_slice(w_qkv, (0, 0, at * width), (WROWS, 3, width)).reshape(WROWS, COLS)
         )
     w, first = spread_weights(weights, (decay, kf, qf, suffix, passes, fac))
     mine = lax.dynamic_slice(tokens, ((2 * x + c) * 64, 0), (64, DEPTH))

time: 201 us -> 197 us (0.980)
  local copies, waits for them, and re-layouts: 20.1 us -> 16.6 us
    reshape x6, local copies, waits for them, and re-layouts: 4.88 us -> 2.74 us  [the longest x4 2.65 us: per_device(): lax.dynamic_slice(w_qkv, (0, 0, at * width), (WROWS, 3, width))]
    unnamed x41 -> x44, local copies, waits for them, and re-layouts: 8.15 us -> 6.33 us
  transfers between devices with their start and end apart: 29 -> 29, of which waited for: 17 -> 17; matrix products, arithmetic and copies ran while one was open for 6% -> 6% of each run, Pallas kernels for 9% -> 10%
where the time goes in v4:
time: 197 us; the launch traced here: 196 us
  waiting for transfers between devices  78.8 us (40%)
  Pallas kernels  47.4 us (24%)
  starting transfers between devices  36.7 us (19%)
  local copies, waits for them, and re-layouts  16.6 us (8%)
  between operations  13.8 us (7%)
  other arithmetic  3 us (2%)
    ppermute x15, waiting for transfers between devices, opposed(): return lax.ppermute(a, (axis, 'c'), perm)  70.5 us
    pallas_call x1, Pallas kernels, call_project(): pl.pallas_call(project_others, out_shape=shape, grid_spec=pltpu.PrefetchS...  22 us
    ppermute x15, starting transfers between devices, opposed(): return lax.ppermute(a, (axis, 'c'), perm)  16.9 us
    pallas_call x1, Pallas kernels, call_project(): pl.pallas_call(project_own, out_shape=(shape, jax.ShapeDtypeStruct(whole,...  12.7 us
    ppermute x3, starting transfers between devices, move_x(): return lax.ppermute(a, 'x', [(s, (s + d) % 4) for s in range(4)])  7.86 us
    ppermute x6, starting transfers between devices, move_z(): return lax.ppermute(a, 'z', [(s, (s + d) % 4) for s in range(4)])  7.7 us
    unnamed x44, local copies, waits for them, and re-layouts  6.33 us
    pallas_call x1, Pallas kernels, per_device(): pl.pallas_call(intras, out_shape=(jax.ShapeDtypeStruct((GROUP, width), jn...  4.25 us
  transfers between devices with their start and end apart: 29, of which 17 were waited for; matrix products, arithmetic and copies ran while one was open for 6% of the time, Pallas kernels for 10%

profile of v4, /device:TPU:0, one launch (start us, length us, event | category | flops | bytes accessed | tf_op | source)
XLA Modules:
  0.0 196.3 jit_solution(8840923544021393245)
XLA Ops:
  6.5 1.8 constant_dynamic-slice_fusion.6
  8.9 2.1 %collective-permute-start = (bf16[384,768]{1,0:T(8,128)(2,1)S(1)}, bf16[384,768]{1,0:T(8,128)(2,1)}, u32[]{:S(2)}, u32[]{:S(2)}) collective-permute-start(bf16[384,768]{1,0:T(8,128)(2,1)S(1)} %copy.58), channel_id=1, source_target_pairs={{0,8},{1,25},{8,16},{9,1},{16,24},{17,9},{24,0},{25,17},{2,10},{3,... | collective-permute-start | bytes 1769480 | tf_op jit(solution)/shard_map/ppermute | solution.py:44
  11.6 2.2 %collective-permute-start.1 = (bf16[384,768]{1,0:T(8,128)(2,1)S(1)}, bf16[384,768]{1,0:T(8,128)(2,1)S(1)}, u32[]{:S(2)}, u32[]{:S(2)}) collective-permute-start(bf16[384,768]{1,0:T(8,128)(2,1)S(1)} %copy.60), channel_id=1, source_target_pairs={{0,24},{1,9},{8,0},{9,17},{16,8},{17,25},{24,16},{25,1},{2,26},{3,... | collective-permute-start | bytes 1769480 | tf_op jit(solution)/shard_map/ppermute | solution.py:44
  13.8 2.1 %constant_dynamic-slice_fusion.10 = bf16[64,6144]{1,0:T(8,128)(2,1)} fusion(bf16[512,6144]{1,0:T(8,128)(2,1)} %x.3, s32[]{:T(128)S(6)} %select_n.133), kind=kLoop, calls=%fused_computation.27 | loop fusion | bytes 1572868 | tf_op jit(solution)/shard_map/dynamic_slice | solution.py:341
  15.9 9.0 %collective-permute-done.refs_4_ = bf16[384,768]{1,0:T(8,128)(2,1)} collective-permute-done((bf16[384,768]{1,0:T(8,128)(2,1)S(1)}, bf16[384,768]{1,0:T(8,128)(2,1)}, u32[]{:S(2)}, u32[]{:S(2)}) %collective-permute-start) | collective-permute-done | bytes 589856 | tf_op jit(solution)/shard_map/ppermute | solution.py:44
  30.1 3.1 %collective-permute-start.8 = (bf16[384,768]{1,0:T(8,128)(2,1)}, bf16[384,768]{1,0:T(8,128)(2,1)}, u32[]{:S(2)}, u32[]{:S(2)}) collective-permute-start(bf16[384,768]{1,0:T(8,128)(2,1)} %copy.64), channel_id=1, source_target_pairs={{0,16},{1,17},{8,24},{9,25},{16,0},{17,1},{24,8},{25,9},{2,18},{3,... | collective-permute-start | bytes 1769480 | tf_op jit(solution)/shard_map/ppermute | solution.py:44
  42.4 1.7 decays.1.decay
  44.1 2.0 %copy-done.3 = f32[8,2,256,256]{3,2,1,0:T(8,128)} copy-done((f32[8,2,256,256]{3,2,1,0:T(8,128)}, f32[8,2,256,256]{3,2,1,0:T(8,128)S(1)}, u32[]{:S(2)}) %copy-start.3) | copy-done | bytes 4194328
  46.1 4.3 %collective-permute-done.3.refs_2_ = bf16[384,768]{1,0:T(8,128)(2,1)} collective-permute-done((bf16[384,768]{1,0:T(8,128)(2,1)}, bf16[384,768]{1,0:T(8,128)(2,1)}, u32[]{:S(2)}, u32[]{:S(2)}) %collective-permute-start.3) | collective-permute-done | bytes 589856 | tf_op jit(solution)/shard_map/ppermute | solution.py:44
  50.7 6.0 %collective-permute-done.5.refs_5_ = bf16[384,768]{1,0:T(8,128)(2,1)} collective-permute-done((bf16[384,768]{1,0:T(8,128)(2,1)}, bf16[384,768]{1,0:T(8,128)(2,1)}, u32[]{:S(2)}, u32[]{:S(2)}) %collective-permute-start.5) | collective-permute-done | bytes 589856 | tf_op jit(solution)/shard_map/ppermute | solution.py:44
  58.6 4.3 %collective-permute-done.4.refs_3_ = bf16[384,768]{1,0:T(8,128)(2,1)S(1)} collective-permute-done((bf16[384,768]{1,0:T(8,128)(2,1)}, bf16[384,768]{1,0:T(8,128)(2,1)S(1)}, u32[]{:S(2)}, u32[]{:S(2)}) %collective-permute-start.4) | collective-permute-done | bytes 589856 | tf_op jit(solution)/shard_map/ppermute | solution.py:44
  62.9 6.3 %collective-permute-done.6.refs_6_ = bf16[384,768]{1,0:T(8,128)(2,1)S(1)} collective-permute-done((bf16[384,768]{1,0:T(8,128)(2,1)}, bf16[384,768]{1,0:T(8,128)(2,1)S(1)}, u32[]{:S(2)}, u32[]{:S(2)}) %collective-permute-start.6) | collective-permute-done | bytes 589856 | tf_op jit(solution)/shard_map/ppermute | solution.py:44
  69.6 6.0 %collective-permute-done.12.refs_13_ = bf16[384,768]{1,0:T(8,128)(2,1)S(1)} collective-permute-done((bf16[384,768]{1,0:T(8,128)(2,1)S(1)}, bf16[384,768]{1,0:T(8,128)(2,1)S(1)}, u32[]{:S(2)}, u32[]{:S(2)}) %collective-permute-start.12) | collective-permute-done | bytes 589856 | tf_op jit(solution)/shard_map/ppermute | solution.py:44
  75.9 6.0 %collective-permute-done.9.refs_9_ = bf16[384,768]{1,0:T(8,128)(2,1)S(1)} collective-permute-done((bf16[384,768]{1,0:T(8,128)(2,1)}, bf16[384,768]{1,0:T(8,128)(2,1)S(1)}, u32[]{:S(2)}, u32[]{:S(2)}) %collective-permute-start.9) | collective-permute-done | bytes 589856 | tf_op jit(solution)/shard_map/ppermute | solution.py:44
  83.5 4.7 %collective-permute-done.13.refs_14_ = bf16[384,768]{1,0:T(8,128)(2,1)S(1)} collective-permute-done((bf16[384,768]{1,0:T(8,128)(2,1)S(1)}, bf16[384,768]{1,0:T(8,128)(2,1)S(1)}, u32[]{:S(2)}, u32[]{:S(2)}) %collective-permute-start.13) | collective-permute-done | bytes 589856 | tf_op jit(solution)/shard_map/ppermute | solution.py:44
  88.5 6.0 %collective-permute-done.10.refs_10_ = bf16[384,768]{1,0:T(8,128)(2,1)S(1)} collective-permute-done((bf16[384,768]{1,0:T(8,128)(2,1)S(1)}, bf16[384,768]{1,0:T(8,128)(2,1)S(1)}, u32[]{:S(2)}, u32[]{:S(2)}) %collective-permute-start.10) | collective-permute-done | bytes 589856 | tf_op jit(solution)/shard_map/ppermute | solution.py:44
  95.4 11.7 %collective-permute-done.14.refs_15_ = bf16[384,768]{1,0:T(8,128)(2,1)S(1)} collective-permute-done((bf16[384,768]{1,0:T(8,128)(2,1)S(1)}, bf16[384,768]{1,0:T(8,128)(2,1)S(1)}, u32[]{:S(2)}, u32[]{:S(2)}) %collective-permute-start.14) | collective-permute-done | bytes 589856 | tf_op jit(solution)/shard_map/ppermute | solution.py:44
  107.9 5.6 %collective-permute-done.11.refs_11_ = bf16[384,768]{1,0:T(8,128)(2,1)} collective-permute-done((bf16[384,768]{1,0:T(8,128)(2,1)S(1)}, bf16[384,768]{1,0:T(8,128)(2,1)}, u32[]{:S(2)}, u32[]{:S(2)}) %collective-permute-start.11) | collective-permute-done | bytes 589856 | tf_op jit(solution)/shard_map/ppermute | solution.py:44
  113.6 12.7 %project_own.1 = (bf16[4,512,768]{2,1,0:T(8,128)(2,1)}, bf16[6144,768]{1,0:T(8,128)(2,1)}) custom-call(s32[4]{0:T(128)} %pad_add_fusion.place, bf16[512,6144]{1,0:T(8,128)(2,1)} %x.3, bf16[384,768]{1,0:T(8,128)(2,1)} %copy.75.refs_0_, bf16[384,768]{1,0:T(8,128)(2,1)} %collective-permute-done.2.refs_1_, bf16[384,768]{1,0:T(8,128)(2,1)} %collective-permute-done.3.refs_2_, ...), custom_call_target="tpu_custom_call" | custom-call | flops 4831838208 | bytes 17825792 | tf_op jit(solution)/shard_map/project_own/pallas_call | solution.py:137
  126.4 22.0 %project_others.1 = bf16[4,512,768]{2,1,0:T(8,128)(2,1)} custom-call(s32[4]{0:T(128)} %pad_add_fusion.place, bf16[4,512,6144]{2,1,0:T(8,128)(2,1)} %bitcast.53, bf16[6144,768]{1,0:T(8,128)(2,1)} %get-tuple-element.30.w, bf16[4,512,768]{2,1,0:T(8,128)(2,1)} %get-tuple-element.31.own), custom_call_target="tpu_custom_call", output_to_operand_aliasing={{}: (3, {})} | custom-call | flops 14495514624 | bytes 32505856 | tf_op jit(solution)/shard_map/project_others/pallas_call | solution.py:160
  148.4 1.9 copy-done.2
  150.3 2.4 %states.1 = (f32[8,2,128,128]{3,2,1,0:T(8,128)S(1)}, bf16[2,128,128]{2,1,0:T(8,128)(2,1)S(1)}) custom-call(bf16[2048,768]{1,0:T(8,128)(2,1)S(1)} %bitcast.36, bf16[2048,768]{1,0:T(8,128)(2,1)S(1)} %bitcast.37, f32[2048,2]{1,0:T(8,128)S(1)} %bitcast.39, f32[2,8]{1,0:T(2,128)S(1)} %concatenate.3.suffix), custom_call_target="tpu_custom_call" | custom-call | flops 134217728 | bytes 4194304 | tf_op jit(solution)/shard_map/states/pallas_call | solution.py:347
  152.9 2.6 %collective-permute-start.16 = (bf16[2,128,128]{2,1,0:T(8,128)(2,1)S(1)}, bf16[2,128,128]{2,1,0:T(8,128)(2,1)S(1)}, u32[]{:S(2)}, u32[]{:S(2)}) collective-permute-start(bf16[2,128,128]{2,1,0:T(8,128)(2,1)S(1)} %get-tuple-element.35), channel_id=1, source_target_pairs={{0,64},{32,96},{64,0},{96,32},{1,65},{33,97},{65,1},{97,33},{2,66}... | collective-permute-start | bytes 196616 | tf_op jit(solution)/shard_map/ppermute | solution.py:27
  157.0 4.2 %intras.1 = (bf16[2048,256]{1,0:T(8,128)(2,1)S(1)}, f32[2048,256]{1,0:T(8,128)S(1)}) custom-call(bf16[2048,768]{1,0:T(8,128)(2,1)S(1)} %bitcast.38, f32[8,2,256,256]{3,2,1,0:T(8,128)S(1)} %copy-done.4, f32[2048,2]{1,0:T(8,128)S(1)} %bitcast.42), custom_call_target="tpu_custom_call" | custom-call | flops 1073741824 | bytes 8388608 | tf_op jit(solution)/shard_map/intras/pallas_call | solution.py:370
  161.3 2.2 %inters.1 = (bf16[512,256]{1,0:T(8,128)(2,1)S(1)}, bf16[512,256]{1,0:T(8,128)(2,1)S(1)}, bf16[512,256]{1,0:T(8,128)(2,1)S(1)}, bf16[512,256]{1,0:T(8,128)(2,1)S(...) custom-call(s32[4]{0:T(128)S(1)} %copy-done.6, ...), custom_call_target="tpu_custom_call" | custom-call | flops 268435456 | bytes 6291456 | tf_op jit(solution)/shard_map/inters/pallas_call | solution.py:387
  165.1 1.8 collective-permute-start.23
  167.1 3.0 %collective-permute-start.19 = (f32[2,8,256]{2,1,0:T(8,128)S(1)}, f32[2,8,256]{2,1,0:T(8,128)S(1)}, u32[]{:S(2)}, u32[]{:S(2)}) collective-permute-start(f32[2,8,256]{2,1,0:T(8,128)S(1)} %get-tuple-element.38), channel_id=1, source_target_pairs={{0,24},{8,0},{16,8},{24,16},{1,25},{9,1},{17,9},{25,17},{2,26},{10... | collective-permute-start | bytes 49160 | tf_op jit(solution)/shard_map/ppermute | solution.py:31
  170.1 2.9 %collective-permute-done.18 = f32[2,8,256]{2,1,0:T(8,128)S(1)} collective-permute-done((f32[2,8,256]{2,1,0:T(8,128)S(1)}, f32[2,8,256]{2,1,0:T(8,128)S(1)}, u32[]{:S(2)}, u32[]{:S(2)}) %collective-permute-start.18) | collective-permute-done | bytes 16416 | tf_op jit(solution)/shard_map/ppermute | solution.py:31
  176.5 4.3 %collective-permute-start.24 = (f32[2,8,256]{2,1,0:T(8,128)S(1)}, f32[2,8,256]{2,1,0:T(8,128)S(1)}, u32[]{:S(2)}, u32[]{:S(2)}) collective-permute-start(f32[2,8,256]{2,1,0:T(8,128)S(1)} %add.198), channel_id=1, source_target_pairs={{0,2},{2,4},{4,6},{6,0},{1,3},{3,5},{5,7},{7,1},{8,10},{10,12},{12... | collective-permute-start | bytes 49160 | tf_op jit(solution)/shard_map/ppermute | solution.py:35
  182.2 2.2 %collective-permute-start.26 = (f32[2,8,256]{2,1,0:T(8,128)S(1)}, f32[2,8,256]{2,1,0:T(8,128)S(1)}, u32[]{:S(2)}, u32[]{:S(2)}) collective-permute-start(f32[2,8,256]{2,1,0:T(8,128)S(1)} %add.198), channel_id=1, source_target_pairs={{0,4},{2,6},{4,0},{6,2},{1,5},{3,7},{5,1},{7,3},{8,12},{10,14},{12... | collective-permute-start | bytes 49160 | tf_op jit(solution)/shard_map/ppermute | solution.py:35
  184.6 2.8 %collective-permute-done.26 = f32[2,8,256]{2,1,0:T(8,128)S(1)} collective-permute-done((f32[2,8,256]{2,1,0:T(8,128)S(1)}, f32[2,8,256]{2,1,0:T(8,128)S(1)}, u32[]{:S(2)}, u32[]{:S(2)}) %collective-permute-start.26) | collective-permute-done | bytes 16416 | tf_op jit(solution)/shard_map/ppermute | solution.py:35
  187.4 2.0 %finish.1 = bf16[512,1024]{1,0:T(8,128)(2,1)} custom-call(s32[4]{0:T(128)S(1)} %copy-done.6, f32[2,8,256]{2,1,0:T(8,128)S(1)} %add_add_fusion.total, f32[1,1024]{1,0:T(1,128)S(1)} %bitcast.44, bf16[512,256]{1,0:T(8,128)(2,1)S(1)} %get-tuple-element.43.p0, bf16[512,256]{1,0:T(8,128)(2,1)S(1)} %collective-permute-done.22.p1, ...), custom_call_target="tpu_custom_call" | custom-call | flops 4194304 | bytes 3145728 | tf_op jit(solution)/shard_map/finish/pallas_call | solution.py:411
  (136 shorter events, 30.8 us)
Async XLA Ops:
  6.5 119.8 %all-gather.2.cloned.1.call-start = ((), (), s32[]{:S(2)}) async-start(), calls=%async_computation | async-start | bytes 25952256 | tf_op jit(solution)/shard_map/all_gather | solution.py:343
  8.9 15.9 %collective-permute-start = (bf16[384,768]{1,0:T(8,128)(2,1)S(1)}, bf16[384,768]{1,0:T(8,128)(2,1)}, u32[]{:S(2)}, u32[]{:S(2)}) collective-permute-start(bf16[384,768]{1,0:T(8,128)(2,1)S(1)} %copy.58), channel_id=1, source_target_pairs={{0,8},{1,25},{8,16},{9,1},{16,24},{17,9},{24,0},{25,17},{2,10},{3,... | collective-permute-start | bytes 1769480 | tf_op jit(solution)/shard_map/ppermute | solution.py:44
  11.6 14.1 %collective-permute-start.1 = (bf16[384,768]{1,0:T(8,128)(2,1)S(1)}, bf16[384,768]{1,0:T(8,128)(2,1)S(1)}, u32[]{:S(2)}, u32[]{:S(2)}) collective-permute-start(bf16[384,768]{1,0:T(8,128)(2,1)S(1)} %copy.60), channel_id=1, source_target_pairs={{0,24},{1,9},{8,0},{9,17},{16,8},{17,25},{24,16},{25,1},{2,26},{3,... | collective-permute-start | bytes 1769480 | tf_op jit(solution)/shard_map/ppermute | solution.py:44
  27.1 11.8 %collective-permute-start.2 = (bf16[384,768]{1,0:T(8,128)(2,1)}, bf16[384,768]{1,0:T(8,128)(2,1)}, u32[]{:S(2)}, u32[]{:S(2)}) collective-permute-start(bf16[384,768]{1,0:T(8,128)(2,1)} %copy.75.refs_0_), channel_id=1, source_target_pairs={{0,32},{1,97},{32,64},{33,1},{64,96},{65,33},{96,0},{97,65},{2,34}... | collective-permute-start | bytes 1769480 | tf_op jit(solution)/shard_map/ppermute | solution.py:44
  30.1 28.5 %collective-permute-start.8 = (bf16[384,768]{1,0:T(8,128)(2,1)}, bf16[384,768]{1,0:T(8,128)(2,1)}, u32[]{:S(2)}, u32[]{:S(2)}) collective-permute-start(bf16[384,768]{1,0:T(8,128)(2,1)} %copy.64), channel_id=1, source_target_pairs={{0,16},{1,17},{8,24},{9,25},{16,0},{17,1},{24,8},{25,9},{2,18},{3,... | collective-permute-start | bytes 1769480 | tf_op jit(solution)/shard_map/ppermute | solution.py:44
  38.9 11.4 %collective-permute-start.3 = (bf16[384,768]{1,0:T(8,128)(2,1)}, bf16[384,768]{1,0:T(8,128)(2,1)}, u32[]{:S(2)}, u32[]{:S(2)}) collective-permute-start(bf16[384,768]{1,0:T(8,128)(2,1)} %collective-permute-done.2.refs_1_), channel_id=1, source_target_pairs={{0,32},{1,97},{32,64},{33,1},{64,96},{65,33},{96,0},{97,65},{2,34}... | collective-permute-start | bytes 1769480 | tf_op jit(solution)/shard_map/ppermute | solution.py:44
  40.5 16.2 %collective-permute-start.5 = (bf16[384,768]{1,0:T(8,128)(2,1)}, bf16[384,768]{1,0:T(8,128)(2,1)}, u32[]{:S(2)}, u32[]{:S(2)}) collective-permute-start(bf16[384,768]{1,0:T(8,128)(2,1)} %collective-permute-done.refs_4_), channel_id=1, source_target_pairs={{0,32},{1,97},{32,64},{33,1},{64,96},{65,33},{96,0},{97,65},{2,34}... | collective-permute-start | bytes 1769480 | tf_op jit(solution)/shard_map/ppermute | solution.py:44
  50.3 12.5 %collective-permute-start.4 = (bf16[384,768]{1,0:T(8,128)(2,1)}, bf16[384,768]{1,0:T(8,128)(2,1)S(1)}, u32[]{:S(2)}, u32[]{:S(2)}) collective-permute-start(bf16[384,768]{1,0:T(8,128)(2,1)} %collective-permute-done.3.refs_2_), channel_id=1, source_target_pairs={{0,32},{1,97},{32,64},{33,1},{64,96},{65,33},{96,0},{97,65},{2,34}... | collective-permute-start | bytes 1769480 | tf_op jit(solution)/shard_map/ppermute | solution.py:44
  56.7 12.5 %collective-permute-start.6 = (bf16[384,768]{1,0:T(8,128)(2,1)}, bf16[384,768]{1,0:T(8,128)(2,1)S(1)}, u32[]{:S(2)}, u32[]{:S(2)}) collective-permute-start(bf16[384,768]{1,0:T(8,128)(2,1)} %collective-permute-done.5.refs_5_), channel_id=1, source_target_pairs={{0,32},{1,97},{32,64},{33,1},{64,96},{65,33},{96,0},{97,65},{2,34}... | collective-permute-start | bytes 1769480 | tf_op jit(solution)/shard_map/ppermute | solution.py:44
  57.3 18.2 %collective-permute-start.12 = (bf16[384,768]{1,0:T(8,128)(2,1)S(1)}, bf16[384,768]{1,0:T(8,128)(2,1)S(1)}, u32[]{:S(2)}, u32[]{:S(2)}) collective-permute-start(bf16[384,768]{1,0:T(8,128)(2,1)S(1)} %copy-done.9), channel_id=1, source_target_pairs={{0,32},{1,97},{32,64},{33,1},{64,96},{65,33},{96,0},{97,65},{2,34}... | collective-permute-start | bytes 1769480 | tf_op jit(solution)/shard_map/ppermute | solution.py:44
  62.9 50.7 %copy-start.10 = (bf16[384,768]{1,0:T(8,128)(2,1)}, bf16[384,768]{1,0:T(8,128)(2,1)S(1)}, u32[]{:S(2)}) copy-start(bf16[384,768]{1,0:T(8,128)(2,1)S(1)} %collective-permute-done.4.refs_3_) | copy-start | bytes 1769476
  69.2 44.3 %copy-start.11 = (bf16[384,768]{1,0:T(8,128)(2,1)}, bf16[384,768]{1,0:T(8,128)(2,1)S(1)}, u32[]{:S(2)}) copy-start(bf16[384,768]{1,0:T(8,128)(2,1)S(1)} %collective-permute-done.6.refs_6_) | copy-start | bytes 1769476
  69.2 12.6 %collective-permute-start.9 = (bf16[384,768]{1,0:T(8,128)(2,1)}, bf16[384,768]{1,0:T(8,128)(2,1)S(1)}, u32[]{:S(2)}, u32[]{:S(2)}) collective-permute-start(bf16[384,768]{1,0:T(8,128)(2,1)} %collective-permute-done.8.refs_8_), channel_id=1, source_target_pairs={{0,32},{1,97},{32,64},{33,1},{64,96},{65,33},{96,0},{97,65},{2,34}... | collective-permute-start | bytes 1769480 | tf_op jit(solution)/shard_map/ppermute | solution.py:44
  75.5 38.0 %copy-start.12 = (bf16[384,768]{1,0:T(8,128)(2,1)}, bf16[384,768]{1,0:T(8,128)(2,1)S(1)}, u32[]{:S(2)}) copy-start(bf16[384,768]{1,0:T(8,128)(2,1)S(1)} %collective-permute-done.12.refs_13_) | copy-start | bytes 1769476
  75.5 12.6 %collective-permute-start.13 = (bf16[384,768]{1,0:T(8,128)(2,1)S(1)}, bf16[384,768]{1,0:T(8,128)(2,1)S(1)}, u32[]{:S(2)}, u32[]{:S(2)}) collective-permute-start(bf16[384,768]{1,0:T(8,128)(2,1)S(1)} %collective-permute-done.12.refs_13_), channel_id=1, source_target_pairs={{0,32},{1,97},{32,64},{33,1},{64,96},{65,33},{96,0},{97,65},{2,34}... | collective-permute-start | bytes 1769480 | tf_op jit(solution)/shard_map/ppermute | solution.py:44
  81.8 12.6 %collective-permute-start.10 = (bf16[384,768]{1,0:T(8,128)(2,1)S(1)}, bf16[384,768]{1,0:T(8,128)(2,1)S(1)}, u32[]{:S(2)}, u32[]{:S(2)}) collective-permute-start(bf16[384,768]{1,0:T(8,128)(2,1)S(1)} %collective-permute-done.9.refs_9_), channel_id=1, source_target_pairs={{0,32},{1,97},{32,64},{33,1},{64,96},{65,33},{96,0},{97,65},{2,34}... | collective-permute-start | bytes 1769480 | tf_op jit(solution)/shard_map/ppermute | solution.py:44
  82.2 24.9 %collective-permute-start.7 = (bf16[384,768]{1,0:T(8,128)(2,1)S(1)}, bf16[384,768]{1,0:T(8,128)(2,1)S(1)}, u32[]{:S(2)}, u32[]{:S(2)}) collective-permute-start(bf16[384,768]{1,0:T(8,128)(2,1)S(1)} %collective-permute-done.6.refs_6_), channel_id=1, source_target_pairs={{0,32},{1,97},{32,64},{33,1},{64,96},{65,33},{96,0},{97,65},{2,34}... | collective-permute-start | bytes 1769480 | tf_op jit(solution)/shard_map/ppermute | solution.py:44
  88.1 19.0 %collective-permute-start.14 = (bf16[384,768]{1,0:T(8,128)(2,1)S(1)}, bf16[384,768]{1,0:T(8,128)(2,1)S(1)}, u32[]{:S(2)}, u32[]{:S(2)}) collective-permute-start(bf16[384,768]{1,0:T(8,128)(2,1)S(1)} %collective-permute-done.13.refs_14_), channel_id=1, source_target_pairs={{0,32},{1,97},{32,64},{33,1},{64,96},{65,33},{96,0},{97,65},{2,34}... | collective-permute-start | bytes 1769480 | tf_op jit(solution)/shard_map/ppermute | solution.py:44
  94.5 19.1 %collective-permute-start.11 = (bf16[384,768]{1,0:T(8,128)(2,1)S(1)}, bf16[384,768]{1,0:T(8,128)(2,1)}, u32[]{:S(2)}, u32[]{:S(2)}) collective-permute-start(bf16[384,768]{1,0:T(8,128)(2,1)S(1)} %collective-permute-done.10.refs_10_), channel_id=1, source_target_pairs={{0,32},{1,97},{32,64},{33,1},{64,96},{65,33},{96,0},{97,65},{2,34}... | collective-permute-start | bytes 1769480 | tf_op jit(solution)/shard_map/ppermute | solution.py:44
  152.7 8.5 %collective-permute-start.15 = (bf16[2,128,128]{2,1,0:T(8,128)(2,1)S(1)}, bf16[2,128,128]{2,1,0:T(8,128)(2,1)S(1)}, u32[]{:S(2)}, u32[]{:S(2)}) collective-permute-start(bf16[2,128,128]{2,1,0:T(8,128)(2,1)S(1)} %get-tuple-element.35), channel_id=1, source_target_pairs={{0,32},{32,64},{64,96},{96,0},{1,33},{33,65},{65,97},{97,1},{2,34}... | collective-permute-start | bytes 196616 | tf_op jit(solution)/shard_map/ppermute | solution.py:27
  152.9 8.3 %collective-permute-start.16 = (bf16[2,128,128]{2,1,0:T(8,128)(2,1)S(1)}, bf16[2,128,128]{2,1,0:T(8,128)(2,1)S(1)}, u32[]{:S(2)}, u32[]{:S(2)}) collective-permute-start(bf16[2,128,128]{2,1,0:T(8,128)(2,1)S(1)} %get-tuple-element.35), channel_id=1, source_target_pairs={{0,64},{32,96},{64,0},{96,32},{1,65},{33,97},{65,1},{97,33},{2,66}... | collective-permute-start | bytes 196616 | tf_op jit(solution)/shard_map/ppermute | solution.py:27
  155.5 5.7 %collective-permute-start.17 = (bf16[2,128,128]{2,1,0:T(8,128)(2,1)S(1)}, bf16[2,128,128]{2,1,0:T(8,128)(2,1)S(1)}, u32[]{:S(2)}, u32[]{:S(2)}) collective-permute-start(bf16[2,128,128]{2,1,0:T(8,128)(2,1)S(1)} %get-tuple-element.35), channel_id=1, source_target_pairs={{0,96},{32,0},{64,32},{96,64},{1,97},{33,1},{65,33},{97,65},{2,98}... | collective-permute-start | bytes 196616 | tf_op jit(solution)/shard_map/ppermute | solution.py:27
  163.5 13.0 %collective-permute-start.22 = (bf16[512,256]{1,0:T(8,128)(2,1)S(1)}, bf16[512,256]{1,0:T(8,128)(2,1)S(1)}, u32[]{:S(2)}, u32[]{:S(2)}) collective-permute-start(bf16[512,256]{1,0:T(8,128)(2,1)S(1)} %get-tuple-element.40), channel_id=1, source_target_pairs={{0,8},{8,16},{16,24},{24,0},{1,9},{9,17},{17,25},{25,1},{2,10},{10... | collective-permute-start | bytes 786440 | tf_op jit(solution)/shard_map/ppermute | solution.py:31
  165.1 11.4 %collective-permute-start.23 = (bf16[512,256]{1,0:T(8,128)(2,1)S(1)}, bf16[512,256]{1,0:T(8,128)(2,1)S(1)}, u32[]{:S(2)}, u32[]{:S(2)}) collective-permute-start(bf16[512,256]{1,0:T(8,128)(2,1)S(1)} %get-tuple-element.41), channel_id=1, source_target_pairs={{0,24},{8,0},{16,8},{24,16},{1,25},{9,1},{17,9},{25,17},{2,26},{10... | collective-permute-start | bytes 786440 | tf_op jit(solution)/shard_map/ppermute | solution.py:31
  166.8 6.1 %collective-permute-start.18 = (f32[2,8,256]{2,1,0:T(8,128)S(1)}, f32[2,8,256]{2,1,0:T(8,128)S(1)}, u32[]{:S(2)}, u32[]{:S(2)}) collective-permute-start(f32[2,8,256]{2,1,0:T(8,128)S(1)} %get-tuple-element.37), channel_id=1, source_target_pairs={{0,8},{8,16},{16,24},{24,0},{1,9},{9,17},{17,25},{25,1},{2,10},{10... | collective-permute-start | bytes 49160 | tf_op jit(solution)/shard_map/ppermute | solution.py:31
  167.1 7.0 %collective-permute-start.19 = (f32[2,8,256]{2,1,0:T(8,128)S(1)}, f32[2,8,256]{2,1,0:T(8,128)S(1)}, u32[]{:S(2)}, u32[]{:S(2)}) collective-permute-start(f32[2,8,256]{2,1,0:T(8,128)S(1)} %get-tuple-element.38), channel_id=1, source_target_pairs={{0,24},{8,0},{16,8},{24,16},{1,25},{9,1},{17,9},{25,17},{2,26},{10... | collective-permute-start | bytes 49160 | tf_op jit(solution)/shard_map/ppermute | solution.py:31
  170.1 5.2 %collective-permute-start.20 = (f32[2,8,256]{2,1,0:T(8,128)S(1)}, f32[2,8,256]{2,1,0:T(8,128)S(1)}, u32[]{:S(2)}, u32[]{:S(2)}) collective-permute-start(f32[2,8,256]{2,1,0:T(8,128)S(1)} %get-tuple-element.39), channel_id=1, source_target_pairs={{0,16},{8,24},{16,0},{24,8},{1,17},{9,25},{17,1},{25,9},{2,18},{10... | collective-permute-start | bytes 49160 | tf_op jit(solution)/shard_map/ppermute | solution.py:31
  173.0 14.5 %collective-permute-start.27 = (bf16[512,256]{1,0:T(8,128)(2,1)S(1)}, bf16[512,256]{1,0:T(8,128)(2,1)S(1)}, u32[]{:S(2)}, u32[]{:S(2)}) collective-permute-start(bf16[512,256]{1,0:T(8,128)(2,1)S(1)} %get-tuple-element.44), channel_id=1, source_target_pairs={{0,16},{8,24},{16,0},{24,8},{1,17},{9,25},{17,1},{25,9},{2,18},{10... | collective-permute-start | bytes 786440 | tf_op jit(solution)/shard_map/ppermute | solution.py:31
  175.3 1.2 collective-permute-start.21
  176.5 7.9 %collective-permute-start.24 = (f32[2,8,256]{2,1,0:T(8,128)S(1)}, f32[2,8,256]{2,1,0:T(8,128)S(1)}, u32[]{:S(2)}, u32[]{:S(2)}) collective-permute-start(f32[2,8,256]{2,1,0:T(8,128)S(1)} %add.198), channel_id=1, source_target_pairs={{0,2},{2,4},{4,6},{6,0},{1,3},{3,5},{5,7},{7,1},{8,10},{10,12},{12... | collective-permute-start | bytes 49160 | tf_op jit(solution)/shard_map/ppermute | solution.py:35
  180.8 3.7 %collective-permute-start.25 = (f32[2,8,256]{2,1,0:T(8,128)S(1)}, f32[2,8,256]{2,1,0:T(8,128)S(1)}, u32[]{:S(2)}, u32[]{:S(2)}) collective-permute-start(f32[2,8,256]{2,1,0:T(8,128)S(1)} %add.198), channel_id=1, source_target_pairs={{0,6},{2,0},{4,2},{6,4},{1,7},{3,1},{5,3},{7,5},{8,14},{10,8},{12,... | collective-permute-start | bytes 49160 | tf_op jit(solution)/shard_map/ppermute | solution.py:35
  182.2 5.2 %collective-permute-start.26 = (f32[2,8,256]{2,1,0:T(8,128)S(1)}, f32[2,8,256]{2,1,0:T(8,128)S(1)}, u32[]{:S(2)}, u32[]{:S(2)}) collective-permute-start(f32[2,8,256]{2,1,0:T(8,128)S(1)} %add.198), channel_id=1, source_target_pairs={{0,4},{2,6},{4,0},{6,2},{1,5},{3,7},{5,1},{7,3},{8,12},{10,14},{12... | collective-permute-start | bytes 49160 | tf_op jit(solution)/shard_map/ppermute | solution.py:35
  (16 other events, 241.5 us)
Sparse Core Ops, SparseCore 0:
  25.9 98.9 all-gather.1

commit v5 on v4

--- a/solution.py
+++ b/solution.py
@@ -24,7 +24,7 @@
 
 
 def move_y(a, d):
-    return lax.ppermute(a, "y", [(s, (s + d) % 4) for s in range(4)])
+    return lax.ppermute(a, "y", [(s, s + d) for s in range(SIDE - d)])
 
 
 def move_z(a, d):

time: 197 us -> 200 us (1.015)
    ppermute x3, starting transfers between devices: 4.22 us -> 7.82 us  [move_y(): return lax.ppermute(a, 'y', [(s, s + d) for s in range(SIDE - d)])]
    ppermute x3, starting transfers between devices: 7.86 us -> 5.07 us  [move_x(): return lax.ppermute(a, 'x', [(s, (s + d) % 4) for s in range(4)])]
  transfers between devices with their start and end apart: 29 -> 29, of which waited for: 17 -> 17; matrix products, arithmetic and copies ran while one was open for 6% -> 6% of each run, Pallas kernels for 10% -> 9%
where the time goes in v5:
time: 200 us; the launch traced here: 198 us
  waiting for transfers between devices  80.1 us (40%)
  Pallas kernels  47.4 us (24%)
  starting transfers between devices  36.7 us (18%)
  local copies, waits for them, and re-layouts  16.6 us (8%)
  between operations  13.8 us (7%)
  other arithmetic  3 us (2%)
    ppermute x15, waiting for transfers between devices, opposed(): return lax.ppermute(a, (axis, 'c'), perm)  70.5 us
    pallas_call x1, Pallas kernels, call_project(): pl.pallas_call(project_others, out_shape=shape, grid_spec=pltpu.PrefetchS...  22 us
    ppermute x15, starting transfers between devices, opposed(): return lax.ppermute(a, (axis, 'c'), perm)  16.9 us
    pallas_call x1, Pallas kernels, call_project(): pl.pallas_call(project_own, out_shape=(shape, jax.ShapeDtypeStruct(whole,...  12.7 us
    ppermute x3, starting transfers between devices, move_y(): return lax.ppermute(a, 'y', [(s, s + d) for s in range(SIDE - d)])  7.82 us
    ppermute x6, starting transfers between devices, move_z(): return lax.ppermute(a, 'z', [(s, (s + d) % 4) for s in range(4)])  6.88 us
    unnamed x44, local copies, waits for them, and re-layouts  6.33 us
    ppermute x3, starting transfers between devices, move_x(): return lax.ppermute(a, 'x', [(s, (s + d) % 4) for s in range(4)])  5.07 us
  transfers between devices with their start and end apart: 29, of which 17 were waited for; matrix products, arithmetic and copies ran while one was open for 6% of the time, Pallas kernels for 9%

profile of v5, /device:TPU:0, one launch (start us, length us, event | category | flops | bytes accessed | tf_op | source)
XLA Modules:
  0.0 197.6 jit_solution(14270968485021580872)
XLA Ops:
  6.5 1.8 constant_dynamic-slice_fusion.6
  8.9 2.1 %collective-permute-start = (bf16[384,768]{1,0:T(8,128)(2,1)S(1)}, bf16[384,768]{1,0:T(8,128)(2,1)}, u32[]{:S(2)}, u32[]{:S(2)}) collective-permute-start(bf16[384,768]{1,0:T(8,128)(2,1)S(1)} %copy.58), channel_id=1, source_target_pairs={{0,8},{1,25},{8,16},{9,1},{16,24},{17,9},{24,0},{25,17},{2,10},{3,... | collective-permute-start | bytes 1769480 | tf_op jit(solution)/shard_map/ppermute | solution.py:44
  11.6 2.2 %collective-permute-start.1 = (bf16[384,768]{1,0:T(8,128)(2,1)S(1)}, bf16[384,768]{1,0:T(8,128)(2,1)S(1)}, u32[]{:S(2)}, u32[]{:S(2)}) collective-permute-start(bf16[384,768]{1,0:T(8,128)(2,1)S(1)} %copy.60), channel_id=1, source_target_pairs={{0,24},{1,9},{8,0},{9,17},{16,8},{17,25},{24,16},{25,1},{2,26},{3,... | collective-permute-start | bytes 1769480 | tf_op jit(solution)/shard_map/ppermute | solution.py:44
  13.8 2.1 %constant_dynamic-slice_fusion.10 = bf16[64,6144]{1,0:T(8,128)(2,1)} fusion(bf16[512,6144]{1,0:T(8,128)(2,1)} %x.3, s32[]{:T(128)S(6)} %select_n.133), kind=kLoop, calls=%fused_computation.27 | loop fusion | bytes 1572868 | tf_op jit(solution)/shard_map/dynamic_slice | solution.py:341
  15.9 9.0 %collective-permute-done.refs_4_ = bf16[384,768]{1,0:T(8,128)(2,1)} collective-permute-done((bf16[384,768]{1,0:T(8,128)(2,1)S(1)}, bf16[384,768]{1,0:T(8,128)(2,1)}, u32[]{:S(2)}, u32[]{:S(2)}) %collective-permute-start) | collective-permute-done | bytes 589856 | tf_op jit(solution)/shard_map/ppermute | solution.py:44
  30.1 3.1 %collective-permute-start.8 = (bf16[384,768]{1,0:T(8,128)(2,1)}, bf16[384,768]{1,0:T(8,128)(2,1)}, u32[]{:S(2)}, u32[]{:S(2)}) collective-permute-start(bf16[384,768]{1,0:T(8,128)(2,1)} %copy.64), channel_id=1, source_target_pairs={{0,16},{1,17},{8,24},{9,25},{16,0},{17,1},{24,8},{25,9},{2,18},{3,... | collective-permute-start | bytes 1769480 | tf_op jit(solution)/shard_map/ppermute | solution.py:44
  44.1 2.0 copy-done.3
  46.1 4.3 %collective-permute-done.3.refs_2_ = bf16[384,768]{1,0:T(8,128)(2,1)} collective-permute-done((bf16[384,768]{1,0:T(8,128)(2,1)}, bf16[384,768]{1,0:T(8,128)(2,1)}, u32[]{:S(2)}, u32[]{:S(2)}) %collective-permute-start.3) | collective-permute-done | bytes 589856 | tf_op jit(solution)/shard_map/ppermute | solution.py:44
  50.7 6.0 %collective-permute-done.5.refs_5_ = bf16[384,768]{1,0:T(8,128)(2,1)} collective-permute-done((bf16[384,768]{1,0:T(8,128)(2,1)}, bf16[384,768]{1,0:T(8,128)(2,1)}, u32[]{:S(2)}, u32[]{:S(2)}) %collective-permute-start.5) | collective-permute-done | bytes 589856 | tf_op jit(solution)/shard_map/ppermute | solution.py:44
  58.6 4.3 %collective-permute-done.4.refs_3_ = bf16[384,768]{1,0:T(8,128)(2,1)S(1)} collective-permute-done((bf16[384,768]{1,0:T(8,128)(2,1)}, bf16[384,768]{1,0:T(8,128)(2,1)S(1)}, u32[]{:S(2)}, u32[]{:S(2)}) %collective-permute-start.4) | collective-permute-done | bytes 589856 | tf_op jit(solution)/shard_map/ppermute | solution.py:44
  62.9 6.3 %collective-permute-done.6.refs_6_ = bf16[384,768]{1,0:T(8,128)(2,1)S(1)} collective-permute-done((bf16[384,768]{1,0:T(8,128)(2,1)}, bf16[384,768]{1,0:T(8,128)(2,1)S(1)}, u32[]{:S(2)}, u32[]{:S(2)}) %collective-permute-start.6) | collective-permute-done | bytes 589856 | tf_op jit(solution)/shard_map/ppermute | solution.py:44
  69.6 6.0 %collective-permute-done.12.refs_13_ = bf16[384,768]{1,0:T(8,128)(2,1)S(1)} collective-permute-done((bf16[384,768]{1,0:T(8,128)(2,1)S(1)}, bf16[384,768]{1,0:T(8,128)(2,1)S(1)}, u32[]{:S(2)}, u32[]{:S(2)}) %collective-permute-start.12) | collective-permute-done | bytes 589856 | tf_op jit(solution)/shard_map/ppermute | solution.py:44
  75.9 6.0 %collective-permute-done.9.refs_9_ = bf16[384,768]{1,0:T(8,128)(2,1)S(1)} collective-permute-done((bf16[384,768]{1,0:T(8,128)(2,1)}, bf16[384,768]{1,0:T(8,128)(2,1)S(1)}, u32[]{:S(2)}, u32[]{:S(2)}) %collective-permute-start.9) | collective-permute-done | bytes 589856 | tf_op jit(solution)/shard_map/ppermute | solution.py:44
  83.5 4.7 %collective-permute-done.13.refs_14_ = bf16[384,768]{1,0:T(8,128)(2,1)S(1)} collective-permute-done((bf16[384,768]{1,0:T(8,128)(2,1)S(1)}, bf16[384,768]{1,0:T(8,128)(2,1)S(1)}, u32[]{:S(2)}, u32[]{:S(2)}) %collective-permute-start.13) | collective-permute-done | bytes 589856 | tf_op jit(solution)/shard_map/ppermute | solution.py:44
  88.5 6.0 %collective-permute-done.10.refs_10_ = bf16[384,768]{1,0:T(8,128)(2,1)S(1)} collective-permute-done((bf16[384,768]{1,0:T(8,128)(2,1)S(1)}, bf16[384,768]{1,0:T(8,128)(2,1)S(1)}, u32[]{:S(2)}, u32[]{:S(2)}) %collective-permute-start.10) | collective-permute-done | bytes 589856 | tf_op jit(solution)/shard_map/ppermute | solution.py:44
  95.4 11.7 %collective-permute-done.14.refs_15_ = bf16[384,768]{1,0:T(8,128)(2,1)S(1)} collective-permute-done((bf16[384,768]{1,0:T(8,128)(2,1)S(1)}, bf16[384,768]{1,0:T(8,128)(2,1)S(1)}, u32[]{:S(2)}, u32[]{:S(2)}) %collective-permute-start.14) | collective-permute-done | bytes 589856 | tf_op jit(solution)/shard_map/ppermute | solution.py:44
  107.9 5.6 %collective-permute-done.11.refs_11_ = bf16[384,768]{1,0:T(8,128)(2,1)} collective-permute-done((bf16[384,768]{1,0:T(8,128)(2,1)S(1)}, bf16[384,768]{1,0:T(8,128)(2,1)}, u32[]{:S(2)}, u32[]{:S(2)}) %collective-permute-start.11) | collective-permute-done | bytes 589856 | tf_op jit(solution)/shard_map/ppermute | solution.py:44
  113.6 12.7 %project_own.1 = (bf16[4,512,768]{2,1,0:T(8,128)(2,1)}, bf16[6144,768]{1,0:T(8,128)(2,1)}) custom-call(s32[4]{0:T(128)} %pad_add_fusion.place, bf16[512,6144]{1,0:T(8,128)(2,1)} %x.3, bf16[384,768]{1,0:T(8,128)(2,1)} %copy.75.refs_0_, bf16[384,768]{1,0:T(8,128)(2,1)} %collective-permute-done.2.refs_1_, bf16[384,768]{1,0:T(8,128)(2,1)} %collective-permute-done.3.refs_2_, ...), custom_call_target="tpu_custom_call" | custom-call | flops 4831838208 | bytes 17825792 | tf_op jit(solution)/shard_map/project_own/pallas_call | solution.py:137
  126.4 22.0 %project_others.1 = bf16[4,512,768]{2,1,0:T(8,128)(2,1)} custom-call(s32[4]{0:T(128)} %pad_add_fusion.place, bf16[4,512,6144]{2,1,0:T(8,128)(2,1)} %bitcast.53, bf16[6144,768]{1,0:T(8,128)(2,1)} %get-tuple-element.30.w, bf16[4,512,768]{2,1,0:T(8,128)(2,1)} %get-tuple-element.31.own), custom_call_target="tpu_custom_call", output_to_operand_aliasing={{}: (3, {})} | custom-call | flops 14495514624 | bytes 32505856 | tf_op jit(solution)/shard_map/project_others/pallas_call | solution.py:160
  148.4 1.9 copy-done.2
  150.3 2.4 %states.1 = (f32[8,2,128,128]{3,2,1,0:T(8,128)S(1)}, bf16[2,128,128]{2,1,0:T(8,128)(2,1)S(1)}) custom-call(bf16[2048,768]{1,0:T(8,128)(2,1)S(1)} %bitcast.36, bf16[2048,768]{1,0:T(8,128)(2,1)S(1)} %bitcast.37, f32[2048,2]{1,0:T(8,128)S(1)} %bitcast.39, f32[2,8]{1,0:T(2,128)S(1)} %concatenate.3.suffix), custom_call_target="tpu_custom_call" | custom-call | flops 134217728 | bytes 4194304 | tf_op jit(solution)/shard_map/states/pallas_call | solution.py:347
  152.7 2.0 %collective-permute-start.15 = (bf16[2,128,128]{2,1,0:T(8,128)(2,1)S(1)}, bf16[2,128,128]{2,1,0:T(8,128)(2,1)S(1)}, u32[]{:S(2)}, u32[]{:S(2)}) collective-permute-start(bf16[2,128,128]{2,1,0:T(8,128)(2,1)S(1)} %get-tuple-element.35), channel_id=1, source_target_pairs={{0,32},{32,64},{64,96},{1,33},{33,65},{65,97},{2,34},{34,66},{66,9... | collective-permute-start | bytes 196616 | tf_op jit(solution)/shard_map/ppermute | solution.py:27
  154.7 4.5 %collective-permute-start.16 = (bf16[2,128,128]{2,1,0:T(8,128)(2,1)S(1)}, bf16[2,128,128]{2,1,0:T(8,128)(2,1)S(1)}, u32[]{:S(2)}, u32[]{:S(2)}) collective-permute-start(bf16[2,128,128]{2,1,0:T(8,128)(2,1)S(1)} %get-tuple-element.35), channel_id=1, source_target_pairs={{0,64},{32,96},{1,65},{33,97},{2,66},{34,98},{3,67},{35,99},{4,68}... | collective-permute-start | bytes 196616 | tf_op jit(solution)/shard_map/ppermute | solution.py:27
  160.6 4.3 %intras.1 = (bf16[2048,256]{1,0:T(8,128)(2,1)S(1)}, f32[2048,256]{1,0:T(8,128)S(1)}) custom-call(bf16[2048,768]{1,0:T(8,128)(2,1)S(1)} %bitcast.38, f32[8,2,256,256]{3,2,1,0:T(8,128)S(1)} %copy-done.4, f32[2048,2]{1,0:T(8,128)S(1)} %bitcast.42), custom_call_target="tpu_custom_call" | custom-call | flops 1073741824 | bytes 8388608 | tf_op jit(solution)/shard_map/intras/pallas_call | solution.py:370
  164.9 2.2 %inters.1 = (bf16[512,256]{1,0:T(8,128)(2,1)S(1)}, bf16[512,256]{1,0:T(8,128)(2,1)S(1)}, bf16[512,256]{1,0:T(8,128)(2,1)S(1)}, bf16[512,256]{1,0:T(8,128)(2,1)S(...) custom-call(s32[4]{0:T(128)S(1)} %copy-done.6, ...), custom_call_target="tpu_custom_call" | custom-call | flops 268435456 | bytes 6291456 | tf_op jit(solution)/shard_map/inters/pallas_call | solution.py:387
  168.0 2.5 %collective-permute-start.23 = (bf16[512,256]{1,0:T(8,128)(2,1)S(1)}, bf16[512,256]{1,0:T(8,128)(2,1)S(1)}, u32[]{:S(2)}, u32[]{:S(2)}) collective-permute-start(bf16[512,256]{1,0:T(8,128)(2,1)S(1)} %get-tuple-element.41), channel_id=1, source_target_pairs={{0,24},{8,0},{16,8},{24,16},{1,25},{9,1},{17,9},{25,17},{2,26},{10... | collective-permute-start | bytes 786440 | tf_op jit(solution)/shard_map/ppermute | solution.py:31
  170.5 3.2 %collective-permute-start.19 = (f32[2,8,256]{2,1,0:T(8,128)S(1)}, f32[2,8,256]{2,1,0:T(8,128)S(1)}, u32[]{:S(2)}, u32[]{:S(2)}) collective-permute-start(f32[2,8,256]{2,1,0:T(8,128)S(1)} %get-tuple-element.38), channel_id=1, source_target_pairs={{0,24},{8,0},{16,8},{24,16},{1,25},{9,1},{17,9},{25,17},{2,26},{10... | collective-permute-start | bytes 49160 | tf_op jit(solution)/shard_map/ppermute | solution.py:31
  173.7 4.0 %collective-permute-done.18 = f32[2,8,256]{2,1,0:T(8,128)S(1)} collective-permute-done((f32[2,8,256]{2,1,0:T(8,128)S(1)}, f32[2,8,256]{2,1,0:T(8,128)S(1)}, u32[]{:S(2)}, u32[]{:S(2)}) %collective-permute-start.18) | collective-permute-done | bytes 16416 | tf_op jit(solution)/shard_map/ppermute | solution.py:31
  181.7 1.8 collective-permute-start.25
  183.5 1.8 collective-permute-start.26
  185.4 3.3 %collective-permute-done.26 = f32[2,8,256]{2,1,0:T(8,128)S(1)} collective-permute-done((f32[2,8,256]{2,1,0:T(8,128)S(1)}, f32[2,8,256]{2,1,0:T(8,128)S(1)}, u32[]{:S(2)}, u32[]{:S(2)}) %collective-permute-start.26) | collective-permute-done | bytes 16416 | tf_op jit(solution)/shard_map/ppermute | solution.py:35
  188.8 2.0 %finish.1 = bf16[512,1024]{1,0:T(8,128)(2,1)} custom-call(s32[4]{0:T(128)S(1)} %copy-done.6, f32[2,8,256]{2,1,0:T(8,128)S(1)} %add_add_fusion.total, f32[1,1024]{1,0:T(1,128)S(1)} %bitcast.44, bf16[512,256]{1,0:T(8,128)(2,1)S(1)} %get-tuple-element.43.p0, bf16[512,256]{1,0:T(8,128)(2,1)S(1)} %collective-permute-done.22.p1, ...), custom_call_target="tpu_custom_call" | custom-call | flops 4194304 | bytes 3145728 | tf_op jit(solution)/shard_map/finish/pallas_call | solution.py:411
  (136 shorter events, 30.2 us)
Async XLA Ops:
  6.5 119.8 %all-gather.2.cloned.1.call-start = ((), (), s32[]{:S(2)}) async-start(), calls=%async_computation | async-start | bytes 25952256 | tf_op jit(solution)/shard_map/all_gather | solution.py:343
  8.9 15.9 %collective-permute-start = (bf16[384,768]{1,0:T(8,128)(2,1)S(1)}, bf16[384,768]{1,0:T(8,128)(2,1)}, u32[]{:S(2)}, u32[]{:S(2)}) collective-permute-start(bf16[384,768]{1,0:T(8,128)(2,1)S(1)} %copy.58), channel_id=1, source_target_pairs={{0,8},{1,25},{8,16},{9,1},{16,24},{17,9},{24,0},{25,17},{2,10},{3,... | collective-permute-start | bytes 1769480 | tf_op jit(solution)/shard_map/ppermute | solution.py:44
  11.6 14.1 %collective-permute-start.1 = (bf16[384,768]{1,0:T(8,128)(2,1)S(1)}, bf16[384,768]{1,0:T(8,128)(2,1)S(1)}, u32[]{:S(2)}, u32[]{:S(2)}) collective-permute-start(bf16[384,768]{1,0:T(8,128)(2,1)S(1)} %copy.60), channel_id=1, source_target_pairs={{0,24},{1,9},{8,0},{9,17},{16,8},{17,25},{24,16},{25,1},{2,26},{3,... | collective-permute-start | bytes 1769480 | tf_op jit(solution)/shard_map/ppermute | solution.py:44
  27.1 11.8 %collective-permute-start.2 = (bf16[384,768]{1,0:T(8,128)(2,1)}, bf16[384,768]{1,0:T(8,128)(2,1)}, u32[]{:S(2)}, u32[]{:S(2)}) collective-permute-start(bf16[384,768]{1,0:T(8,128)(2,1)} %copy.75.refs_0_), channel_id=1, source_target_pairs={{0,32},{1,97},{32,64},{33,1},{64,96},{65,33},{96,0},{97,65},{2,34}... | collective-permute-start | bytes 1769480 | tf_op jit(solution)/shard_map/ppermute | solution.py:44
  30.1 28.5 %collective-permute-start.8 = (bf16[384,768]{1,0:T(8,128)(2,1)}, bf16[384,768]{1,0:T(8,128)(2,1)}, u32[]{:S(2)}, u32[]{:S(2)}) collective-permute-start(bf16[384,768]{1,0:T(8,128)(2,1)} %copy.64), channel_id=1, source_target_pairs={{0,16},{1,17},{8,24},{9,25},{16,0},{17,1},{24,8},{25,9},{2,18},{3,... | collective-permute-start | bytes 1769480 | tf_op jit(solution)/shard_map/ppermute | solution.py:44
  38.9 11.4 %collective-permute-start.3 = (bf16[384,768]{1,0:T(8,128)(2,1)}, bf16[384,768]{1,0:T(8,128)(2,1)}, u32[]{:S(2)}, u32[]{:S(2)}) collective-permute-start(bf16[384,768]{1,0:T(8,128)(2,1)} %collective-permute-done.2.refs_1_), channel_id=1, source_target_pairs={{0,32},{1,97},{32,64},{33,1},{64,96},{65,33},{96,0},{97,65},{2,34}... | collective-permute-start | bytes 1769480 | tf_op jit(solution)/shard_map/ppermute | solution.py:44
  40.5 16.2 %collective-permute-start.5 = (bf16[384,768]{1,0:T(8,128)(2,1)}, bf16[384,768]{1,0:T(8,128)(2,1)}, u32[]{:S(2)}, u32[]{:S(2)}) collective-permute-start(bf16[384,768]{1,0:T(8,128)(2,1)} %collective-permute-done.refs_4_), channel_id=1, source_target_pairs={{0,32},{1,97},{32,64},{33,1},{64,96},{65,33},{96,0},{97,65},{2,34}... | collective-permute-start | bytes 1769480 | tf_op jit(solution)/shard_map/ppermute | solution.py:44
  50.3 12.5 %collective-permute-start.4 = (bf16[384,768]{1,0:T(8,128)(2,1)}, bf16[384,768]{1,0:T(8,128)(2,1)S(1)}, u32[]{:S(2)}, u32[]{:S(2)}) collective-permute-start(bf16[384,768]{1,0:T(8,128)(2,1)} %collective-permute-done.3.refs_2_), channel_id=1, source_target_pairs={{0,32},{1,97},{32,64},{33,1},{64,96},{65,33},{96,0},{97,65},{2,34}... | collective-permute-start | bytes 1769480 | tf_op jit(solution)/shard_map/ppermute | solution.py:44
  56.7 12.5 %collective-permute-start.6 = (bf16[384,768]{1,0:T(8,128)(2,1)}, bf16[384,768]{1,0:T(8,128)(2,1)S(1)}, u32[]{:S(2)}, u32[]{:S(2)}) collective-permute-start(bf16[384,768]{1,0:T(8,128)(2,1)} %collective-permute-done.5.refs_5_), channel_id=1, source_target_pairs={{0,32},{1,97},{32,64},{33,1},{64,96},{65,33},{96,0},{97,65},{2,34}... | collective-permute-start | bytes 1769480 | tf_op jit(solution)/shard_map/ppermute | solution.py:44
  57.3 18.2 %collective-permute-start.12 = (bf16[384,768]{1,0:T(8,128)(2,1)S(1)}, bf16[384,768]{1,0:T(8,128)(2,1)S(1)}, u32[]{:S(2)}, u32[]{:S(2)}) collective-permute-start(bf16[384,768]{1,0:T(8,128)(2,1)S(1)} %copy-done.9), channel_id=1, source_target_pairs={{0,32},{1,97},{32,64},{33,1},{64,96},{65,33},{96,0},{97,65},{2,34}... | collective-permute-start | bytes 1769480 | tf_op jit(solution)/shard_map/ppermute | solution.py:44
  62.9 50.7 %copy-start.10 = (bf16[384,768]{1,0:T(8,128)(2,1)}, bf16[384,768]{1,0:T(8,128)(2,1)S(1)}, u32[]{:S(2)}) copy-start(bf16[384,768]{1,0:T(8,128)(2,1)S(1)} %collective-permute-done.4.refs_3_) | copy-start | bytes 1769476
  69.2 44.3 %copy-start.11 = (bf16[384,768]{1,0:T(8,128)(2,1)}, bf16[384,768]{1,0:T(8,128)(2,1)S(1)}, u32[]{:S(2)}) copy-start(bf16[384,768]{1,0:T(8,128)(2,1)S(1)} %collective-permute-done.6.refs_6_) | copy-start | bytes 1769476
  69.2 12.6 %collective-permute-start.9 = (bf16[384,768]{1,0:T(8,128)(2,1)}, bf16[384,768]{1,0:T(8,128)(2,1)S(1)}, u32[]{:S(2)}, u32[]{:S(2)}) collective-permute-start(bf16[384,768]{1,0:T(8,128)(2,1)} %collective-permute-done.8.refs_8_), channel_id=1, source_target_pairs={{0,32},{1,97},{32,64},{33,1},{64,96},{65,33},{96,0},{97,65},{2,34}... | collective-permute-start | bytes 1769480 | tf_op jit(solution)/shard_map/ppermute | solution.py:44
  75.5 38.0 %copy-start.12 = (bf16[384,768]{1,0:T(8,128)(2,1)}, bf16[384,768]{1,0:T(8,128)(2,1)S(1)}, u32[]{:S(2)}) copy-start(bf16[384,768]{1,0:T(8,128)(2,1)S(1)} %collective-permute-done.12.refs_13_) | copy-start | bytes 1769476
  75.5 12.6 %collective-permute-start.13 = (bf16[384,768]{1,0:T(8,128)(2,1)S(1)}, bf16[384,768]{1,0:T(8,128)(2,1)S(1)}, u32[]{:S(2)}, u32[]{:S(2)}) collective-permute-start(bf16[384,768]{1,0:T(8,128)(2,1)S(1)} %collective-permute-done.12.refs_13_), channel_id=1, source_target_pairs={{0,32},{1,97},{32,64},{33,1},{64,96},{65,33},{96,0},{97,65},{2,34}... | collective-permute-start | bytes 1769480 | tf_op jit(solution)/shard_map/ppermute | solution.py:44
  81.8 12.6 %collective-permute-start.10 = (bf16[384,768]{1,0:T(8,128)(2,1)S(1)}, bf16[384,768]{1,0:T(8,128)(2,1)S(1)}, u32[]{:S(2)}, u32[]{:S(2)}) collective-permute-start(bf16[384,768]{1,0:T(8,128)(2,1)S(1)} %collective-permute-done.9.refs_9_), channel_id=1, source_target_pairs={{0,32},{1,97},{32,64},{33,1},{64,96},{65,33},{96,0},{97,65},{2,34}... | collective-permute-start | bytes 1769480 | tf_op jit(solution)/shard_map/ppermute | solution.py:44
  82.2 24.9 %collective-permute-start.7 = (bf16[384,768]{1,0:T(8,128)(2,1)S(1)}, bf16[384,768]{1,0:T(8,128)(2,1)S(1)}, u32[]{:S(2)}, u32[]{:S(2)}) collective-permute-start(bf16[384,768]{1,0:T(8,128)(2,1)S(1)} %collective-permute-done.6.refs_6_), channel_id=1, source_target_pairs={{0,32},{1,97},{32,64},{33,1},{64,96},{65,33},{96,0},{97,65},{2,34}... | collective-permute-start | bytes 1769480 | tf_op jit(solution)/shard_map/ppermute | solution.py:44
  88.1 19.0 %collective-permute-start.14 = (bf16[384,768]{1,0:T(8,128)(2,1)S(1)}, bf16[384,768]{1,0:T(8,128)(2,1)S(1)}, u32[]{:S(2)}, u32[]{:S(2)}) collective-permute-start(bf16[384,768]{1,0:T(8,128)(2,1)S(1)} %collective-permute-done.13.refs_14_), channel_id=1, source_target_pairs={{0,32},{1,97},{32,64},{33,1},{64,96},{65,33},{96,0},{97,65},{2,34}... | collective-permute-start | bytes 1769480 | tf_op jit(solution)/shard_map/ppermute | solution.py:44
  94.5 19.1 %collective-permute-start.11 = (bf16[384,768]{1,0:T(8,128)(2,1)S(1)}, bf16[384,768]{1,0:T(8,128)(2,1)}, u32[]{:S(2)}, u32[]{:S(2)}) collective-permute-start(bf16[384,768]{1,0:T(8,128)(2,1)S(1)} %collective-permute-done.10.refs_10_), channel_id=1, source_target_pairs={{0,32},{1,97},{32,64},{33,1},{64,96},{65,33},{96,0},{97,65},{2,34}... | collective-permute-start | bytes 1769480 | tf_op jit(solution)/shard_map/ppermute | solution.py:44
  152.7 12.2 %collective-permute-start.15 = (bf16[2,128,128]{2,1,0:T(8,128)(2,1)S(1)}, bf16[2,128,128]{2,1,0:T(8,128)(2,1)S(1)}, u32[]{:S(2)}, u32[]{:S(2)}) collective-permute-start(bf16[2,128,128]{2,1,0:T(8,128)(2,1)S(1)} %get-tuple-element.35), channel_id=1, source_target_pairs={{0,32},{32,64},{64,96},{1,33},{33,65},{65,97},{2,34},{34,66},{66,9... | collective-permute-start | bytes 196616 | tf_op jit(solution)/shard_map/ppermute | solution.py:27
  154.7 10.2 %collective-permute-start.16 = (bf16[2,128,128]{2,1,0:T(8,128)(2,1)S(1)}, bf16[2,128,128]{2,1,0:T(8,128)(2,1)S(1)}, u32[]{:S(2)}, u32[]{:S(2)}) collective-permute-start(bf16[2,128,128]{2,1,0:T(8,128)(2,1)S(1)} %get-tuple-element.35), channel_id=1, source_target_pairs={{0,64},{32,96},{1,65},{33,97},{2,66},{34,98},{3,67},{35,99},{4,68}... | collective-permute-start | bytes 196616 | tf_op jit(solution)/shard_map/ppermute | solution.py:27
  159.3 5.6 %collective-permute-start.17 = (bf16[2,128,128]{2,1,0:T(8,128)(2,1)S(1)}, bf16[2,128,128]{2,1,0:T(8,128)(2,1)S(1)}, u32[]{:S(2)}, u32[]{:S(2)}) collective-permute-start(bf16[2,128,128]{2,1,0:T(8,128)(2,1)S(1)} %get-tuple-element.35), channel_id=1, source_target_pairs={{0,96},{1,97},{2,98},{3,99},{4,100},{5,101},{6,102},{7,103},{8,104... | collective-permute-start | bytes 196616 | tf_op jit(solution)/shard_map/ppermute | solution.py:27
  167.2 13.0 %collective-permute-start.22 = (bf16[512,256]{1,0:T(8,128)(2,1)S(1)}, bf16[512,256]{1,0:T(8,128)(2,1)S(1)}, u32[]{:S(2)}, u32[]{:S(2)}) collective-permute-start(bf16[512,256]{1,0:T(8,128)(2,1)S(1)} %get-tuple-element.40), channel_id=1, source_target_pairs={{0,8},{8,16},{16,24},{24,0},{1,9},{9,17},{17,25},{25,1},{2,10},{10... | collective-permute-start | bytes 786440 | tf_op jit(solution)/shard_map/ppermute | solution.py:31
  168.0 12.2 %collective-permute-start.23 = (bf16[512,256]{1,0:T(8,128)(2,1)S(1)}, bf16[512,256]{1,0:T(8,128)(2,1)S(1)}, u32[]{:S(2)}, u32[]{:S(2)}) collective-permute-start(bf16[512,256]{1,0:T(8,128)(2,1)S(1)} %get-tuple-element.41), channel_id=1, source_target_pairs={{0,24},{8,0},{16,8},{24,16},{1,25},{9,1},{17,9},{25,17},{2,26},{10... | collective-permute-start | bytes 786440 | tf_op jit(solution)/shard_map/ppermute | solution.py:31
  170.5 7.2 %collective-permute-start.18 = (f32[2,8,256]{2,1,0:T(8,128)S(1)}, f32[2,8,256]{2,1,0:T(8,128)S(1)}, u32[]{:S(2)}, u32[]{:S(2)}) collective-permute-start(f32[2,8,256]{2,1,0:T(8,128)S(1)} %get-tuple-element.37), channel_id=1, source_target_pairs={{0,8},{8,16},{16,24},{24,0},{1,9},{9,17},{17,25},{25,1},{2,10},{10... | collective-permute-start | bytes 49160 | tf_op jit(solution)/shard_map/ppermute | solution.py:31
  170.5 7.6 %collective-permute-start.19 = (f32[2,8,256]{2,1,0:T(8,128)S(1)}, f32[2,8,256]{2,1,0:T(8,128)S(1)}, u32[]{:S(2)}, u32[]{:S(2)}) collective-permute-start(f32[2,8,256]{2,1,0:T(8,128)S(1)} %get-tuple-element.38), channel_id=1, source_target_pairs={{0,24},{8,0},{16,8},{24,16},{1,25},{9,1},{17,9},{25,17},{2,26},{10... | collective-permute-start | bytes 49160 | tf_op jit(solution)/shard_map/ppermute | solution.py:31
  173.7 5.2 %collective-permute-start.20 = (f32[2,8,256]{2,1,0:T(8,128)S(1)}, f32[2,8,256]{2,1,0:T(8,128)S(1)}, u32[]{:S(2)}, u32[]{:S(2)}) collective-permute-start(f32[2,8,256]{2,1,0:T(8,128)S(1)} %get-tuple-element.39), channel_id=1, source_target_pairs={{0,16},{8,24},{16,0},{24,8},{1,17},{9,25},{17,1},{25,9},{2,18},{10... | collective-permute-start | bytes 49160 | tf_op jit(solution)/shard_map/ppermute | solution.py:31
  177.7 11.0 %collective-permute-start.27 = (bf16[512,256]{1,0:T(8,128)(2,1)S(1)}, bf16[512,256]{1,0:T(8,128)(2,1)S(1)}, u32[]{:S(2)}, u32[]{:S(2)}) collective-permute-start(bf16[512,256]{1,0:T(8,128)(2,1)S(1)} %get-tuple-element.44), channel_id=1, source_target_pairs={{0,16},{8,24},{16,0},{24,8},{1,17},{9,25},{17,1},{25,9},{2,18},{10... | collective-permute-start | bytes 786440 | tf_op jit(solution)/shard_map/ppermute | solution.py:31
  179.0 1.2 collective-permute-start.21
  180.2 5.1 %collective-permute-start.24 = (f32[2,8,256]{2,1,0:T(8,128)S(1)}, f32[2,8,256]{2,1,0:T(8,128)S(1)}, u32[]{:S(2)}, u32[]{:S(2)}) collective-permute-start(f32[2,8,256]{2,1,0:T(8,128)S(1)} %add.198), channel_id=1, source_target_pairs={{0,2},{2,4},{4,6},{6,0},{1,3},{3,5},{5,7},{7,1},{8,10},{10,12},{12... | collective-permute-start | bytes 49160 | tf_op jit(solution)/shard_map/ppermute | solution.py:35
  181.7 3.7 %collective-permute-start.25 = (f32[2,8,256]{2,1,0:T(8,128)S(1)}, f32[2,8,256]{2,1,0:T(8,128)S(1)}, u32[]{:S(2)}, u32[]{:S(2)}) collective-permute-start(f32[2,8,256]{2,1,0:T(8,128)S(1)} %add.198), channel_id=1, source_target_pairs={{0,6},{2,0},{4,2},{6,4},{1,7},{3,1},{5,3},{7,5},{8,14},{10,8},{12,... | collective-permute-start | bytes 49160 | tf_op jit(solution)/shard_map/ppermute | solution.py:35
  183.5 5.2 %collective-permute-start.26 = (f32[2,8,256]{2,1,0:T(8,128)S(1)}, f32[2,8,256]{2,1,0:T(8,128)S(1)}, u32[]{:S(2)}, u32[]{:S(2)}) collective-permute-start(f32[2,8,256]{2,1,0:T(8,128)S(1)} %add.198), channel_id=1, source_target_pairs={{0,4},{2,6},{4,0},{6,2},{1,5},{3,7},{5,1},{7,3},{8,12},{10,14},{12... | collective-permute-start | bytes 49160 | tf_op jit(solution)/shard_map/ppermute | solution.py:35
  (16 other events, 247.7 us)
Sparse Core Ops, SparseCore 0:
  25.9 98.9 all-gather.1

commit v6 on v4

--- a/solution.py
+++ b/solution.py
@@ -65,6 +65,7 @@
 
 def spread_weights(weights, early):
     got = {"z0": weights[0], "early": early}
+    weights[3] = lax.optimization_barrier((weights[3], weights[0]))[0]
     for name, after in ORDER:
         if name[0] == "z":
             source = weights[int(name[1])]

time: 197 us -> 197 us (level)
  transfers between devices with their start and end apart: 29 -> 29, of which waited for: 17 -> 17; matrix products, arithmetic and copies ran while one was open for 6% -> 6% of each run, Pallas kernels for 10% -> 9%
where the time goes in v6:
time: 197 us; the launch traced here: 196 us
  waiting for transfers between devices  78.5 us (40%)
  Pallas kernels  47.3 us (24%)
  starting transfers between devices  37.4 us (19%)
  local copies, waits for them, and re-layouts  16.6 us (8%)
  between operations  13.8 us (7%)
  other arithmetic  3 us (2%)
    ppermute x15, waiting for transfers between devices, opposed(): return lax.ppermute(a, (axis, 'c'), perm)  70.1 us
    pallas_call x1, Pallas kernels, call_project(): pl.pallas_call(project_others, out_shape=shape, grid_spec=pltpu.PrefetchS...  22 us
    ppermute x15, starting transfers between devices, opposed(): return lax.ppermute(a, (axis, 'c'), perm)  17.2 us
    pallas_call x1, Pallas kernels, call_project(): pl.pallas_call(project_own, out_shape=(shape, jax.ShapeDtypeStruct(whole,...  12.6 us
    ppermute x3, starting transfers between devices, move_x(): return lax.ppermute(a, 'x', [(s, (s + d) % 4) for s in range(4)])  7.85 us
    ppermute x6, starting transfers between devices, move_z(): return lax.ppermute(a, 'z', [(s, (s + d) % 4) for s in range(4)])  7.69 us
    unnamed x44, local copies, waits for them, and re-layouts  6.33 us
    ppermute x3, starting transfers between devices, move_y(): return lax.ppermute(a, 'y', [(s, (s + d) % 4) for s in range(4)])  4.59 us
  transfers between devices with their start and end apart: 29, of which 17 were waited for; matrix products, arithmetic and copies ran while one was open for 6% of the time, Pallas kernels for 9%

profile of v6, /device:TPU:0, one launch (start us, length us, event | category | flops | bytes accessed | tf_op | source)
XLA Modules:
  0.0 196.5 jit_solution(2907185529749318888)
XLA Ops:
  6.5 1.8 constant_dynamic-slice_fusion.6
  8.9 2.1 %collective-permute-start = (bf16[384,768]{1,0:T(8,128)(2,1)S(1)}, bf16[384,768]{1,0:T(8,128)(2,1)}, u32[]{:S(2)}, u32[]{:S(2)}) collective-permute-start(bf16[384,768]{1,0:T(8,128)(2,1)S(1)} %copy.58), channel_id=1, source_target_pairs={{0,8},{1,25},{8,16},{9,1},{16,24},{17,9},{24,0},{25,17},{2,10},{3,... | collective-permute-start | bytes 1769480 | tf_op jit(solution)/shard_map/ppermute | solution.py:44
  11.9 2.2 %collective-permute-start.1 = (bf16[384,768]{1,0:T(8,128)(2,1)S(1)}, bf16[384,768]{1,0:T(8,128)(2,1)S(1)}, u32[]{:S(2)}, u32[]{:S(2)}) collective-permute-start(bf16[384,768]{1,0:T(8,128)(2,1)S(1)} %copy.61), channel_id=1, source_target_pairs={{0,24},{1,9},{8,0},{9,17},{16,8},{17,25},{24,16},{25,1},{2,26},{3,... | collective-permute-start | bytes 1769480 | tf_op jit(solution)/shard_map/ppermute | solution.py:44
  14.1 2.1 %constant_dynamic-slice_fusion.10 = bf16[64,6144]{1,0:T(8,128)(2,1)} fusion(bf16[512,6144]{1,0:T(8,128)(2,1)} %x.3, s32[]{:T(128)S(6)} %select_n.133), kind=kLoop, calls=%fused_computation.27 | loop fusion | bytes 1572868 | tf_op jit(solution)/shard_map/dynamic_slice | solution.py:342
  16.2 8.4 %collective-permute-done.refs_4_ = bf16[384,768]{1,0:T(8,128)(2,1)} collective-permute-done((bf16[384,768]{1,0:T(8,128)(2,1)S(1)}, bf16[384,768]{1,0:T(8,128)(2,1)}, u32[]{:S(2)}, u32[]{:S(2)}) %collective-permute-start) | collective-permute-done | bytes 589856 | tf_op jit(solution)/shard_map/ppermute | solution.py:44
  29.8 3.4 %collective-permute-start.8 = (bf16[384,768]{1,0:T(8,128)(2,1)}, bf16[384,768]{1,0:T(8,128)(2,1)}, u32[]{:S(2)}, u32[]{:S(2)}) collective-permute-start(bf16[384,768]{1,0:T(8,128)(2,1)} %copy.64), channel_id=1, source_target_pairs={{0,16},{1,17},{8,24},{9,25},{16,0},{17,1},{24,8},{25,9},{2,18},{3,... | collective-permute-start | bytes 1769480 | tf_op jit(solution)/shard_map/ppermute | solution.py:44
  42.4 1.7 decays.1.decay
  44.1 2.0 %copy-done.3 = f32[8,2,256,256]{3,2,1,0:T(8,128)} copy-done((f32[8,2,256,256]{3,2,1,0:T(8,128)}, f32[8,2,256,256]{3,2,1,0:T(8,128)S(1)}, u32[]{:S(2)}) %copy-start.3) | copy-done | bytes 4194328
  46.1 4.3 %collective-permute-done.3.refs_2_ = bf16[384,768]{1,0:T(8,128)(2,1)} collective-permute-done((bf16[384,768]{1,0:T(8,128)(2,1)}, bf16[384,768]{1,0:T(8,128)(2,1)}, u32[]{:S(2)}, u32[]{:S(2)}) %collective-permute-start.3) | collective-permute-done | bytes 589856 | tf_op jit(solution)/shard_map/ppermute | solution.py:44
  50.7 6.0 %collective-permute-done.5.refs_5_ = bf16[384,768]{1,0:T(8,128)(2,1)} collective-permute-done((bf16[384,768]{1,0:T(8,128)(2,1)}, bf16[384,768]{1,0:T(8,128)(2,1)}, u32[]{:S(2)}, u32[]{:S(2)}) %collective-permute-start.5) | collective-permute-done | bytes 589856 | tf_op jit(solution)/shard_map/ppermute | solution.py:44
  58.6 4.3 %collective-permute-done.4.refs_3_ = bf16[384,768]{1,0:T(8,128)(2,1)S(1)} collective-permute-done((bf16[384,768]{1,0:T(8,128)(2,1)}, bf16[384,768]{1,0:T(8,128)(2,1)S(1)}, u32[]{:S(2)}, u32[]{:S(2)}) %collective-permute-start.4) | collective-permute-done | bytes 589856 | tf_op jit(solution)/shard_map/ppermute | solution.py:44
  62.9 6.3 %collective-permute-done.6.refs_6_ = bf16[384,768]{1,0:T(8,128)(2,1)S(1)} collective-permute-done((bf16[384,768]{1,0:T(8,128)(2,1)}, bf16[384,768]{1,0:T(8,128)(2,1)S(1)}, u32[]{:S(2)}, u32[]{:S(2)}) %collective-permute-start.6) | collective-permute-done | bytes 589856 | tf_op jit(solution)/shard_map/ppermute | solution.py:44
  69.6 6.0 %collective-permute-done.12.refs_13_ = bf16[384,768]{1,0:T(8,128)(2,1)S(1)} collective-permute-done((bf16[384,768]{1,0:T(8,128)(2,1)S(1)}, bf16[384,768]{1,0:T(8,128)(2,1)S(1)}, u32[]{:S(2)}, u32[]{:S(2)}) %collective-permute-start.12) | collective-permute-done | bytes 589856 | tf_op jit(solution)/shard_map/ppermute | solution.py:44
  75.9 6.0 %collective-permute-done.9.refs_9_ = bf16[384,768]{1,0:T(8,128)(2,1)S(1)} collective-permute-done((bf16[384,768]{1,0:T(8,128)(2,1)}, bf16[384,768]{1,0:T(8,128)(2,1)S(1)}, u32[]{:S(2)}, u32[]{:S(2)}) %collective-permute-start.9) | collective-permute-done | bytes 589856 | tf_op jit(solution)/shard_map/ppermute | solution.py:44
  83.5 4.7 %collective-permute-done.13.refs_14_ = bf16[384,768]{1,0:T(8,128)(2,1)S(1)} collective-permute-done((bf16[384,768]{1,0:T(8,128)(2,1)S(1)}, bf16[384,768]{1,0:T(8,128)(2,1)S(1)}, u32[]{:S(2)}, u32[]{:S(2)}) %collective-permute-start.13) | collective-permute-done | bytes 589856 | tf_op jit(solution)/shard_map/ppermute | solution.py:44
  88.5 6.0 %collective-permute-done.10.refs_10_ = bf16[384,768]{1,0:T(8,128)(2,1)S(1)} collective-permute-done((bf16[384,768]{1,0:T(8,128)(2,1)S(1)}, bf16[384,768]{1,0:T(8,128)(2,1)S(1)}, u32[]{:S(2)}, u32[]{:S(2)}) %collective-permute-start.10) | collective-permute-done | bytes 589856 | tf_op jit(solution)/shard_map/ppermute | solution.py:44
  95.4 11.7 %collective-permute-done.14.refs_15_ = bf16[384,768]{1,0:T(8,128)(2,1)S(1)} collective-permute-done((bf16[384,768]{1,0:T(8,128)(2,1)S(1)}, bf16[384,768]{1,0:T(8,128)(2,1)S(1)}, u32[]{:S(2)}, u32[]{:S(2)}) %collective-permute-start.14) | collective-permute-done | bytes 589856 | tf_op jit(solution)/shard_map/ppermute | solution.py:44
  107.9 5.6 %collective-permute-done.11.refs_11_ = bf16[384,768]{1,0:T(8,128)(2,1)} collective-permute-done((bf16[384,768]{1,0:T(8,128)(2,1)S(1)}, bf16[384,768]{1,0:T(8,128)(2,1)}, u32[]{:S(2)}, u32[]{:S(2)}) %collective-permute-start.11) | collective-permute-done | bytes 589856 | tf_op jit(solution)/shard_map/ppermute | solution.py:44
  113.6 12.6 %project_own.1 = (bf16[4,512,768]{2,1,0:T(8,128)(2,1)}, bf16[6144,768]{1,0:T(8,128)(2,1)}) custom-call(s32[4]{0:T(128)} %pad_add_fusion.place, bf16[512,6144]{1,0:T(8,128)(2,1)} %x.3, bf16[384,768]{1,0:T(8,128)(2,1)} %copy.75.refs_0_, bf16[384,768]{1,0:T(8,128)(2,1)} %collective-permute-done.2.refs_1_, bf16[384,768]{1,0:T(8,128)(2,1)} %collective-permute-done.3.refs_2_, ...), custom_call_target="tpu_custom_call" | custom-call | flops 4831838208 | bytes 17825792 | tf_op jit(solution)/shard_map/project_own/pallas_call | solution.py:138
  126.2 22.0 %project_others.1 = bf16[4,512,768]{2,1,0:T(8,128)(2,1)} custom-call(s32[4]{0:T(128)} %pad_add_fusion.place, bf16[4,512,6144]{2,1,0:T(8,128)(2,1)} %bitcast.53, bf16[6144,768]{1,0:T(8,128)(2,1)} %get-tuple-element.32.w, bf16[4,512,768]{2,1,0:T(8,128)(2,1)} %get-tuple-element.33.own), custom_call_target="tpu_custom_call", output_to_operand_aliasing={{}: (3, {})} | custom-call | flops 14495514624 | bytes 32505856 | tf_op jit(solution)/shard_map/project_others/pallas_call | solution.py:161
  148.2 1.9 copy-done.2
  150.1 2.4 %states.1 = (f32[8,2,128,128]{3,2,1,0:T(8,128)S(1)}, bf16[2,128,128]{2,1,0:T(8,128)(2,1)S(1)}) custom-call(bf16[2048,768]{1,0:T(8,128)(2,1)S(1)} %bitcast.36, bf16[2048,768]{1,0:T(8,128)(2,1)S(1)} %bitcast.37, f32[2048,2]{1,0:T(8,128)S(1)} %bitcast.39, f32[2,8]{1,0:T(2,128)S(1)} %concatenate.3.suffix), custom_call_target="tpu_custom_call" | custom-call | flops 134217728 | bytes 4194304 | tf_op jit(solution)/shard_map/states/pallas_call | solution.py:348
  153.0 2.8 %collective-permute-start.16 = (bf16[2,128,128]{2,1,0:T(8,128)(2,1)S(1)}, bf16[2,128,128]{2,1,0:T(8,128)(2,1)S(1)}, u32[]{:S(2)}, u32[]{:S(2)}) collective-permute-start(bf16[2,128,128]{2,1,0:T(8,128)(2,1)S(1)} %get-tuple-element.37), channel_id=1, source_target_pairs={{0,64},{32,96},{64,0},{96,32},{1,65},{33,97},{65,1},{97,33},{2,66}... | collective-permute-start | bytes 196616 | tf_op jit(solution)/shard_map/ppermute | solution.py:27
  157.2 4.3 %intras.1 = (bf16[2048,256]{1,0:T(8,128)(2,1)S(1)}, f32[2048,256]{1,0:T(8,128)S(1)}) custom-call(bf16[2048,768]{1,0:T(8,128)(2,1)S(1)} %bitcast.38, f32[8,2,256,256]{3,2,1,0:T(8,128)S(1)} %copy-done.4, f32[2048,2]{1,0:T(8,128)S(1)} %bitcast.42), custom_call_target="tpu_custom_call" | custom-call | flops 1073741824 | bytes 8388608 | tf_op jit(solution)/shard_map/intras/pallas_call | solution.py:371
  161.5 2.2 %inters.1 = (bf16[512,256]{1,0:T(8,128)(2,1)S(1)}, bf16[512,256]{1,0:T(8,128)(2,1)S(1)}, bf16[512,256]{1,0:T(8,128)(2,1)S(1)}, bf16[512,256]{1,0:T(8,128)(2,1)S(...) custom-call(s32[4]{0:T(128)S(1)} %copy-done.6, ...), custom_call_target="tpu_custom_call" | custom-call | flops 268435456 | bytes 6291456 | tf_op jit(solution)/shard_map/inters/pallas_call | solution.py:388
  164.7 2.4 %collective-permute-start.23 = (bf16[512,256]{1,0:T(8,128)(2,1)S(1)}, bf16[512,256]{1,0:T(8,128)(2,1)S(1)}, u32[]{:S(2)}, u32[]{:S(2)}) collective-permute-start(bf16[512,256]{1,0:T(8,128)(2,1)S(1)} %get-tuple-element.43), channel_id=1, source_target_pairs={{0,24},{8,0},{16,8},{24,16},{1,25},{9,1},{17,9},{25,17},{2,26},{10... | collective-permute-start | bytes 786440 | tf_op jit(solution)/shard_map/ppermute | solution.py:31
  167.0 3.2 %collective-permute-start.19 = (f32[2,8,256]{2,1,0:T(8,128)S(1)}, f32[2,8,256]{2,1,0:T(8,128)S(1)}, u32[]{:S(2)}, u32[]{:S(2)}) collective-permute-start(f32[2,8,256]{2,1,0:T(8,128)S(1)} %get-tuple-element.40), channel_id=1, source_target_pairs={{0,24},{8,0},{16,8},{24,16},{1,25},{9,1},{17,9},{25,17},{2,26},{10... | collective-permute-start | bytes 49160 | tf_op jit(solution)/shard_map/ppermute | solution.py:31
  170.3 2.9 %collective-permute-done.18 = f32[2,8,256]{2,1,0:T(8,128)S(1)} collective-permute-done((f32[2,8,256]{2,1,0:T(8,128)S(1)}, f32[2,8,256]{2,1,0:T(8,128)S(1)}, u32[]{:S(2)}, u32[]{:S(2)}) %collective-permute-start.18) | collective-permute-done | bytes 16416 | tf_op jit(solution)/shard_map/ppermute | solution.py:31
  176.7 4.3 %collective-permute-start.24 = (f32[2,8,256]{2,1,0:T(8,128)S(1)}, f32[2,8,256]{2,1,0:T(8,128)S(1)}, u32[]{:S(2)}, u32[]{:S(2)}) collective-permute-start(f32[2,8,256]{2,1,0:T(8,128)S(1)} %add.198), channel_id=1, source_target_pairs={{0,2},{2,4},{4,6},{6,0},{1,3},{3,5},{5,7},{7,1},{8,10},{10,12},{12... | collective-permute-start | bytes 49160 | tf_op jit(solution)/shard_map/ppermute | solution.py:35
  182.4 2.2 %collective-permute-start.26 = (f32[2,8,256]{2,1,0:T(8,128)S(1)}, f32[2,8,256]{2,1,0:T(8,128)S(1)}, u32[]{:S(2)}, u32[]{:S(2)}) collective-permute-start(f32[2,8,256]{2,1,0:T(8,128)S(1)} %add.198), channel_id=1, source_target_pairs={{0,4},{2,6},{4,0},{6,2},{1,5},{3,7},{5,1},{7,3},{8,12},{10,14},{12... | collective-permute-start | bytes 49160 | tf_op jit(solution)/shard_map/ppermute | solution.py:35
  184.8 2.8 %collective-permute-done.26 = f32[2,8,256]{2,1,0:T(8,128)S(1)} collective-permute-done((f32[2,8,256]{2,1,0:T(8,128)S(1)}, f32[2,8,256]{2,1,0:T(8,128)S(1)}, u32[]{:S(2)}, u32[]{:S(2)}) %collective-permute-start.26) | collective-permute-done | bytes 16416 | tf_op jit(solution)/shard_map/ppermute | solution.py:35
  187.6 2.0 %finish.1 = bf16[512,1024]{1,0:T(8,128)(2,1)} custom-call(s32[4]{0:T(128)S(1)} %copy-done.6, f32[2,8,256]{2,1,0:T(8,128)S(1)} %add_add_fusion.total, f32[1,1024]{1,0:T(1,128)S(1)} %bitcast.44, bf16[512,256]{1,0:T(8,128)(2,1)S(1)} %get-tuple-element.45.p0, bf16[512,256]{1,0:T(8,128)(2,1)S(1)} %collective-permute-done.22.p1, ...), custom_call_target="tpu_custom_call" | custom-call | flops 4194304 | bytes 3145728 | tf_op jit(solution)/shard_map/finish/pallas_call | solution.py:412
  (136 shorter events, 30.4 us)
Async XLA Ops:
  6.5 119.7 %all-gather.2.cloned.1.call-start = ((), (), s32[]{:S(2)}) async-start(), calls=%async_computation | async-start | bytes 25952256 | tf_op jit(solution)/shard_map/all_gather | solution.py:344
  8.9 15.6 %collective-permute-start = (bf16[384,768]{1,0:T(8,128)(2,1)S(1)}, bf16[384,768]{1,0:T(8,128)(2,1)}, u32[]{:S(2)}, u32[]{:S(2)}) collective-permute-start(bf16[384,768]{1,0:T(8,128)(2,1)S(1)} %copy.58), channel_id=1, source_target_pairs={{0,8},{1,25},{8,16},{9,1},{16,24},{17,9},{24,0},{25,17},{2,10},{3,... | collective-permute-start | bytes 1769480 | tf_op jit(solution)/shard_map/ppermute | solution.py:44
  11.9 13.8 %collective-permute-start.1 = (bf16[384,768]{1,0:T(8,128)(2,1)S(1)}, bf16[384,768]{1,0:T(8,128)(2,1)S(1)}, u32[]{:S(2)}, u32[]{:S(2)}) collective-permute-start(bf16[384,768]{1,0:T(8,128)(2,1)S(1)} %copy.61), channel_id=1, source_target_pairs={{0,24},{1,9},{8,0},{9,17},{16,8},{17,25},{24,16},{25,1},{2,26},{3,... | collective-permute-start | bytes 1769480 | tf_op jit(solution)/shard_map/ppermute | solution.py:44
  26.8 12.1 %collective-permute-start.2 = (bf16[384,768]{1,0:T(8,128)(2,1)}, bf16[384,768]{1,0:T(8,128)(2,1)}, u32[]{:S(2)}, u32[]{:S(2)}) collective-permute-start(bf16[384,768]{1,0:T(8,128)(2,1)} %copy.75.refs_0_), channel_id=1, source_target_pairs={{0,32},{1,97},{32,64},{33,1},{64,96},{65,33},{96,0},{97,65},{2,34}... | collective-permute-start | bytes 1769480 | tf_op jit(solution)/shard_map/ppermute | solution.py:44
  29.8 28.9 %collective-permute-start.8 = (bf16[384,768]{1,0:T(8,128)(2,1)}, bf16[384,768]{1,0:T(8,128)(2,1)}, u32[]{:S(2)}, u32[]{:S(2)}) collective-permute-start(bf16[384,768]{1,0:T(8,128)(2,1)} %copy.64), channel_id=1, source_target_pairs={{0,16},{1,17},{8,24},{9,25},{16,0},{17,1},{24,8},{25,9},{2,18},{3,... | collective-permute-start | bytes 1769480 | tf_op jit(solution)/shard_map/ppermute | solution.py:44
  38.9 11.4 %collective-permute-start.3 = (bf16[384,768]{1,0:T(8,128)(2,1)}, bf16[384,768]{1,0:T(8,128)(2,1)}, u32[]{:S(2)}, u32[]{:S(2)}) collective-permute-start(bf16[384,768]{1,0:T(8,128)(2,1)} %collective-permute-done.2.refs_1_), channel_id=1, source_target_pairs={{0,32},{1,97},{32,64},{33,1},{64,96},{65,33},{96,0},{97,65},{2,34}... | collective-permute-start | bytes 1769480 | tf_op jit(solution)/shard_map/ppermute | solution.py:44
  40.5 16.2 %collective-permute-start.5 = (bf16[384,768]{1,0:T(8,128)(2,1)}, bf16[384,768]{1,0:T(8,128)(2,1)}, u32[]{:S(2)}, u32[]{:S(2)}) collective-permute-start(bf16[384,768]{1,0:T(8,128)(2,1)} %collective-permute-done.refs_4_), channel_id=1, source_target_pairs={{0,32},{1,97},{32,64},{33,1},{64,96},{65,33},{96,0},{97,65},{2,34}... | collective-permute-start | bytes 1769480 | tf_op jit(solution)/shard_map/ppermute | solution.py:44
  50.3 12.5 %collective-permute-start.4 = (bf16[384,768]{1,0:T(8,128)(2,1)}, bf16[384,768]{1,0:T(8,128)(2,1)S(1)}, u32[]{:S(2)}, u32[]{:S(2)}) collective-permute-start(bf16[384,768]{1,0:T(8,128)(2,1)} %collective-permute-done.3.refs_2_), channel_id=1, source_target_pairs={{0,32},{1,97},{32,64},{33,1},{64,96},{65,33},{96,0},{97,65},{2,34}... | collective-permute-start | bytes 1769480 | tf_op jit(solution)/shard_map/ppermute | solution.py:44
  56.7 12.5 %collective-permute-start.6 = (bf16[384,768]{1,0:T(8,128)(2,1)}, bf16[384,768]{1,0:T(8,128)(2,1)S(1)}, u32[]{:S(2)}, u32[]{:S(2)}) collective-permute-start(bf16[384,768]{1,0:T(8,128)(2,1)} %collective-permute-done.5.refs_5_), channel_id=1, source_target_pairs={{0,32},{1,97},{32,64},{33,1},{64,96},{65,33},{96,0},{97,65},{2,34}... | collective-permute-start | bytes 1769480 | tf_op jit(solution)/shard_map/ppermute | solution.py:44
  57.3 18.2 %collective-permute-start.12 = (bf16[384,768]{1,0:T(8,128)(2,1)S(1)}, bf16[384,768]{1,0:T(8,128)(2,1)S(1)}, u32[]{:S(2)}, u32[]{:S(2)}) collective-permute-start(bf16[384,768]{1,0:T(8,128)(2,1)S(1)} %copy-done.9), channel_id=1, source_target_pairs={{0,32},{1,97},{32,64},{33,1},{64,96},{65,33},{96,0},{97,65},{2,34}... | collective-permute-start | bytes 1769480 | tf_op jit(solution)/shard_map/ppermute | solution.py:44
  62.9 50.7 %copy-start.10 = (bf16[384,768]{1,0:T(8,128)(2,1)}, bf16[384,768]{1,0:T(8,128)(2,1)S(1)}, u32[]{:S(2)}) copy-start(bf16[384,768]{1,0:T(8,128)(2,1)S(1)} %collective-permute-done.4.refs_3_) | copy-start | bytes 1769476
  69.2 44.3 %copy-start.11 = (bf16[384,768]{1,0:T(8,128)(2,1)}, bf16[384,768]{1,0:T(8,128)(2,1)S(1)}, u32[]{:S(2)}) copy-start(bf16[384,768]{1,0:T(8,128)(2,1)S(1)} %collective-permute-done.6.refs_6_) | copy-start | bytes 1769476
  69.2 12.6 %collective-permute-start.9 = (bf16[384,768]{1,0:T(8,128)(2,1)}, bf16[384,768]{1,0:T(8,128)(2,1)S(1)}, u32[]{:S(2)}, u32[]{:S(2)}) collective-permute-start(bf16[384,768]{1,0:T(8,128)(2,1)} %collective-permute-done.8.refs_8_), channel_id=1, source_target_pairs={{0,32},{1,97},{32,64},{33,1},{64,96},{65,33},{96,0},{97,65},{2,34}... | collective-permute-start | bytes 1769480 | tf_op jit(solution)/shard_map/ppermute | solution.py:44
  75.5 38.0 %copy-start.12 = (bf16[384,768]{1,0:T(8,128)(2,1)}, bf16[384,768]{1,0:T(8,128)(2,1)S(1)}, u32[]{:S(2)}) copy-start(bf16[384,768]{1,0:T(8,128)(2,1)S(1)} %collective-permute-done.12.refs_13_) | copy-start | bytes 1769476
  75.5 12.6 %collective-permute-start.13 = (bf16[384,768]{1,0:T(8,128)(2,1)S(1)}, bf16[384,768]{1,0:T(8,128)(2,1)S(1)}, u32[]{:S(2)}, u32[]{:S(2)}) collective-permute-start(bf16[384,768]{1,0:T(8,128)(2,1)S(1)} %collective-permute-done.12.refs_13_), channel_id=1, source_target_pairs={{0,32},{1,97},{32,64},{33,1},{64,96},{65,33},{96,0},{97,65},{2,34}... | collective-permute-start | bytes 1769480 | tf_op jit(solution)/shard_map/ppermute | solution.py:44
  81.8 12.6 %collective-permute-start.10 = (bf16[384,768]{1,0:T(8,128)(2,1)S(1)}, bf16[384,768]{1,0:T(8,128)(2,1)S(1)}, u32[]{:S(2)}, u32[]{:S(2)}) collective-permute-start(bf16[384,768]{1,0:T(8,128)(2,1)S(1)} %collective-permute-done.9.refs_9_), channel_id=1, source_target_pairs={{0,32},{1,97},{32,64},{33,1},{64,96},{65,33},{96,0},{97,65},{2,34}... | collective-permute-start | bytes 1769480 | tf_op jit(solution)/shard_map/ppermute | solution.py:44
  82.2 24.9 %collective-permute-start.7 = (bf16[384,768]{1,0:T(8,128)(2,1)S(1)}, bf16[384,768]{1,0:T(8,128)(2,1)S(1)}, u32[]{:S(2)}, u32[]{:S(2)}) collective-permute-start(bf16[384,768]{1,0:T(8,128)(2,1)S(1)} %collective-permute-done.6.refs_6_), channel_id=1, source_target_pairs={{0,32},{1,97},{32,64},{33,1},{64,96},{65,33},{96,0},{97,65},{2,34}... | collective-permute-start | bytes 1769480 | tf_op jit(solution)/shard_map/ppermute | solution.py:44
  88.1 19.0 %collective-permute-start.14 = (bf16[384,768]{1,0:T(8,128)(2,1)S(1)}, bf16[384,768]{1,0:T(8,128)(2,1)S(1)}, u32[]{:S(2)}, u32[]{:S(2)}) collective-permute-start(bf16[384,768]{1,0:T(8,128)(2,1)S(1)} %collective-permute-done.13.refs_14_), channel_id=1, source_target_pairs={{0,32},{1,97},{32,64},{33,1},{64,96},{65,33},{96,0},{97,65},{2,34}... | collective-permute-start | bytes 1769480 | tf_op jit(solution)/shard_map/ppermute | solution.py:44
  94.5 19.1 %collective-permute-start.11 = (bf16[384,768]{1,0:T(8,128)(2,1)S(1)}, bf16[384,768]{1,0:T(8,128)(2,1)}, u32[]{:S(2)}, u32[]{:S(2)}) collective-permute-start(bf16[384,768]{1,0:T(8,128)(2,1)S(1)} %collective-permute-done.10.refs_10_), channel_id=1, source_target_pairs={{0,32},{1,97},{32,64},{33,1},{64,96},{65,33},{96,0},{97,65},{2,34}... | collective-permute-start | bytes 1769480 | tf_op jit(solution)/shard_map/ppermute | solution.py:44
  152.6 8.9 %collective-permute-start.15 = (bf16[2,128,128]{2,1,0:T(8,128)(2,1)S(1)}, bf16[2,128,128]{2,1,0:T(8,128)(2,1)S(1)}, u32[]{:S(2)}, u32[]{:S(2)}) collective-permute-start(bf16[2,128,128]{2,1,0:T(8,128)(2,1)S(1)} %get-tuple-element.37), channel_id=1, source_target_pairs={{0,32},{32,64},{64,96},{96,0},{1,33},{33,65},{65,97},{97,1},{2,34}... | collective-permute-start | bytes 196616 | tf_op jit(solution)/shard_map/ppermute | solution.py:27
  153.0 8.4 %collective-permute-start.16 = (bf16[2,128,128]{2,1,0:T(8,128)(2,1)S(1)}, bf16[2,128,128]{2,1,0:T(8,128)(2,1)S(1)}, u32[]{:S(2)}, u32[]{:S(2)}) collective-permute-start(bf16[2,128,128]{2,1,0:T(8,128)(2,1)S(1)} %get-tuple-element.37), channel_id=1, source_target_pairs={{0,64},{32,96},{64,0},{96,32},{1,65},{33,97},{65,1},{97,33},{2,66}... | collective-permute-start | bytes 196616 | tf_op jit(solution)/shard_map/ppermute | solution.py:27
  155.8 5.7 %collective-permute-start.17 = (bf16[2,128,128]{2,1,0:T(8,128)(2,1)S(1)}, bf16[2,128,128]{2,1,0:T(8,128)(2,1)S(1)}, u32[]{:S(2)}, u32[]{:S(2)}) collective-permute-start(bf16[2,128,128]{2,1,0:T(8,128)(2,1)S(1)} %get-tuple-element.37), channel_id=1, source_target_pairs={{0,96},{32,0},{64,32},{96,64},{1,97},{33,1},{65,33},{97,65},{2,98}... | collective-permute-start | bytes 196616 | tf_op jit(solution)/shard_map/ppermute | solution.py:27
  163.7 13.0 %collective-permute-start.22 = (bf16[512,256]{1,0:T(8,128)(2,1)S(1)}, bf16[512,256]{1,0:T(8,128)(2,1)S(1)}, u32[]{:S(2)}, u32[]{:S(2)}) collective-permute-start(bf16[512,256]{1,0:T(8,128)(2,1)S(1)} %get-tuple-element.42), channel_id=1, source_target_pairs={{0,8},{8,16},{16,24},{24,0},{1,9},{9,17},{17,25},{25,1},{2,10},{10... | collective-permute-start | bytes 786440 | tf_op jit(solution)/shard_map/ppermute | solution.py:31
  164.7 12.0 %collective-permute-start.23 = (bf16[512,256]{1,0:T(8,128)(2,1)S(1)}, bf16[512,256]{1,0:T(8,128)(2,1)S(1)}, u32[]{:S(2)}, u32[]{:S(2)}) collective-permute-start(bf16[512,256]{1,0:T(8,128)(2,1)S(1)} %get-tuple-element.43), channel_id=1, source_target_pairs={{0,24},{8,0},{16,8},{24,16},{1,25},{9,1},{17,9},{25,17},{2,26},{10... | collective-permute-start | bytes 786440 | tf_op jit(solution)/shard_map/ppermute | solution.py:31
  167.0 6.1 %collective-permute-start.18 = (f32[2,8,256]{2,1,0:T(8,128)S(1)}, f32[2,8,256]{2,1,0:T(8,128)S(1)}, u32[]{:S(2)}, u32[]{:S(2)}) collective-permute-start(f32[2,8,256]{2,1,0:T(8,128)S(1)} %get-tuple-element.39), channel_id=1, source_target_pairs={{0,8},{8,16},{16,24},{24,0},{1,9},{9,17},{17,25},{25,1},{2,10},{10... | collective-permute-start | bytes 49160 | tf_op jit(solution)/shard_map/ppermute | solution.py:31
  167.0 7.3 %collective-permute-start.19 = (f32[2,8,256]{2,1,0:T(8,128)S(1)}, f32[2,8,256]{2,1,0:T(8,128)S(1)}, u32[]{:S(2)}, u32[]{:S(2)}) collective-permute-start(f32[2,8,256]{2,1,0:T(8,128)S(1)} %get-tuple-element.40), channel_id=1, source_target_pairs={{0,24},{8,0},{16,8},{24,16},{1,25},{9,1},{17,9},{25,17},{2,26},{10... | collective-permute-start | bytes 49160 | tf_op jit(solution)/shard_map/ppermute | solution.py:31
  170.3 5.2 %collective-permute-start.20 = (f32[2,8,256]{2,1,0:T(8,128)S(1)}, f32[2,8,256]{2,1,0:T(8,128)S(1)}, u32[]{:S(2)}, u32[]{:S(2)}) collective-permute-start(f32[2,8,256]{2,1,0:T(8,128)S(1)} %get-tuple-element.41), channel_id=1, source_target_pairs={{0,16},{8,24},{16,0},{24,8},{1,17},{9,25},{17,1},{25,9},{2,18},{10... | collective-permute-start | bytes 49160 | tf_op jit(solution)/shard_map/ppermute | solution.py:31
  173.2 14.4 %collective-permute-start.27 = (bf16[512,256]{1,0:T(8,128)(2,1)S(1)}, bf16[512,256]{1,0:T(8,128)(2,1)S(1)}, u32[]{:S(2)}, u32[]{:S(2)}) collective-permute-start(bf16[512,256]{1,0:T(8,128)(2,1)S(1)} %get-tuple-element.46), channel_id=1, source_target_pairs={{0,16},{8,24},{16,0},{24,8},{1,17},{9,25},{17,1},{25,9},{2,18},{10... | collective-permute-start | bytes 786440 | tf_op jit(solution)/shard_map/ppermute | solution.py:31
  175.5 1.2 collective-permute-start.21
  176.7 7.9 %collective-permute-start.24 = (f32[2,8,256]{2,1,0:T(8,128)S(1)}, f32[2,8,256]{2,1,0:T(8,128)S(1)}, u32[]{:S(2)}, u32[]{:S(2)}) collective-permute-start(f32[2,8,256]{2,1,0:T(8,128)S(1)} %add.198), channel_id=1, source_target_pairs={{0,2},{2,4},{4,6},{6,0},{1,3},{3,5},{5,7},{7,1},{8,10},{10,12},{12... | collective-permute-start | bytes 49160 | tf_op jit(solution)/shard_map/ppermute | solution.py:35
  181.1 3.7 %collective-permute-start.25 = (f32[2,8,256]{2,1,0:T(8,128)S(1)}, f32[2,8,256]{2,1,0:T(8,128)S(1)}, u32[]{:S(2)}, u32[]{:S(2)}) collective-permute-start(f32[2,8,256]{2,1,0:T(8,128)S(1)} %add.198), channel_id=1, source_target_pairs={{0,6},{2,0},{4,2},{6,4},{1,7},{3,1},{5,3},{7,5},{8,14},{10,8},{12,... | collective-permute-start | bytes 49160 | tf_op jit(solution)/shard_map/ppermute | solution.py:35
  182.4 5.2 %collective-permute-start.26 = (f32[2,8,256]{2,1,0:T(8,128)S(1)}, f32[2,8,256]{2,1,0:T(8,128)S(1)}, u32[]{:S(2)}, u32[]{:S(2)}) collective-permute-start(f32[2,8,256]{2,1,0:T(8,128)S(1)} %add.198), channel_id=1, source_target_pairs={{0,4},{2,6},{4,0},{6,2},{1,5},{3,7},{5,1},{7,3},{8,12},{10,14},{12... | collective-permute-start | bytes 49160 | tf_op jit(solution)/shard_map/ppermute | solution.py:35
  (16 other events, 242.6 us)
Sparse Core Ops, SparseCore 0:
  25.9 99.1 all-gather.1
